TPU v7x, 128 devices: a whole 4x4x4 slice. The times are simulated.
128 devices in a mesh: dp: 16 (over z, x), tensor: 8 (over y, core).
Axes of the slice: x: 4, y: 4, z: 4, core: 2. Of those that a mesh axis runs over, the one named last changes fastest.
Arguments:
- hidden: bfloat16 [2048, 8192], P(('dp', 'tensor')), may hold values from -400 to 400
- gain: float32 [8192], replicated, may hold values from 0.5 to 1.5
- w_query: bfloat16 [8192, 8192], P(None, 'tensor'), may hold values from -16 to 16
- w_key: bfloat16 [8192, 1024], P(None, 'tensor'), may hold values from -1 to 1
- w_value: bfloat16 [8192, 1024], P(None, 'tensor'), may hold values from -0.0625 to 0.0625
- out_grad: bfloat16 [2048, 8192], P(('dp', 'tensor')), may hold values from -6 to 6
- owner: int32 [2048, 1], P(('dp', 'tensor')), may hold values from 0 to 15; in each aligned block of 16 rows (0 to 15, 16 to 31, ...) at most 2 rows name the same one
- completion: int32 [2048], P(('dp', 'tensor')), may hold values from 0 to 15
- rewards: int32 [16, 16], P('dp'), may hold values from -512 to 511
Outputs:
- grad_hidden: bfloat16 [2048, 8192], P(('dp', 'tensor'))
Inputs may be any that keep to these rules, and one draw needn't show every extreme that they name: Among the rows of one device, one owner group is named at most 2 times; in every draw some device names some group exactly 2 times. Fixed-point rewards in units of 1/256.
All inputs are finite; a program needn't handle non-finite values.
Results may differ from a plain program's by a relative error of at most 0.015.
Values may be sent and summed in bfloat16 or wider, within the bound.
No kernel may reach another device: no remote copies, remote signals or barrier semaphores. Data moves between devices by JAX's collectives and lax.ppermute only.
A program may use at most 128 MiB of HBM per device.

v0:
```python
import jax
import jax.numpy as jnp
from jax import lax
from jax.sharding import PartitionSpec as P

HD = 128
KC = 16


epsilon = 1e-05
base_freq = 500000.0


def angles(position, size):
    half = size // 2
    freq = base_freq ** (-2.0 * jnp.arange(half, dtype=jnp.float32) / size)
    angle = position.astype(jnp.float32)[:, None] * freq[None, :]
    return (jnp.cos(angle), jnp.sin(angle))


def rotate(values, cosine, sine):
    half = values.shape[-1] // 2
    first = values[..., :half]
    second = values[..., half:]
    return jnp.concatenate(
        [first * cosine - second * sine, second * cosine + first * sine], axis=-1
    )


def positions(labels, kinds):
    member = (labels[:, None] == jnp.arange(kinds, dtype=jnp.int32)[None, :]).astype(jnp.int32)
    return jnp.sum((jnp.cumsum(member, axis=0) - member) * member, axis=1)


def project_slots(slot_rows, cosine, sine, w_query, w_key, w_value, head_count, kv_count, share):
    slots = slot_rows.shape[0]
    query = rotate(
        jnp.dot(slot_rows, w_query, preferred_element_type=jnp.float32)
        .reshape(slots, head_count, HD)
        .transpose(1, 0, 2),
        cosine,
        sine,
    )
    query = query.astype(jnp.bfloat16).reshape(kv_count, share, slots, HD)
    keys = rotate(
        jnp.dot(slot_rows, w_key, preferred_element_type=jnp.float32)
        .reshape(slots, kv_count, HD)
        .transpose(1, 0, 2),
        cosine,
        sine,
    ).astype(jnp.bfloat16)
    values = (
        jnp.dot(slot_rows, w_value, preferred_element_type=jnp.float32)
        .astype(jnp.bfloat16)
        .reshape(slots, kv_count, HD)
        .transpose(1, 0, 2)
    )
    return (query, keys, values)


def attend_back(query, keys, values, grad_head, labels, order):
    size = query.shape[-1]
    factor = size ** (-0.5)
    allowed = (labels[:, None] == labels[None, :]) & (order[None, :] <= order[:, None])
    scores = jnp.einsum("gpqd,gkd->gpqk", query, keys, preferred_element_type=jnp.float32) * factor
    scores = jnp.where(allowed, scores, -1e30)
    highest = jnp.max(scores, axis=-1, keepdims=True)
    weights = jnp.exp(scores - highest)
    probs = weights / jnp.sum(weights, axis=-1, keepdims=True)
    rounded_probs = probs.astype(jnp.bfloat16)
    grad_value = jnp.einsum(
        "gpqk,gpqd->gkd", rounded_probs, grad_head, preferred_element_type=jnp.float32
    ).astype(jnp.bfloat16)
    grad_probs = jnp.einsum("gpqd,gkd->gpqk", grad_head, values, preferred_element_type=jnp.float32)
    inner = jnp.sum(probs * grad_probs, axis=-1, keepdims=True)
    grad_scores = (probs * (grad_probs - inner) * factor).astype(jnp.bfloat16)
    grad_query = jnp.einsum("gpqk,gkd->gpqd", grad_scores, keys, preferred_element_type=jnp.float32)
    grad_key = jnp.einsum("gpqk,gpqd->gkd", grad_scores, query, preferred_element_type=jnp.float32)
    return (grad_query, grad_key, grad_value)


def on_device(hidden, gain, w_query, w_key, w_value, out_grad, owner, completion, rewards):
    groups = lax.axis_size("dp")
    ranks = lax.axis_size("tensor")
    count, width = hidden.shape
    capacity = 2 * count // groups
    query_cols = w_query.shape[1]
    key_cols = w_key.shape[1]
    head_count = query_cols // HD
    kv_count = key_cols // HD
    share = head_count // kv_count
    wide = hidden.astype(jnp.float32)
    inverse = lax.rsqrt(jnp.mean(wide * wide, axis=1, keepdims=True) + epsilon)
    normed = (wide * inverse * gain[None, :]).astype(jnp.bfloat16)
    target = owner[:, 0]
    member = (target[:, None] == jnp.arange(groups, dtype=jnp.int32)[None, :]).astype(jnp.int32)
    slot_rank = jnp.sum((jnp.cumsum(member, axis=0) - member) * member, axis=1)
    place = target * capacity + slot_rank
    select = jnp.arange(groups * capacity, dtype=jnp.int32)[:, None] == place[None, :]
    picker = select.astype(jnp.bfloat16)
    send_rows = jnp.dot(picker, normed, preferred_element_type=jnp.float32).astype(jnp.bfloat16)
    send_grad = jnp.dot(picker, out_grad, preferred_element_type=jnp.float32).astype(jnp.bfloat16)
    send_labels = (jnp.sum(jnp.where(select, completion[None, :] + 1, 0), axis=1) - 1).astype(
        jnp.bfloat16
    )
    rows_all = jnp.broadcast_to(
        send_rows.reshape(groups, 1, capacity, width), (groups, ranks, capacity, width)
    ).reshape(groups * ranks, capacity, width)
    grad_all = (
        send_grad.reshape(groups, capacity, ranks, query_cols)
        .transpose(0, 2, 1, 3)
        .reshape(groups * ranks, capacity, query_cols)
    )
    labels_all = jnp.broadcast_to(
        send_labels.reshape(groups, 1, capacity), (groups, ranks, capacity)
    ).reshape(groups * ranks, capacity)
    got_rows, got_grad, got_labels = (
        lax.all_to_all(rows_all, ("dp", "tensor"), split_axis=0, concat_axis=0, tiled=True),
        lax.all_to_all(grad_all, ("dp", "tensor"), split_axis=0, concat_axis=0, tiled=True),
        lax.all_to_all(labels_all, ("dp", "tensor"), split_axis=0, concat_axis=0, tiled=True),
    )
    slot_rows = got_rows.reshape(-1, width)
    slot_grad = got_grad.reshape(-1, query_cols)
    slot_labels = got_labels.reshape(-1).astype(jnp.int32)
    slot_order = positions(slot_labels, KC)
    slots = slot_rows.shape[0]
    cosine, sine = angles(slot_order, HD)
    cosine = cosine[None]
    sine = sine[None]
    query, keys, values = project_slots(
        slot_rows, cosine, sine, w_query, w_key, w_value, head_count, kv_count, share
    )
    scaled = rewards[0].astype(jnp.float32) / 256.0
    advantage = scaled - (jnp.sum(scaled) - scaled) / (KC - 1)
    slot_weight = jnp.sum(
        jnp.where(
            slot_labels[:, None] == jnp.arange(KC, dtype=jnp.int32)[None, :],
            advantage[None, :],
            0.0,
        ),
        axis=1,
    )
    grad_head = (slot_grad.astype(jnp.float32) * slot_weight[:, None]).astype(jnp.bfloat16)
    grad_head = (
        grad_head.reshape(slots, head_count, HD)
        .transpose(1, 0, 2)
        .reshape(kv_count, share, slots, HD)
    )
    grad_query, grad_key, grad_value = attend_back(
        query, keys, values, grad_head, slot_labels, slot_order
    )
    back_query = (
        rotate(grad_query.reshape(head_count, slots, HD), cosine, -sine)
        .astype(jnp.bfloat16)
        .transpose(1, 0, 2)
        .reshape(slots, query_cols)
    )
    back_key = (
        rotate(grad_key, cosine, -sine)
        .astype(jnp.bfloat16)
        .transpose(1, 0, 2)
        .reshape(slots, key_cols)
    )
    back_value = grad_value.transpose(1, 0, 2).reshape(slots, key_cols)
    partial_value = jnp.einsum("sc,dc->sd", back_query, w_query, preferred_element_type=jnp.float32)
    partial_value = partial_value + jnp.einsum(
        "sc,dc->sd", back_key, w_key, preferred_element_type=jnp.float32
    )
    partial_value = partial_value + jnp.einsum(
        "sc,dc->sd", back_value, w_value, preferred_element_type=jnp.float32
    )
    partial_value = partial_value.astype(jnp.bfloat16)
    returned = lax.all_to_all(
        partial_value.reshape(groups * ranks, capacity, width),
        ("dp", "tensor"),
        split_axis=0,
        concat_axis=0,
        tiled=True,
    )
    summed = jnp.sum(
        returned.reshape(groups, ranks, capacity, width).astype(jnp.float32), axis=1
    ).reshape(groups * capacity, width)
    grad_normed = summed[place]
    scaled_grad = grad_normed * gain[None, :]
    inner = jnp.mean(scaled_grad * wide, axis=1, keepdims=True)
    return (inverse * scaled_grad - wide * inverse * inverse * inverse * inner).astype(jnp.bfloat16)


def solution(mesh):
    return jax.shard_map(
        on_device,
        mesh=mesh,
        in_specs=(
            P(("dp", "tensor"), None),
            P(),
            P(None, "tensor"),
            P(None, "tensor"),
            P(None, "tensor"),
            P(("dp", "tensor"), None),
            P(("dp", "tensor"), None),
            P(("dp", "tensor")),
            P("dp", None),
        ),
        out_specs=P(("dp", "tensor"), None),
        check_vma=False,
    )
```

profile of v0, /device:TPU:1, one launch (start us, length us, event | category | flops | bytes accessed | tf_op | source)
XLA Modules:
  0.0 274.0 jit_solution(9213353571851617464)
XLA Ops:
  0.0 0.9 fusion.72
  0.9 0.8 select_reduce_fusion.2
  1.8 0.7 multiply_add_fusion
  2.9 0.8 copy.47
  3.7 11.5 %all-to-all-start = ((bf16[128,1,2]{2,1,0:T(2,128)(2,1)}), bf16[128,1,2]{2,1,0:T(2,128)(2,1)S(1)}, u32[]{:S(2)}, u32[]{:S(2)}) async-start(bf16[128,1,2]{2,1,0:T(2,128)(2,1)} %copy.47), calls=%async_computation | async-start | bytes 131072 | tf_op jit(solution)/shard_map/all_to_all | solution.py:120
  15.2 1.4 convolution_convert_fusion
  16.6 0.3 copy.65
  16.9 1.3 copy.53
  18.2 6.5 %all-to-all-done = bf16[128,1,2]{2,1,0:T(2,128)(2,1)S(1)} async-done(((bf16[128,1,2]{2,1,0:T(2,128)(2,1)}), bf16[128,1,2]{2,1,0:T(2,128)(2,1)S(1)}, u32[]{:S(2)}, u32[]{:S(2)}) %all-to-all-start) | async-done | bytes 544 | tf_op jit(solution)/shard_map/all_to_all | solution.py:120
  24.7 4.4 %all-to-all-start.2 = ((bf16[128,2,1024]{2,1,0:T(2,128)(2,1)}), bf16[128,2,1024]{2,1,0:T(2,128)(2,1)S(1)}, u32[]{:S(2)}, u32[]{:S(2)}) async-start(bf16[128,2,1024]{2,1,0:T(2,128)(2,1)} %copy.53), calls=%async_computation.2 | async-start | bytes 1048576 | tf_op jit(solution)/shard_map/all_to_all | solution.py:119
  29.1 0.2 fusion.33
  29.3 1.2 convolution_convert_fusion.1
  30.6 1.4 broadcast_in_dim.42
  31.9 10.7 %all-to-all-done.2 = bf16[128,2,1024]{2,1,0:T(2,128)(2,1)S(1)} async-done(((bf16[128,2,1024]{2,1,0:T(2,128)(2,1)}), bf16[128,2,1024]{2,1,0:T(2,128)(2,1)S(1)}, u32[]{:S(2)}, u32[]{:S(2)}) %all-to-all-start.2) | async-done | bytes 524320 | tf_op jit(solution)/shard_map/all_to_all | solution.py:119
  42.6 6.1 %broadcast_in_dim.43 = bf16[16,8,2,8192]{3,2,1,0:T(2,128)(2,1)} broadcast(bf16[16,2,8192]{2,1,0:T(2,128)(2,1)S(1)} %broadcast_in_dim.42), dimensions={0,2,3} | broadcast | bytes 4718592 | tf_op jit(solution)/shard_map/broadcast_in_dim | solution.py:106
  48.8 5.6 %all-to-all-start.1 = ((bf16[128,2,8192]{2,1,0:T(2,128)(2,1)}), bf16[128,2,8192]{2,1,0:T(2,128)(2,1)}, u32[]{:S(2)}, u32[]{:S(2)}) async-start(bf16[128,2,8192]{2,1,0:T(2,128)(2,1)} %bitcast.100), calls=%async_computation.1 | async-start | bytes 8388608 | tf_op jit(solution)/shard_map/all_to_all | solution.py:118
  54.4 20.9 %copy.62 = bf16[1024,8192]{1,0:T(8,128)(2,1)} copy(bf16[1024,8192]{0,1:T(8,128)(2,1)} %bitcast.98) | data formatting | bytes 33554432 | tf_op jit(solution)/shard_map/dot_general | solution.py:38
  75.4 0.6 fusion.76
  76.0 0.7 subtract_bitcast_fusion
  76.6 0.2 convert_reduce_fusion.1
  77.2 0.6 reduce-window.6
  78.4 0.3 fusion.67
  78.7 1.4 reshape.378
  80.0 1.6 fusion.35
  81.6 25.8 %all-to-all-done.1 = bf16[128,2,8192]{2,1,0:T(2,128)(2,1)} async-done(((bf16[128,2,8192]{2,1,0:T(2,128)(2,1)}), bf16[128,2,8192]{2,1,0:T(2,128)(2,1)}, u32[]{:S(2)}, u32[]{:S(2)}) %all-to-all-start.1) | async-done | bytes 4194336 | tf_op jit(solution)/shard_map/all_to_all | solution.py:118
  107.4 7.2 %reshape.370 = bf16[256,8192]{1,0:T(8,128)(2,1)} reshape(bf16[128,2,8192]{2,1,0:T(2,128)(2,1)} %all-to-all-done.1) | data formatting | bytes 8388608 | tf_op jit(solution)/shard_map/reshape | solution.py:122
  114.6 4.4 %convolution_bitcast_fusion.1 = f32[1,256,128]{1,2,0:T(8,128)S(1)} fusion(bf16[256,8192]{1,0:T(8,128)(2,1)} %reshape.370, bf16[8192,128]{1,0:T(8,128)(2,1)} %param.12), kind=kOutput, calls=%fused_computation.19 | convolution fusion | flops 536870912 | bytes 6422528 | tf_op jit(solution)/shard_map/dot_general | solution.py:46
  118.9 0.3 fusion.64
  119.3 5.2 %fusion.18 = f32[8,256,256]{1,2,0:T(8,128)} fusion(bf16[256,8192]{1,0:T(8,128)(2,1)} %reshape.370, bf16[8192,128]{1,0:T(8,128)(2,1)S(1)} %copy-done, bf16[8,256,128]{2,0,1:T(8,128)(2,1)S(1)} %fusion.35), kind=kOutput, calls=%fused_computation.24 | convolution fusion | flops 671121408 | bytes 8912896 | tf_op jit(solution)/shard_map/gpqd,gkd->gpqk/dot_general | solution.py:74
  124.4 7.2 %reshape.388 = bf16[256,8192,1]{1,0,2:T(8,128)(2,1)} reshape(bf16[128,2,8192]{2,1,0:T(2,128)(2,1)} %all-to-all-done.1) | data formatting | bytes 8388608 | tf_op jit(solution)/shard_map/reshape | solution.py:122
  131.6 9.3 %convolution_bitcast_fusion = f32[8,256,128]{1,2,0:T(8,128)S(1)} fusion(bf16[256,8192,1]{1,0,2:T(8,128)(2,1)} %reshape.388, bf16[8,128,8192]{2,1,0:T(8,128)(2,1)} %bitcast.99), kind=kOutput, calls=%fused_computation.17 | convolution fusion | flops 4294967296 | bytes 22020096 | tf_op jit(solution)/shard_map/dot_general | solution.py:38
  141.0 0.8 subtract_convert_fusion.1
  141.8 3.1 %fusion.89 = (f32[8,256]{1,0:T(8,128)S(1)}, f32[8,256,256]{1,2,0:T(8,128)}) fusion(pred[256,256]{0,1:T(8,128)(4,1)S(1)} %compare_and_fusion, bf16[8,256,64]{1,2,0:T(8,128)(2,1)} %get-tuple-element.8, bf16[8,256,64]{1,2,0:T(8,128)(2,1)S(1)} %get-tuple-element.7, bf16[256,64]{0,1:T(8,128)(2,1)S(1)} %get-tuple-element.12, ...), kind=kOutput, calls=%fused_computation.131 | convolution fusion | flops 137494784 | bytes 2760704 | tf_op jit(solution)/shard_map/sub | solution.py:68
  144.9 5.2 %fusion.11 = f32[8,256,128]{1,2,0:T(8,128)} fusion(f32[8,256,256]{1,2,0:T(8,128)} %fusion.18, bf16[256,64]{0,1:T(8,128)(2,1)S(1)} %get-tuple-element.12, bf16[256,64]{0,1:T(8,128)(2,1)S(1)} %get-tuple-element.11, f32[8,256,256]{1,2,0:T(8,128)} %get-tuple-element.17, f32[8,256]{1,0:T(8,128)S(1)} %get-tuple-element.16), kind=kOutput, calls=%fused_computation.16 | convolution fusion | flops 138021120 | bytes 5316608 | tf_op jit(solution)/shard_map/gpqk,gkd->gpqd/dot_general | solution.py:77
  150.2 4.9 %fusion.13 = f32[1,256,128]{1,2,0:T(8,128)} fusion(f32[8,256,256]{1,2,0:T(8,128)} %fusion.18, bf16[8,256,64]{1,2,0:T(8,128)(2,1)} %get-tuple-element.8, bf16[8,256,64]{1,2,0:T(8,128)(2,1)S(1)} %get-tuple-element.7, f32[8,256,256]{1,2,0:T(8,128)} %get-tuple-element.17, f32[8,256]{1,0:T(8,128)S(1)} %get-tuple-element.16), kind=kOutput, calls=%fused_computation.18 | convolution fusion | flops 138938624 | bytes 4857856 | tf_op jit(solution)/shard_map/gpqk,gpqd->gkd/dot_general | solution.py:78
  155.1 1.3 subtract_convert_fusion
  156.5 19.3 %fusion.90 = f32[256,8192]{1,0:T(8,128)} fusion(bf16[256,1024]{0,1:T(8,128)(2,1)S(1)} %bitcast.101, bf16[8192,1024]{1,0:T(8,128)(2,1)} %param.11), kind=kOutput, calls=%fused_computation.132 | convolution fusion | flops 4294967296 | bytes 25690112 | tf_op jit(solution)/shard_map/sc,dc->sd/dot_general | solution.py:165
  175.7 1.2 fusion.66
  176.9 8.5 %convolution_add_fusion.1 = f32[256,8192]{1,0:T(8,128)} fusion(f32[256,8192]{1,0:T(8,128)} %fusion.90, bf16[8192,128]{1,0:T(8,128)(2,1)} %param.12, bf16[256,64]{0,1:T(8,128)(2,1)S(1)} %get-tuple-element.10, bf16[256,64]{0,1:T(8,128)(2,1)S(1)} %get-tuple-element.9), kind=kOutput, calls=%fused_computation.4 | convolution fusion | flops 539099136 | bytes 18939904 | tf_op jit(solution)/shard_map/sc,dc->sd/dot_general | solution.py:166
  185.5 7.6 %fusion.2 = bf16[256,8192]{1,0:T(8,128)(2,1)} fusion(f32[256,8192]{1,0:T(8,128)} %convolution_add_fusion.1, bf16[8192,128]{1,0:T(8,128)(2,1)S(1)} %copy-done, bf16[8,256,128]{2,0,1:T(8,128)(2,1)S(1)} %fusion.35, f32[8,256,256]{1,2,0:T(8,128)} %get-tuple-element.17, f32[8,256]{1,0:T(8,128)S(1)} %get-tuple-element.16), kind=kOutput, calls=%fused_computation.5 | convolution fusion | flops 676364288 | bytes 17309696 | tf_op jit(solution)/shard_map/sc,dc->sd/dot_general | solution.py:169
  193.1 7.6 %reshape.374 = bf16[128,2,8192]{2,1,0:T(2,128)(2,1)} reshape(bf16[256,8192]{1,0:T(8,128)(2,1)} %fusion.2) | data formatting | bytes 8388608 | tf_op jit(solution)/shard_map/reshape | solution.py:174
  200.7 5.5 %all-to-all-start.3 = ((bf16[128,2,8192]{2,1,0:T(2,128)(2,1)}), bf16[128,2,8192]{2,1,0:T(2,128)(2,1)}, u32[]{:S(2)}, u32[]{:S(2)}) async-start(bf16[128,2,8192]{2,1,0:T(2,128)(2,1)} %reshape.374), calls=%async_computation.3 | async-start | bytes 8388608 | tf_op jit(solution)/shard_map/all_to_all | solution.py:173
  206.3 52.9 %all-to-all-done.3 = bf16[128,2,8192]{2,1,0:T(2,128)(2,1)} async-done(((bf16[128,2,8192]{2,1,0:T(2,128)(2,1)}), bf16[128,2,8192]{2,1,0:T(2,128)(2,1)}, u32[]{:S(2)}, u32[]{:S(2)}) %all-to-all-start.3) | async-done | bytes 4194336 | tf_op jit(solution)/shard_map/all_to_all | solution.py:173
  259.2 8.2 %convert_reduce_fusion = f32[16,2,8192]{2,1,0:T(2,128)} fusion(bf16[128,2,8192]{2,1,0:T(2,128)(2,1)} %all-to-all-done.3), kind=kLoop, calls=%fused_computation.8 | loop fusion | flops 3932160 | bytes 5242880 | tf_op jit(solution)/shard_map/reduce_sum | solution.py:180
  267.4 1.9 reshape.375
  269.3 1.5 gather_fusion
  270.8 1.2 fusion.34
  272.0 1.9 fusion.32
  (35 shorter events, 1.5 us)
Async XLA Ops:
  0.0 119.3 %copy-start = (bf16[8192,128]{1,0:T(8,128)(2,1)S(1)}, bf16[8192,128]{1,0:T(8,128)(2,1)}, u32[]{:S(2)}) copy-start(bf16[8192,128]{1,0:T(8,128)(2,1)} %param.13) | copy-start | bytes 6291460
  3.7 21.0 %all-to-all-start = ((bf16[128,1,2]{2,1,0:T(2,128)(2,1)}), bf16[128,1,2]{2,1,0:T(2,128)(2,1)S(1)}, u32[]{:S(2)}, u32[]{:S(2)}) async-start(bf16[128,1,2]{2,1,0:T(2,128)(2,1)} %copy.47), calls=%async_computation | async-start | bytes 131072 | tf_op jit(solution)/shard_map/all_to_all | solution.py:120
  16.5 12.6 %copy-start.1 = (bf16[16,8192]{1,0:T(8,128)(2,1)S(1)}, bf16[16,8192]{1,0:T(8,128)(2,1)}, u32[]{:S(2)}) copy-start(bf16[16,8192]{1,0:T(8,128)(2,1)} %param.9) | copy-start | bytes 786436
  16.6 12.8 %copy-start.2 = (f32[8192]{0:T(1024)S(1)}, f32[8192]{0:T(1024)}, u32[]{:S(2)}) copy-start(f32[8192]{0:T(1024)} %param.10) | copy-start | bytes 98308
  24.7 17.9 %all-to-all-start.2 = ((bf16[128,2,1024]{2,1,0:T(2,128)(2,1)}), bf16[128,2,1024]{2,1,0:T(2,128)(2,1)S(1)}, u32[]{:S(2)}, u32[]{:S(2)}) async-start(bf16[128,2,1024]{2,1,0:T(2,128)(2,1)} %copy.53), calls=%async_computation.2 | async-start | bytes 1048576 | tf_op jit(solution)/shard_map/all_to_all | solution.py:119
  48.8 58.6 %all-to-all-start.1 = ((bf16[128,2,8192]{2,1,0:T(2,128)(2,1)}), bf16[128,2,8192]{2,1,0:T(2,128)(2,1)}, u32[]{:S(2)}, u32[]{:S(2)}) async-start(bf16[128,2,8192]{2,1,0:T(2,128)(2,1)} %bitcast.100), calls=%async_computation.1 | async-start | bytes 8388608 | tf_op jit(solution)/shard_map/all_to_all | solution.py:118
  54.4 20.9 %copy-start.4 = (s32[1,16]{1,0:T(1,128)S(1)}, s32[1,16]{1,0:T(1,128)}, u32[]{:S(2)}) copy-start(s32[1,16]{1,0:T(1,128)} %param.17) | copy-start | bytes 196
  200.7 5.5 %copy-start.3 = (s32[16,1]{0,1:T(1,128)S(1)}, s32[16,1]{0,1:T(1,128)}, u32[]{:S(2)}) copy-start(s32[16,1]{0,1:T(1,128)} %param.15) | copy-start | bytes 196
  200.7 58.5 %all-to-all-start.3 = ((bf16[128,2,8192]{2,1,0:T(2,128)(2,1)}), bf16[128,2,8192]{2,1,0:T(2,128)(2,1)}, u32[]{:S(2)}, u32[]{:S(2)}) async-start(bf16[128,2,8192]{2,1,0:T(2,128)(2,1)} %reshape.374), calls=%async_computation.3 | async-start | bytes 8388608 | tf_op jit(solution)/shard_map/all_to_all | solution.py:173
where the time goes:
time: 276 us; the launch traced here: 274 us
  waiting for transfers between devices  95.8 us (35%)
  matrix products  70.1 us (25%)
  local copies, waits for them, and re-layouts  58.5 us (21%)
  starting transfers between devices  27.1 us (10%)
  other arithmetic  22.2 us (8%)
    all_to_all x1, waiting for transfers between devices, on_device(): lax.all_to_all(partial_value.reshape(groups * ranks, capacity, width), ('...  52.9 us
    all_to_all x1, waiting for transfers between devices, on_device(): lax.all_to_all(rows_all, ('dp', 'tensor'), split_axis=0, concat_axis=0, t...  25.8 us
    dot_general x1, local copies, waits for them, and re-layouts, project_slots(): jnp.dot(slot_rows, w_query, preferred_element_type=jnp.float32)  20.9 us
    dot_general x1, matrix products, on_device(): jnp.einsum('sc,dc->sd', back_query, w_query, preferred_element_type=jnp.f...  19.3 us
    reshape x2, local copies, waits for them, and re-layouts, on_device(): slot_rows = got_rows.reshape(-1, width)  14.4 us
    all_to_all x1, starting transfers between devices, on_device(): lax.all_to_all(labels_all, ('dp', 'tensor'), split_axis=0, concat_axis=0,...  11.5 us
    all_to_all x1, waiting for transfers between devices, on_device(): lax.all_to_all(grad_all, ('dp', 'tensor'), split_axis=0, concat_axis=0, t...  10.7 us
    dot_general x1, matrix products, project_slots(): jnp.dot(slot_rows, w_query, preferred_element_type=jnp.float32)  9.35 us
  transfers between devices with their start and end apart: 4, of which 4 were waited for; matrix products, arithmetic and copies ran while one was open for 12% of the time, Pallas kernels for 0%

commit v1 on v0

v1 whole, which is shorter than its diff:
```python
import jax
import jax.numpy as jnp
from jax import lax
from jax.experimental import pallas as pl
from jax.experimental.pallas import tpu as pltpu
from jax.sharding import PartitionSpec as P

HD = 128
KC = 16
PARTS = 2
EXT = 128
STEP = 1024
EPSILON = 1e-05
BASE = 500000.0
F32 = jnp.float32
BF16 = jnp.bfloat16

VMEM = pl.BlockSpec(memory_space=pltpu.VMEM)


def params(mib=48):
    return pltpu.CompilerParams(vmem_limit_bytes=mib * 2**20)


def dot(a, b, dims):
    return lax.dot_general(a, b, (dims, ((), ())), preferred_element_type=F32)


def iota(shape, axis):
    return lax.broadcasted_iota(jnp.int32, shape, axis)


def norm_kernel(groups, hidden_ref, gain_ref, owner_ref, owner_row_ref, completion_ref, grad_ref, *outs):
    part_refs, slot_grad_ref = outs[:-1], outs[-1]
    count, width = hidden_ref.shape
    wide = hidden_ref[...].astype(F32)
    inverse = lax.rsqrt(jnp.mean(wide * wide, axis=1, keepdims=True) + EPSILON)
    normed = (wide * inverse * gain_ref[...]).astype(BF16)
    owner = owner_ref[...]
    owner_row = owner_row_ref[...]
    same = owner == owner_row
    rows, cols = iota((count, count), 0), iota((count, count), 1)
    rank = jnp.sum(jnp.where(same & (cols < rows), 1.0, 0.0), axis=1, keepdims=True)
    rank_row = jnp.sum(jnp.where(same & (rows < cols), 1.0, 0.0), axis=0, keepdims=True)
    here = lax.axis_index("tensor").astype(F32)
    slot = owner.astype(F32) * 16.0 + here * 2.0 + rank
    lane = iota((count, EXT), 1)
    ext = jnp.where(lane == 0, slot, jnp.where(lane == 1, completion_ref[...].astype(F32) + 1.0, 0.0))
    span = width // PARTS
    for i, ref in enumerate(part_refs):
        ref[:, 0:span] = normed[:, i * span : (i + 1) * span]
    part_refs[0][:, span : span + EXT] = ext.astype(BF16)
    place = owner_row.astype(F32) * 2.0 + rank_row
    pick = (iota((2 * groups, count), 0).astype(F32) == place).astype(BF16)
    slot_grad_ref[...] = dot(pick, grad_ref[...], ((1,), (0,))).astype(BF16)


def project_kernel(count, first, last, *refs):
    refs = list(refs)
    blocks = [refs.pop(0) for _ in range(count)]
    exts = [refs.pop(0) for _ in range(count)] if last else None
    wq_ref, wk_ref, wv_ref = refs.pop(0), refs.pop(0), refs.pop(0)
    before_ref = None if first else refs.pop(0)
    out_ref = refs.pop(0)
    total = refs.pop(0) if last else out_ref
    step = pl.program_id(0)
    x = jnp.concatenate([b[...] for b in blocks], axis=0)
    qc = wq_ref.shape[1]

    def add(cols, value):
        @pl.when(step == 0)
        def _():
            total[:, cols] = value if first else before_ref[:, cols] + value

        @pl.when(step > 0)
        def _():
            total[:, cols] += value

    add(slice(0, qc), dot(x, wq_ref[...], ((1,), (0,))))
    wkv = jnp.concatenate([wk_ref[...], wv_ref[...]], axis=1)
    add(slice(qc, qc + 2 * HD), dot(x, wkv, ((1,), (0,))))

    if last:

        @pl.when(step == pl.num_programs(0) - 1)
        def _():
            ext = jnp.concatenate([e[...] for e in exts], axis=0)
            rows = ext.shape[0]
            slots = out_ref.shape[0]
            hot = (ext[:, 0:1].astype(F32) == iota((rows, slots), 1).astype(F32)).astype(BF16)
            cols = total.shape[1]
            out_ref[:, 0:cols] = dot(hot, total[...].astype(BF16), ((0,), (0,))).astype(BF16)
            out_ref[:, cols : cols + EXT] = dot(hot, ext, ((0,), (0,))).astype(BF16)


def project(blocks, exts, wq, wk, wv, part, before, last, slots):
    rows = sum(b.shape[0] for b in blocks)
    span = wq.shape[0] // PARTS
    steps = span // STEP
    cols = wq.shape[1] + wk.shape[1] + wv.shape[1]
    ext_at = span // EXT
    specs = [pl.BlockSpec((b.shape[0], STEP), lambda k: (0, k)) for b in blocks]
    operands = list(blocks)
    if last:
        specs += [pl.BlockSpec((b.shape[0], EXT), lambda k: (0, ext_at)) for b in exts]
        operands += list(exts)
    for w in (wq, wk, wv):
        specs.append(pl.BlockSpec((STEP, w.shape[1]), lambda k: (k + part * steps, 0)))
        operands.append(w)
    if before is not None:
        specs.append(pl.BlockSpec((rows, cols), lambda k: (0, 0)))
        operands.append(before)
    if last:
        out = jax.ShapeDtypeStruct((slots, cols + EXT), BF16)
        out_spec = pl.BlockSpec((slots, cols + EXT), lambda k: (0, 0))
        scratch = [pltpu.VMEM((rows, cols), F32)]
    else:
        out = jax.ShapeDtypeStruct((rows, cols), F32)
        out_spec = pl.BlockSpec((rows, cols), lambda k: (0, 0))
        scratch = []

    def body(*refs):
        project_kernel(len(blocks), before is None, last, *refs)

    return pl.pallas_call(
        body,
        grid=(steps,),
        in_specs=specs,
        out_specs=out_spec,
        out_shape=out,
        scratch_shapes=scratch,
        compiler_params=params(),
        cost_estimate=pl.CostEstimate(
            flops=2 * rows * span * cols, bytes_accessed=2 * span * cols, transcendentals=0
        ),
        name="project",
    )(*operands)


def attend_kernel(ranks, got_ref, grad_ref, rewards_ref, out_ref):
    slots = got_ref.shape[0]
    heads = grad_ref.shape[1] // HD
    kcol = heads * HD
    vcol = kcol + HD
    ecol = vcol + HD
    factor = HD**-0.5
    ext = got_ref[:, ecol : ecol + EXT].astype(F32)
    label = ext[:, 1:2]
    label_row = jnp.transpose(ext)[1:2, :]
    rows, cols = iota((slots, slots), 0), iota((slots, slots), 1)
    same = label == label_row
    allowed = same & (cols <= rows)
    position = jnp.sum(jnp.where(same & (cols < rows), 1.0, 0.0), axis=1, keepdims=True)
    lane = iota((slots, HD), 1)
    half = HD // 2
    index = jnp.where(lane < half, lane, lane - half).astype(F32)
    freq = jnp.exp(index * (-2.0 / HD * jnp.log(F32(BASE))))
    angle = position * freq
    cosine = jnp.cos(angle)
    sine = jnp.where(lane < half, -jnp.sin(angle), jnp.sin(angle))

    def rope(u, sign):
        return u * cosine + pltpu.roll(u, half, 1) * (sine * sign)

    scaled = rewards_ref[...].astype(F32) / 256.0
    advantage = scaled - (jnp.sum(scaled) - scaled) / (KC - 1)
    advantage = jnp.concatenate([advantage, jnp.zeros((1, EXT - KC), F32)], axis=1)
    weight = jnp.sum(jnp.where(label - 1.0 == lane.astype(F32), advantage, 0.0), axis=1, keepdims=True)

    dp_ranks = slots // (2 * ranks)
    source = ((rows // 2) % ranks) * (2 * dp_ranks) + (rows // (2 * ranks)) * 2 + rows % 2
    move = (cols == source).astype(BF16)
    grads = dot(move, grad_ref[...], ((1,), (0,)))
    grads = (grads * weight).astype(BF16)

    key = rope(got_ref[:, kcol : kcol + HD].astype(F32), 1.0).astype(BF16)
    value = got_ref[:, vcol : vcol + HD]
    grad_key = jnp.zeros((slots, HD), F32)
    grad_value = jnp.zeros((slots, HD), F32)
    for h in range(heads):
        at = slice(h * HD, (h + 1) * HD)
        query = rope(got_ref[:, at].astype(F32), 1.0).astype(BF16)
        grad = grads[:, at]
        scores = dot(query, key, ((1,), (1,))) * factor
        scores = jnp.where(allowed, scores, -1e30)
        highest = jnp.max(scores, axis=1, keepdims=True)
        weights = jnp.exp(scores - highest)
        probs = weights / jnp.sum(weights, axis=1, keepdims=True)
        grad_value = grad_value + dot(probs.astype(BF16), grad, ((0,), (0,)))
        grad_probs = dot(grad, value, ((1,), (1,)))
        inner = jnp.sum(probs * grad_probs, axis=1, keepdims=True)
        grad_scores = (probs * (grad_probs - inner) * factor).astype(BF16)
        grad_query = dot(grad_scores, key, ((1,), (0,)))
        grad_key = grad_key + dot(grad_scores, query, ((0,), (0,)))
        out_ref[:, at] = rope(grad_query, -1.0).astype(BF16)
    out_ref[:, kcol : kcol + HD] = rope(grad_key, -1.0).astype(BF16)
    out_ref[:, vcol : vcol + HD] = grad_value.astype(BF16)


def back_kernel(count, *refs):
    exts = refs[:count]
    slots_ref, wq_ref, wk_ref, wv_ref, keep_ref, send_ref, held = refs[count:]
    half = keep_ref.shape[0]
    qc = wq_ref.shape[1]

    @pl.when(pl.program_id(0) == 0)
    def _():
        ext = jnp.concatenate([e[...] for e in exts], axis=0)
        slots = slots_ref.shape[0]
        hot = (ext[:, 0:1].astype(F32) == iota((ext.shape[0], slots), 1).astype(F32)).astype(BF16)
        held[...] = dot(hot, slots_ref[...], ((1,), (0,))).astype(BF16)

    wkv = jnp.concatenate([wk_ref[...], wv_ref[...]], axis=1)
    term = dot(held[:, 0:qc], wq_ref[...], ((1,), (1,))) + dot(held[:, qc:], wkv, ((1,), (1,)))
    term = term.astype(BF16)
    keep_ref[...] = term[0:half]
    send_ref[...] = term[half:]


def back(exts, slot_grads, wq, wk, wv, part):
    rows = sum(e.shape[0] for e in exts)
    span = wq.shape[0] // PARTS
    steps = span // STEP
    ext_at = span // EXT
    cols = wq.shape[1] + wk.shape[1] + wv.shape[1]
    specs = [pl.BlockSpec((e.shape[0], EXT), lambda k: (0, ext_at)) for e in exts]
    specs.append(pl.BlockSpec(slot_grads.shape, lambda k: (0, 0)))
    for w in (wq, wk, wv):
        specs.append(pl.BlockSpec((STEP, w.shape[1]), lambda k: (k + part * steps, 0)))

    def body(*refs):
        back_kernel(len(exts), *refs)

    out = jax.ShapeDtypeStruct((rows // 2, span), BF16)
    out_spec = pl.BlockSpec((rows // 2, STEP), lambda k: (0, k))
    return pl.pallas_call(
        body,
        grid=(steps,),
        in_specs=specs,
        out_specs=[out_spec, out_spec],
        out_shape=[out, out],
        scratch_shapes=[pltpu.VMEM((rows, cols), BF16)],
        compiler_params=params(),
        cost_estimate=pl.CostEstimate(
            flops=2 * rows * span * cols, bytes_accessed=2 * span * cols, transcendentals=0
        ),
        name="back",
    )(*exts, slot_grads, wq, wk, wv)


def finish_kernel(hidden_ref, gain_ref, *refs):
    out_ref = refs[-1]
    wide = hidden_ref[...].astype(F32)
    inverse = lax.rsqrt(jnp.mean(wide * wide, axis=1, keepdims=True) + EPSILON)
    parts = []
    for i in range(PARTS):
        a, b, c = refs[3 * i : 3 * i + 3]
        parts.append(a[...].astype(F32) + b[...].astype(F32) + c[...].astype(F32))
    scaled = jnp.concatenate(parts, axis=1) * gain_ref[...]
    inner = jnp.mean(scaled * wide, axis=1, keepdims=True)
    out_ref[...] = (inverse * scaled - wide * inverse * inverse * inverse * inner).astype(BF16)


def on_device(hidden, gain, w_query, w_key, w_value, out_grad, owner, completion, rewards):
    groups = lax.axis_size("dp")
    ranks = lax.axis_size("tensor")
    chips = ranks // 2
    count, width = hidden.shape
    query_cols = w_query.shape[1]
    slots = 2 * groups * ranks
    span = width // PARTS

    swap_pairs = [(t, t ^ 1) for t in range(ranks)]
    flow_pairs = [(t, (t // 2 + (1 if t % 2 == 0 else chips - 1)) % chips * 2 + t % 2) for t in range(ranks)]

    def swap(x):
        return lax.ppermute(x, "tensor", swap_pairs)

    def flow(x):
        return lax.ppermute(x, "tensor", flow_pairs)

    row_types = [jax.ShapeDtypeStruct((count, span + (EXT if i == 0 else 0)), BF16) for i in range(PARTS)]
    *mine, slot_grad = pl.pallas_call(
        lambda *refs: norm_kernel(groups, *refs),
        in_specs=[VMEM] * 6,
        out_specs=[VMEM] * (PARTS + 1),
        out_shape=row_types + [jax.ShapeDtypeStruct((2 * groups, width), BF16)],
        compiler_params=params(),
        name="norm",
    )(hidden, gain.reshape(1, width), owner, owner.reshape(1, count), completion.reshape(count, 1), out_grad)

    by_group = lax.all_to_all(slot_grad.reshape(groups, 2, width), "dp", split_axis=0, concat_axis=0, tiled=True)
    by_group = by_group.reshape(2 * groups, ranks, query_cols).transpose(1, 0, 2)
    by_head = lax.all_to_all(by_group, "tensor", split_axis=0, concat_axis=0, tiled=True)
    grad_slots = by_head.reshape(slots, query_cols)

    blocks = []
    total = None
    for i in range(PARTS):
        m = mine[i]
        ms = swap(m)
        near = flow(jnp.concatenate([m, ms], axis=0))
        far = flow(near[:count])
        nears = swap(near)
        fars = swap(far)
        blocks.append((m, ms, near, nears, far, fars))
    exts = blocks[0]
    for i in range(PARTS):
        last = i == PARTS - 1
        total = project(blocks[i], exts if last else None, w_query, w_key, w_value, i, total, last, slots)
    got = lax.all_to_all(
        total.reshape(groups, 2 * ranks, total.shape[1]), "dp", split_axis=0, concat_axis=0, tiled=True
    ).reshape(total.shape)

    grads = pl.pallas_call(
        lambda *refs: attend_kernel(ranks, *refs),
        in_specs=[VMEM] * 3,
        out_specs=VMEM,
        out_shape=jax.ShapeDtypeStruct((slots, total.shape[1] - EXT), BF16),
        compiler_params=params(),
        name="attend",
    )(got, grad_slots, rewards)
    slot_grads = lax.all_to_all(
        grads.reshape(groups, 2 * ranks, grads.shape[1]), "dp", split_axis=0, concat_axis=0, tiled=True
    ).reshape(grads.shape)

    m, ms, near, nears, far, fars = exts
    pieces = []
    for i in range(PARTS):
        keep, send = back((m, nears, far, ms, near, fars), slot_grads, w_query, w_key, w_value, i)
        both = (keep.astype(F32) + swap(send).astype(F32)).astype(BF16)
        passed = flow(both[3 * count :])
        onward = both[count : 3 * count]
        onward = jnp.concatenate(
            [onward[:count], (onward[count:].astype(F32) + passed.astype(F32)).astype(BF16)], axis=0
        )
        came = flow(onward)
        pieces += [both[:count], came[count:], swap(came[:count])]

    return pl.pallas_call(
        finish_kernel,
        in_specs=[VMEM] * (2 + len(pieces)),
        out_specs=VMEM,
        out_shape=jax.ShapeDtypeStruct((count, width), BF16),
        compiler_params=params(),
        name="finish",
    )(hidden, gain.reshape(1, width), *pieces)


def solution(mesh):
    return jax.shard_map(
        on_device,
        mesh=mesh,
        in_specs=(
            P(("dp", "tensor"), None),
            P(),
            P(None, "tensor"),
            P(None, "tensor"),
            P(None, "tensor"),
            P(("dp", "tensor"), None),
            P(("dp", "tensor"), None),
            P(("dp", "tensor")),
            P("dp", None),
        ),
        out_specs=P(("dp", "tensor"), None),
        check_vma=False,
    )
```

time: 276 us -> 140 us (0.51)
  waiting for transfers between devices: 95.8 us -> 14.5 us
  matrix products: 70.1 us -> 0 us
  local copies, waits for them, and re-layouts: 58.5 us -> 13 us
  Pallas kernels: 0 us -> 35.3 us
  blocking collectives: 0 us -> 32.2 us
  other arithmetic: 22.2 us -> 1.13 us
  starting transfers between devices: 27.1 us -> 42.9 us
    all_to_all x4 -> x2, waiting for transfers between devices: 95.8 us -> 0.91 us  [the longest x1 0.91 us: on_device(): lax.all_to_all(slot_grad.reshape(groups, 2, width), 'dp', split_axis=0, c...]
    dot_general x10 -> x0, matrix products: 67 us -> none  [the longest x1 19.3 us: on_device(): jnp.einsum('sc,dc->sd', back_query, w_query, preferred_element_type=jnp.f...]
    pallas_call x0 -> x7, Pallas kernels: none -> 35.3 us  [the longest x2 13.5 us: back(): pl.pallas_call(body, grid=(steps,), in_specs=specs, out_specs=[out_spec,...]
    all_to_all x0 -> x2, blocking collectives: none -> 32.2 us  [the longest x1 17.8 us: on_device(): lax.all_to_all(total.reshape(groups, 2 * ranks, total.shape[1]), 'dp', sp...]
    ppermute x0 -> x18, starting transfers between devices: none -> 29.3 us  [the longest x8 14.8 us: flow(): return lax.ppermute(x, 'tensor', flow_pairs)]
    reshape x6 -> x3, local copies, waits for them, and re-layouts: 25.3 us -> 4.17 us  [the longest x1 2.26 us: on_device(): by_group.reshape(2 * groups, ranks, query_cols).transpose(1, 0, 2)]
    dot_general x1 -> x0, local copies, waits for them, and re-layouts: 20.9 us -> none  [project_slots(): jnp.dot(slot_rows, w_query, preferred_element_type=jnp.float32)]
    ppermute x0 -> x18, waiting for transfers between devices: none -> 13.6 us  [the longest x8 11.6 us: flow(): return lax.ppermute(x, 'tensor', flow_pairs)]
  transfers between devices with their start and end apart: 4 -> 20, of which waited for: 4 -> 8; matrix products, arithmetic and copies ran while one was open for 12% -> 5% of each run, Pallas kernels for 0% -> 14%
where the time goes in v1:
time: 140 us; the launch traced here: 139 us
  starting transfers between devices  42.9 us (31%)
  Pallas kernels  35.3 us (25%)
  blocking collectives  32.2 us (23%)
  waiting for transfers between devices  14.5 us (10%)
  local copies, waits for them, and re-layouts  13 us (9%)
    all_to_all x1, blocking collectives, on_device(): lax.all_to_all(total.reshape(groups, 2 * ranks, total.shape[1]), 'dp', sp...  17.8 us
    ppermute x8, starting transfers between devices, flow(): return lax.ppermute(x, 'tensor', flow_pairs)  14.8 us
    ppermute x10, starting transfers between devices, swap(): return lax.ppermute(x, 'tensor', swap_pairs)  14.5 us
    all_to_all x1, blocking collectives, on_device(): lax.all_to_all(grads.reshape(groups, 2 * ranks, grads.shape[1]), 'dp', sp...  14.4 us
    pallas_call x2, Pallas kernels, back(): pl.pallas_call(body, grid=(steps,), in_specs=specs, out_specs=[out_spec,...  13.5 us
    pallas_call x2, Pallas kernels, project(): pl.pallas_call(body, grid=(steps,), in_specs=specs, out_specs=out_spec, o...  13.5 us
    ppermute x8, waiting for transfers between devices, flow(): return lax.ppermute(x, 'tensor', flow_pairs)  11.6 us
    all_to_all x1, starting transfers between devices, on_device(): lax.all_to_all(slot_grad.reshape(groups, 2, width), 'dp', split_axis=0, c...  7.74 us
  transfers between devices with their start and end apart: 20, of which 8 were waited for; matrix products, arithmetic and copies ran while one was open for 5% of the time, Pallas kernels for 14%

profile of v1, /device:TPU:1, one launch (start us, length us, event | category | flops | bytes accessed | tf_op | source)
XLA Modules:
  0.0 139.3 jit_solution(11323934194616682258)
XLA Ops:
  0.0 0.7 copy.16.refs_4_
  0.7 0.7 copy.15.refs_2_
  1.5 0.9 copy-done.3
  2.4 0.9 copy-done.9
  3.4 0.8 copy-done.10
  4.1 0.7 copy-done.12
  4.8 0.4 norm.1
  5.2 1.5 %collective-permute-start = (bf16[16,4224]{1,0:T(8,128)(2,1)S(1)}, bf16[16,4224]{1,0:T(8,128)(2,1)S(1)}, u32[]{:S(2)}, u32[]{:S(2)}) collective-permute-start(bf16[16,4224]{1,0:T(8,128)(2,1)S(1)} %get-tuple-element.12.refs_0_.refs_6_), channel_id=1, source_target_pairs={{0,1},{1,0},{2,3},{3,2},{4,5},{5,4},{6,7},{7,6},{8,9},{9,8},{10,11... | collective-permute-start | bytes 405512 | tf_op jit(solution)/shard_map/ppermute | solution.py:277
  6.7 1.2 reshape.36
  7.9 7.7 %all-to-all-start.1 = ((bf16[16,2,8192]{2,1,0:T(2,128)(2,1)}), bf16[16,2,8192]{2,1,0:T(2,128)(2,1)}, u32[]{:S(2)}, u32[]{:S(2)}) async-start(bf16[16,2,8192]{2,1,0:T(2,128)(2,1)} %reshape.36), calls=%async_computation.1 | async-start | bytes 1048576 | tf_op jit(solution)/shard_map/all_to_all | solution.py:292
  15.6 0.4 collective-permute-start.5
  16.0 2.8 %collective-permute-start.1 = (bf16[32,4224]{1,0:T(8,128)(2,1)S(1)}, bf16[32,4224]{1,0:T(8,128)(2,1)S(1)}, u32[]{:S(2)}, u32[]{:S(2)}) collective-permute-start(bf16[32,4224]{1,0:T(8,128)(2,1)S(1)} %pad_maximum_fusion), channel_id=1, source_target_pairs={{0,2},{1,7},{2,4},{3,1},{4,6},{5,3},{6,0},{7,5},{8,10},{9,15},{10,... | collective-permute-start | bytes 811016 | tf_op jit(solution)/shard_map/ppermute | solution.py:280
  18.8 0.7 pad_maximum_fusion.1
  19.6 0.9 collective-permute-start.6
  20.5 1.7 %collective-permute-done.1.refs_2_.refs_8_.refs_4_ = bf16[32,4224]{1,0:T(8,128)(2,1)S(1)} collective-permute-done((bf16[32,4224]{1,0:T(8,128)(2,1)S(1)}, bf16[32,4224]{1,0:T(8,128)(2,1)S(1)}, u32[]{:S(2)}, u32[]{:S(2)}) %collective-permute-start.1) | collective-permute-done | bytes 270368 | tf_op jit(solution)/shard_map/ppermute | solution.py:280
  22.2 3.6 %collective-permute-start.3 = (bf16[16,4224]{1,0:T(8,128)(2,1)S(1)}, bf16[16,4224]{1,0:T(8,128)(2,1)S(1)}, u32[]{:S(2)}, u32[]{:S(2)}) collective-permute-start(bf16[16,4224]{1,0:T(8,128)(2,1)S(1)} %slice.62), channel_id=1, source_target_pairs={{0,2},{1,7},{2,4},{3,1},{4,6},{5,3},{6,0},{7,5},{8,10},{9,15},{10,... | collective-permute-start | bytes 405512 | tf_op jit(solution)/shard_map/ppermute | solution.py:280
  25.8 0.9 all-to-all-done.1
  26.7 2.3 %reshape.37 = bf16[32,8,1024]{2,1,0:T(8,128)(2,1)} reshape(bf16[16,2,8192]{2,1,0:T(2,128)(2,1)} %all-to-all-done.1) | data formatting | bytes 1048576 | tf_op jit(solution)/shard_map/reshape | solution.py:293
  29.0 2.1 %copy.17 = bf16[8,32,1024]{2,1,0:T(8,128)(2,1)} copy(bf16[8,32,1024]{2,0,1:T(8,128)(2,1)} %bitcast.17) | data formatting | bytes 1048576 | tf_op jit(solution)/shard_map/transpose | solution.py:293
  31.1 5.9 %all-to-all-start.2 = ((bf16[8,32,1024]{2,1,0:T(8,128)(2,1)}), bf16[8,32,1024]{2,1,0:T(8,128)(2,1)}, u32[]{:S(2)}, u32[]{:S(2)}) async-start(bf16[8,32,1024]{2,1,0:T(8,128)(2,1)} %copy.17), calls=%async_computation.2 | async-start | bytes 1048576 | tf_op jit(solution)/shard_map/all_to_all | solution.py:294
  37.0 2.7 %collective-permute-start.8 = (bf16[16,4096]{1,0:T(8,128)(2,1)S(1)}, bf16[16,4096]{1,0:T(8,128)(2,1)S(1)}, u32[]{:S(2)}, u32[]{:S(2)}) collective-permute-start(bf16[16,4096]{1,0:T(8,128)(2,1)S(1)} %slice.63), channel_id=1, source_target_pairs={{0,2},{1,7},{2,4},{3,1},{4,6},{5,3},{6,0},{7,5},{8,10},{9,15},{10,... | collective-permute-start | bytes 393224 | tf_op jit(solution)/shard_map/ppermute | solution.py:280
  39.7 0.5 collective-permute-start.4
  40.2 6.8 %collective-permute-done.8.refs_4_ = bf16[16,4096]{1,0:T(8,128)(2,1)S(1)} collective-permute-done((bf16[16,4096]{1,0:T(8,128)(2,1)S(1)}, bf16[16,4096]{1,0:T(8,128)(2,1)S(1)}, u32[]{:S(2)}, u32[]{:S(2)}) %collective-permute-start.8) | collective-permute-done | bytes 131104 | tf_op jit(solution)/shard_map/ppermute | solution.py:280
  47.0 1.5 %collective-permute-start.9 = (bf16[16,4096]{1,0:T(8,128)(2,1)S(1)}, bf16[16,4096]{1,0:T(8,128)(2,1)S(1)}, u32[]{:S(2)}, u32[]{:S(2)}) collective-permute-start(bf16[16,4096]{1,0:T(8,128)(2,1)S(1)} %collective-permute-done.8.refs_4_), channel_id=1, source_target_pairs={{0,1},{1,0},{2,3},{3,2},{4,5},{5,4},{6,7},{7,6},{8,9},{9,8},{10,11... | collective-permute-start | bytes 393224 | tf_op jit(solution)/shard_map/ppermute | solution.py:277
  48.5 1.6 %copy-done.1 = bf16[8192,128]{1,0:T(8,128)(2,1)S(1)} copy-done((bf16[8192,128]{1,0:T(8,128)(2,1)S(1)}, bf16[8192,128]{1,0:T(8,128)(2,1)}, u32[]{:S(2)}) %copy-start.1) | copy-done | bytes 2097176
  50.1 6.7 %project.2.refs_15_ = f32[128,1280]{1,0:T(8,128)S(1)} custom-call(bf16[16,4224]{1,0:T(8,128)(2,1)S(1)} %get-tuple-element.12.refs_0_.refs_6_, bf16[16,4224]{1,0:T(8,128)(2,1)S(1)} %collective-permute-done.refs_1_.refs_7_.refs_3_, bf16[32,4224]{1,0:T(8,128)(2,1)S(1)} %collective-permute-done.1.refs_2_.refs_8_.refs_4_, ...), custom_call_target="tpu_custom_call" | custom-call | flops 1342177280 | bytes 10485760 | tf_op jit(solution)/shard_map/project/pallas_call | solution.py:125
  56.8 6.8 %project.3 = bf16[256,1408]{1,0:T(8,128)(2,1)S(1)} custom-call(bf16[16,4096]{1,0:T(8,128)(2,1)S(1)} %copy-done.6, bf16[16,4096]{1,0:T(8,128)(2,1)S(1)} %copy-done.8, bf16[32,4096]{1,0:T(8,128)(2,1)S(1)} %collective-permute-done.6.refs_2_, bf16[32,4096]{1,0:T(8,128)(2,1)S(1)} %collective-permute-done.7.refs_3_, ...), custom_call_target="tpu_custom_call" | custom-call | flops 1342177280 | bytes 10485760 | tf_op jit(solution)/shard_map/project/pallas_call | solution.py:125
  63.6 0.9 copy-done.2
  64.5 17.8 %all_to_all.20 = bf16[16,16,1408]{2,1,0:T(8,128)(2,1)S(1)} all-to-all(bf16[16,16,1408]{2,1,0:T(8,128)(2,1)} %bitcast.11), channel_id=1, replica_groups=mesh['dp'=16,'tensor'=8] {'dp'}, dimensions={0} | all-to-all | bytes 1441792 | tf_op jit(solution)/shard_map/all_to_all | solution.py:311
  82.3 6.9 %attend.1 = bf16[256,1280]{1,0:T(8,128)(2,1)S(1)} custom-call(bf16[256,1408]{1,0:T(8,128)(2,1)S(1)} %bitcast.12, bf16[256,1024]{1,0:T(8,128)(2,1)} %bitcast.6.refs_1_, s32[1,16]{1,0:T(1,128)S(1)} %copy-done.13), custom_call_target="tpu_custom_call" | custom-call | tf_op jit(solution)/shard_map/attend/pallas_call | solution.py:315
  89.2 14.4 %all_to_all.21 = bf16[16,16,1280]{2,1,0:T(8,128)(2,1)S(1)} all-to-all(bf16[16,16,1280]{2,1,0:T(8,128)(2,1)S(1)} %bitcast.13), channel_id=1, replica_groups=mesh['dp'=16,'tensor'=8] {'dp'}, dimensions={0} | all-to-all | bytes 1310720 | tf_op jit(solution)/shard_map/all_to_all | solution.py:323
  103.6 6.7 %back.3 = (bf16[64,4096]{1,0:T(8,128)(2,1)S(1)}, bf16[64,4096]{1,0:T(8,128)(2,1)S(1)}) custom-call(bf16[16,4224]{1,0:T(8,128)(2,1)S(1)} %get-tuple-element.12.refs_0_.refs_6_, bf16[32,4224]{1,0:T(8,128)(2,1)S(1)} %collective-permute-done.2.refs_3_.refs_9_.refs_1_, bf16[16,4224]{1,0:T(8,128)(2,1)S(1)} %collective-permute-done.3.refs_4_.refs_10_.refs_2_, ...), custom_call_target="tpu_custom_call" | custom-call | flops 1342177280 | bytes 10485760 | tf_op jit(solution)/shard_map/back/pallas_call | solution.py:236
  110.3 2.5 %collective-permute-start.14 = (bf16[64,4096]{1,0:T(8,128)(2,1)S(1)}, bf16[64,4096]{1,0:T(8,128)(2,1)S(1)}, u32[]{:S(2)}, u32[]{:S(2)}) collective-permute-start(bf16[64,4096]{1,0:T(8,128)(2,1)S(1)} %get-tuple-element.18), channel_id=1, source_target_pairs={{0,1},{1,0},{2,3},{3,2},{4,5},{5,4},{6,7},{7,6},{8,9},{9,8},{10,11... | collective-permute-start | bytes 1572872 | tf_op jit(solution)/shard_map/ppermute | solution.py:277
  112.9 6.7 %back.2 = (bf16[64,4096]{1,0:T(8,128)(2,1)S(1)}, bf16[64,4096]{1,0:T(8,128)(2,1)S(1)}) custom-call(bf16[16,4224]{1,0:T(8,128)(2,1)S(1)} %get-tuple-element.12.refs_0_.refs_6_, bf16[32,4224]{1,0:T(8,128)(2,1)S(1)} %collective-permute-done.2.refs_3_.refs_9_.refs_1_, bf16[16,4224]{1,0:T(8,128)(2,1)S(1)} %collective-permute-done.3.refs_4_.refs_10_.refs_2_, ...), custom_call_target="tpu_custom_call" | custom-call | flops 1342177280 | bytes 10485760 | tf_op jit(solution)/shard_map/back/pallas_call | solution.py:236
  119.7 0.1 add_convert_fusion
  119.9 0.7 collective-permute-start.15
  120.6 1.0 collective-permute-done.10
  121.6 0.1 add_convert_fusion.1
  121.8 0.7 collective-permute-start.11
  122.5 1.3 collective-permute-done.15
  123.8 1.9 %collective-permute-start.16 = (bf16[32,4096]{1,0:T(8,128)(2,1)S(1)}, bf16[32,4096]{1,0:T(8,128)(2,1)S(1)}, u32[]{:S(2)}, u32[]{:S(2)}) collective-permute-start(bf16[32,4096]{1,0:T(8,128)(2,1)S(1)} %pad_maximum_fusion.3), channel_id=1, source_target_pairs={{0,2},{1,7},{2,4},{3,1},{4,6},{5,3},{6,0},{7,5},{8,10},{9,15},{10,... | collective-permute-start | bytes 786440 | tf_op jit(solution)/shard_map/ppermute | solution.py:280
  125.7 0.2 collective-permute-done.11
  126.0 1.6 %collective-permute-start.12 = (bf16[32,4096]{1,0:T(8,128)(2,1)S(1)}, bf16[32,4096]{1,0:T(8,128)(2,1)S(1)}, u32[]{:S(2)}, u32[]{:S(2)}) collective-permute-start(bf16[32,4096]{1,0:T(8,128)(2,1)S(1)} %pad_maximum_fusion.2), channel_id=1, source_target_pairs={{0,2},{1,7},{2,4},{3,1},{4,6},{5,3},{6,0},{7,5},{8,10},{9,15},{10,... | collective-permute-start | bytes 786440 | tf_op jit(solution)/shard_map/ppermute | solution.py:280
  127.6 1.5 %collective-permute-done.16 = bf16[32,4096]{1,0:T(8,128)(2,1)S(1)} collective-permute-done((bf16[32,4096]{1,0:T(8,128)(2,1)S(1)}, bf16[32,4096]{1,0:T(8,128)(2,1)S(1)}, u32[]{:S(2)}, u32[]{:S(2)}) %collective-permute-start.16) | collective-permute-done | bytes 262176 | tf_op jit(solution)/shard_map/ppermute | solution.py:280
  129.1 5.3 %collective-permute-start.17 = (bf16[16,4096]{1,0:T(8,128)(2,1)S(1)}, bf16[16,4096]{1,0:T(8,128)(2,1)S(1)}, u32[]{:S(2)}, u32[]{:S(2)}) collective-permute-start(bf16[16,4096]{1,0:T(8,128)(2,1)S(1)} %get-tuple-element.25), channel_id=1, source_target_pairs={{0,1},{1,0},{2,3},{3,2},{4,5},{5,4},{6,7},{7,6},{8,9},{9,8},{10,11... | collective-permute-start | bytes 393224 | tf_op jit(solution)/shard_map/ppermute | solution.py:277
  134.5 2.8 %collective-permute-start.13 = (bf16[16,4096]{1,0:T(8,128)(2,1)S(1)}, bf16[16,4096]{1,0:T(8,128)(2,1)S(1)}, u32[]{:S(2)}, u32[]{:S(2)}) collective-permute-start(bf16[16,4096]{1,0:T(8,128)(2,1)S(1)} %get-tuple-element.27), channel_id=1, source_target_pairs={{0,1},{1,0},{2,3},{3,2},{4,5},{5,4},{6,7},{7,6},{8,9},{9,8},{10,11... | collective-permute-start | bytes 393224 | tf_op jit(solution)/shard_map/ppermute | solution.py:277
  137.2 1.0 collective-permute-done.13.refs_2_
  138.2 1.1 finish.1
  (48 shorter events, 0.5 us)
Async XLA Ops:
  1.5 0.9 copy-start.3
  2.4 0.9 copy-start.9
  3.4 0.8 copy-start.10
  4.1 0.7 copy-start.12
  5.2 17.1 %copy-start.5 = (bf16[16,4096]{1,0:T(8,128)(2,1)}, bf16[16,4096]{1,0:T(8,128)(2,1)S(1)}, u32[]{:S(2)}) copy-start(bf16[16,4096]{1,0:T(8,128)(2,1)S(1)} %get-tuple-element.13.refs_0_) | copy-start | bytes 393220
  5.2 10.8 %collective-permute-start = (bf16[16,4224]{1,0:T(8,128)(2,1)S(1)}, bf16[16,4224]{1,0:T(8,128)(2,1)S(1)}, u32[]{:S(2)}, u32[]{:S(2)}) collective-permute-start(bf16[16,4224]{1,0:T(8,128)(2,1)S(1)} %get-tuple-element.12.refs_0_.refs_6_), channel_id=1, source_target_pairs={{0,1},{1,0},{2,3},{3,2},{4,5},{5,4},{6,7},{7,6},{8,9},{9,8},{10,11... | collective-permute-start | bytes 405512 | tf_op jit(solution)/shard_map/ppermute | solution.py:277
  7.9 18.9 %all-to-all-start.1 = ((bf16[16,2,8192]{2,1,0:T(2,128)(2,1)}), bf16[16,2,8192]{2,1,0:T(2,128)(2,1)}, u32[]{:S(2)}, u32[]{:S(2)}) async-start(bf16[16,2,8192]{2,1,0:T(2,128)(2,1)} %reshape.36), calls=%async_computation.1 | async-start | bytes 1048576 | tf_op jit(solution)/shard_map/all_to_all | solution.py:292
  15.6 3.2 %collective-permute-start.5 = (bf16[16,4096]{1,0:T(8,128)(2,1)S(1)}, bf16[16,4096]{1,0:T(8,128)(2,1)S(1)}, u32[]{:S(2)}, u32[]{:S(2)}) collective-permute-start(bf16[16,4096]{1,0:T(8,128)(2,1)S(1)} %get-tuple-element.13.refs_0_), channel_id=1, source_target_pairs={{0,1},{1,0},{2,3},{3,2},{4,5},{5,4},{6,7},{7,6},{8,9},{9,8},{10,11... | collective-permute-start | bytes 393224 | tf_op jit(solution)/shard_map/ppermute | solution.py:277
  16.0 32.5 %copy-start = (bf16[8192,128]{1,0:T(8,128)(2,1)S(1)}, bf16[8192,128]{1,0:T(8,128)(2,1)}, u32[]{:S(2)}) copy-start(bf16[8192,128]{1,0:T(8,128)(2,1)} %refs_8_.5) | copy-start | bytes 6291460
  16.0 6.2 %collective-permute-start.1 = (bf16[32,4224]{1,0:T(8,128)(2,1)S(1)}, bf16[32,4224]{1,0:T(8,128)(2,1)S(1)}, u32[]{:S(2)}, u32[]{:S(2)}) collective-permute-start(bf16[32,4224]{1,0:T(8,128)(2,1)S(1)} %pad_maximum_fusion), channel_id=1, source_target_pairs={{0,2},{1,7},{2,4},{3,1},{4,6},{5,3},{6,0},{7,5},{8,10},{9,15},{10,... | collective-permute-start | bytes 811016 | tf_op jit(solution)/shard_map/ppermute | solution.py:280
  18.8 7.0 %copy-start.7 = (bf16[16,4096]{1,0:T(8,128)(2,1)}, bf16[16,4096]{1,0:T(8,128)(2,1)S(1)}, u32[]{:S(2)}) copy-start(bf16[16,4096]{1,0:T(8,128)(2,1)S(1)} %collective-permute-done.5.refs_1_) | copy-start | bytes 393220
  19.6 17.4 %collective-permute-start.6 = (bf16[32,4096]{1,0:T(8,128)(2,1)}, bf16[32,4096]{1,0:T(8,128)(2,1)S(1)}, u32[]{:S(2)}, u32[]{:S(2)}) collective-permute-start(bf16[32,4096]{1,0:T(8,128)(2,1)} %pad_maximum_fusion.1), channel_id=1, source_target_pairs={{0,2},{1,7},{2,4},{3,1},{4,6},{5,3},{6,0},{7,5},{8,10},{9,15},{10,... | collective-permute-start | bytes 786440 | tf_op jit(solution)/shard_map/ppermute | solution.py:280
  22.2 17.5 %collective-permute-start.3 = (bf16[16,4224]{1,0:T(8,128)(2,1)S(1)}, bf16[16,4224]{1,0:T(8,128)(2,1)S(1)}, u32[]{:S(2)}, u32[]{:S(2)}) collective-permute-start(bf16[16,4224]{1,0:T(8,128)(2,1)S(1)} %slice.62), channel_id=1, source_target_pairs={{0,2},{1,7},{2,4},{3,1},{4,6},{5,3},{6,0},{7,5},{8,10},{9,15},{10,... | collective-permute-start | bytes 405512 | tf_op jit(solution)/shard_map/ppermute | solution.py:280
  25.8 22.6 %collective-permute-start.2 = (bf16[32,4224]{1,0:T(8,128)(2,1)S(1)}, bf16[32,4224]{1,0:T(8,128)(2,1)S(1)}, u32[]{:S(2)}, u32[]{:S(2)}) collective-permute-start(bf16[32,4224]{1,0:T(8,128)(2,1)S(1)} %collective-permute-done.1.refs_2_.refs_8_.refs_4_), channel_id=1, source_target_pairs={{0,1},{1,0},{2,3},{3,2},{4,5},{5,4},{6,7},{7,6},{8,9},{9,8},{10,11... | collective-permute-start | bytes 811016 | tf_op jit(solution)/shard_map/ppermute | solution.py:277
  31.1 33.3 %all-to-all-start.2 = ((bf16[8,32,1024]{2,1,0:T(8,128)(2,1)}), bf16[8,32,1024]{2,1,0:T(8,128)(2,1)}, u32[]{:S(2)}, u32[]{:S(2)}) async-start(bf16[8,32,1024]{2,1,0:T(8,128)(2,1)} %copy.17), calls=%async_computation.2 | async-start | bytes 1048576 | tf_op jit(solution)/shard_map/all_to_all | solution.py:294
  37.0 19.8 %copy-start.6 = (bf16[16,4096]{1,0:T(8,128)(2,1)S(1)}, bf16[16,4096]{1,0:T(8,128)(2,1)}, u32[]{:S(2)}) copy-start(bf16[16,4096]{1,0:T(8,128)(2,1)} %copy-done.5) | copy-start | bytes 393220
  37.0 19.8 %copy-start.8 = (bf16[16,4096]{1,0:T(8,128)(2,1)S(1)}, bf16[16,4096]{1,0:T(8,128)(2,1)}, u32[]{:S(2)}) copy-start(bf16[16,4096]{1,0:T(8,128)(2,1)} %copy-done.7) | copy-start | bytes 393220
  37.0 10.0 %collective-permute-start.8 = (bf16[16,4096]{1,0:T(8,128)(2,1)S(1)}, bf16[16,4096]{1,0:T(8,128)(2,1)S(1)}, u32[]{:S(2)}, u32[]{:S(2)}) collective-permute-start(bf16[16,4096]{1,0:T(8,128)(2,1)S(1)} %slice.63), channel_id=1, source_target_pairs={{0,2},{1,7},{2,4},{3,1},{4,6},{5,3},{6,0},{7,5},{8,10},{9,15},{10,... | collective-permute-start | bytes 393224 | tf_op jit(solution)/shard_map/ppermute | solution.py:280
  39.7 17.1 %collective-permute-start.7 = (bf16[32,4096]{1,0:T(8,128)(2,1)S(1)}, bf16[32,4096]{1,0:T(8,128)(2,1)S(1)}, u32[]{:S(2)}, u32[]{:S(2)}) collective-permute-start(bf16[32,4096]{1,0:T(8,128)(2,1)S(1)} %collective-permute-done.6.refs_2_), channel_id=1, source_target_pairs={{0,1},{1,0},{2,3},{3,2},{4,5},{5,4},{6,7},{7,6},{8,9},{9,8},{10,11... | collective-permute-start | bytes 786440 | tf_op jit(solution)/shard_map/ppermute | solution.py:277
  39.7 8.8 %collective-permute-start.4 = (bf16[16,4224]{1,0:T(8,128)(2,1)S(1)}, bf16[16,4224]{1,0:T(8,128)(2,1)S(1)}, u32[]{:S(2)}, u32[]{:S(2)}) collective-permute-start(bf16[16,4224]{1,0:T(8,128)(2,1)S(1)} %collective-permute-done.3.refs_4_.refs_10_.refs_2_), channel_id=1, source_target_pairs={{0,1},{1,0},{2,3},{3,2},{4,5},{5,4},{6,7},{7,6},{8,9},{9,8},{10,11... | collective-permute-start | bytes 405512 | tf_op jit(solution)/shard_map/ppermute | solution.py:277
  47.0 9.8 %collective-permute-start.9 = (bf16[16,4096]{1,0:T(8,128)(2,1)S(1)}, bf16[16,4096]{1,0:T(8,128)(2,1)S(1)}, u32[]{:S(2)}, u32[]{:S(2)}) collective-permute-start(bf16[16,4096]{1,0:T(8,128)(2,1)S(1)} %collective-permute-done.8.refs_4_), channel_id=1, source_target_pairs={{0,1},{1,0},{2,3},{3,2},{4,5},{5,4},{6,7},{7,6},{8,9},{9,8},{10,11... | collective-permute-start | bytes 393224 | tf_op jit(solution)/shard_map/ppermute | solution.py:277
  48.5 1.6 %copy-start.1 = (bf16[8192,128]{1,0:T(8,128)(2,1)S(1)}, bf16[8192,128]{1,0:T(8,128)(2,1)}, u32[]{:S(2)}) copy-start(bf16[8192,128]{1,0:T(8,128)(2,1)} %refs_9_.3) | copy-start | bytes 6291460
  56.8 25.5 %copy-start.13 = (s32[1,16]{1,0:T(1,128)S(1)}, s32[1,16]{1,0:T(1,128)}, u32[]{:S(2)}) copy-start(s32[1,16]{1,0:T(1,128)} %refs_2_.2) | copy-start | bytes 196
  63.6 0.9 copy-start.2
  110.3 9.4 %collective-permute-start.14 = (bf16[64,4096]{1,0:T(8,128)(2,1)S(1)}, bf16[64,4096]{1,0:T(8,128)(2,1)S(1)}, u32[]{:S(2)}, u32[]{:S(2)}) collective-permute-start(bf16[64,4096]{1,0:T(8,128)(2,1)S(1)} %get-tuple-element.18), channel_id=1, source_target_pairs={{0,1},{1,0},{2,3},{3,2},{4,5},{5,4},{6,7},{7,6},{8,9},{9,8},{10,11... | collective-permute-start | bytes 1572872 | tf_op jit(solution)/shard_map/ppermute | solution.py:277
  119.6 2.0 %collective-permute-start.10 = (bf16[64,4096]{1,0:T(8,128)(2,1)S(1)}, bf16[64,4096]{1,0:T(8,128)(2,1)S(1)}, u32[]{:S(2)}, u32[]{:S(2)}) collective-permute-start(bf16[64,4096]{1,0:T(8,128)(2,1)S(1)} %get-tuple-element.16), channel_id=1, source_target_pairs={{0,1},{1,0},{2,3},{3,2},{4,5},{5,4},{6,7},{7,6},{8,9},{9,8},{10,11... | collective-permute-start | bytes 1572872 | tf_op jit(solution)/shard_map/ppermute | solution.py:277
  119.9 3.9 %collective-permute-start.15 = (bf16[16,4096]{1,0:T(8,128)(2,1)S(1)}, bf16[16,4096]{1,0:T(8,128)(2,1)S(1)}, u32[]{:S(2)}, u32[]{:S(2)}) collective-permute-start(bf16[16,4096]{1,0:T(8,128)(2,1)S(1)} %get-tuple-element.20), channel_id=1, source_target_pairs={{0,2},{1,7},{2,4},{3,1},{4,6},{5,3},{6,0},{7,5},{8,10},{9,15},{10,... | collective-permute-start | bytes 393224 | tf_op jit(solution)/shard_map/ppermute | solution.py:280
  121.7 16.5 %copy-start.4 = (bf16[16,8192]{1,0:T(8,128)(2,1)S(1)}, bf16[16,8192]{1,0:T(8,128)(2,1)}, u32[]{:S(2)}) copy-start(bf16[16,8192]{1,0:T(8,128)(2,1)} %hidden_ref.1) | copy-start | bytes 786436
  121.7 16.5 %copy-start.11 = (f32[8192]{0:T(1024)S(1)}, f32[8192]{0:T(1024)}, u32[]{:S(2)}) copy-start(f32[8192]{0:T(1024)} %param.10) | copy-start | bytes 98308
  121.8 4.2 %collective-permute-start.11 = (bf16[16,4096]{1,0:T(8,128)(2,1)S(1)}, bf16[16,4096]{1,0:T(8,128)(2,1)S(1)}, u32[]{:S(2)}, u32[]{:S(2)}) collective-permute-start(bf16[16,4096]{1,0:T(8,128)(2,1)S(1)} %get-tuple-element.23), channel_id=1, source_target_pairs={{0,2},{1,7},{2,4},{3,1},{4,6},{5,3},{6,0},{7,5},{8,10},{9,15},{10,... | collective-permute-start | bytes 393224 | tf_op jit(solution)/shard_map/ppermute | solution.py:280
  123.8 5.3 %collective-permute-start.16 = (bf16[32,4096]{1,0:T(8,128)(2,1)S(1)}, bf16[32,4096]{1,0:T(8,128)(2,1)S(1)}, u32[]{:S(2)}, u32[]{:S(2)}) collective-permute-start(bf16[32,4096]{1,0:T(8,128)(2,1)S(1)} %pad_maximum_fusion.3), channel_id=1, source_target_pairs={{0,2},{1,7},{2,4},{3,1},{4,6},{5,3},{6,0},{7,5},{8,10},{9,15},{10,... | collective-permute-start | bytes 786440 | tf_op jit(solution)/shard_map/ppermute | solution.py:280
  126.0 8.4 %collective-permute-start.12 = (bf16[32,4096]{1,0:T(8,128)(2,1)S(1)}, bf16[32,4096]{1,0:T(8,128)(2,1)S(1)}, u32[]{:S(2)}, u32[]{:S(2)}) collective-permute-start(bf16[32,4096]{1,0:T(8,128)(2,1)S(1)} %pad_maximum_fusion.2), channel_id=1, source_target_pairs={{0,2},{1,7},{2,4},{3,1},{4,6},{5,3},{6,0},{7,5},{8,10},{9,15},{10,... | collective-permute-start | bytes 786440 | tf_op jit(solution)/shard_map/ppermute | solution.py:280
  129.1 8.1 %collective-permute-start.17 = (bf16[16,4096]{1,0:T(8,128)(2,1)S(1)}, bf16[16,4096]{1,0:T(8,128)(2,1)S(1)}, u32[]{:S(2)}, u32[]{:S(2)}) collective-permute-start(bf16[16,4096]{1,0:T(8,128)(2,1)S(1)} %get-tuple-element.25), channel_id=1, source_target_pairs={{0,1},{1,0},{2,3},{3,2},{4,5},{5,4},{6,7},{7,6},{8,9},{9,8},{10,11... | collective-permute-start | bytes 393224 | tf_op jit(solution)/shard_map/ppermute | solution.py:277
  134.5 3.8 %collective-permute-start.13 = (bf16[16,4096]{1,0:T(8,128)(2,1)S(1)}, bf16[16,4096]{1,0:T(8,128)(2,1)S(1)}, u32[]{:S(2)}, u32[]{:S(2)}) collective-permute-start(bf16[16,4096]{1,0:T(8,128)(2,1)S(1)} %get-tuple-element.27), channel_id=1, source_target_pairs={{0,1},{1,0},{2,3},{3,2},{4,5},{5,4},{6,7},{7,6},{8,9},{9,8},{10,11... | collective-permute-start | bytes 393224 | tf_op jit(solution)/shard_map/ppermute | solution.py:277

commit v2 on v1

v2 whole, which is shorter than its diff:
```python
import jax
import jax.numpy as jnp
from jax import lax
from jax.experimental import pallas as pl
from jax.experimental.pallas import tpu as pltpu
from jax.sharding import PartitionSpec as P

HD = 128
KC = 16
PARTS = 2
EXT = 128
STEP = 1024
PIECES = 4
EPSILON = 1e-05
BASE = 500000.0
F32 = jnp.float32
BF16 = jnp.bfloat16

VMEM = pl.BlockSpec(memory_space=pltpu.VMEM)
ANY = pl.BlockSpec(memory_space=pl.ANY)


def params(mib=12):
    return pltpu.CompilerParams(vmem_limit_bytes=mib * 2**20)


def in_hbm(x):
    return pltpu.with_memory_space_constraint(x, pltpu.HBM)


def dot(a, b, dims):
    return lax.dot_general(a, b, (dims, ((), ())), preferred_element_type=F32)


def iota(shape, axis):
    return lax.broadcasted_iota(jnp.int32, shape, axis)


def norm_kernel(hidden_hbm, gain_hbm, owner_hbm, completion_hbm, out_ref, *rest):
    hidden_ref, gain_ref, owner_ref, completion_ref, sems = rest
    copies = [
        pltpu.make_async_copy(src, dst, sems.at[i])
        for i, (src, dst) in enumerate(
            (
                (hidden_hbm, hidden_ref),
                (gain_hbm, gain_ref),
                (owner_hbm, owner_ref),
                (completion_hbm, completion_ref),
            )
        )
    ]
    for copy in copies:
        copy.start()
    for copy in copies:
        copy.wait()
    count, width = hidden_ref.shape
    wide = hidden_ref[...].astype(F32)
    inverse = lax.rsqrt(jnp.mean(wide * wide, axis=1, keepdims=True) + EPSILON)
    rows, cols = iota((count, count), 0), iota((count, count), 1)
    owner_row = owner_ref[...].astype(F32)
    owner = jnp.sum(jnp.where(rows == cols, owner_row, 0.0), axis=1, keepdims=True)
    label = jnp.sum(
        jnp.where(rows == cols, completion_ref[...].astype(F32) + 1.0, 0.0), axis=1, keepdims=True
    )
    rank = jnp.sum(jnp.where((owner == owner_row) & (cols < rows), 1.0, 0.0), axis=1, keepdims=True)
    here = lax.axis_index("tensor").astype(F32)
    slot = owner * 16.0 + here * 2.0 + rank
    lane = iota((count, EXT), 1)
    ext = jnp.where(lane == 0, slot, jnp.where(lane == 1, label, 0.0))
    out_ref[:, 0:width] = (wide * inverse * gain_ref[...]).astype(BF16)
    out_ref[:, width:] = ext.astype(BF16)


def join_kernel(mine_ref, other_ref, *part_refs):
    count = mine_ref.shape[0]
    at = 0
    for ref in part_refs:
        n = ref.shape[1]
        ref[0:count, :] = mine_ref[:, at : at + n]
        ref[count:, :] = other_ref[:, at : at + n]
        at += n


def pack_kernel(grad_ref, mine_ref, _, out_ref):
    count = grad_ref.shape[0]
    n = out_ref.shape[1] - EXT
    for t in range(grad_ref.shape[1] // n):
        at = slice(t * count, (t + 1) * count)
        out_ref[at, 0:n] = grad_ref[:, t * n : (t + 1) * n]
        out_ref[at, n:] = mine_ref[:, mine_ref.shape[1] - EXT :]


def relay_kernel(near_ref, out_ref):
    out_ref[...] = near_ref[0 : out_ref.shape[0], :]


def gather_rows(blocks, x_ref):
    at = 0
    span = x_ref.shape[1]
    for b in blocks:
        x_ref[at : at + b.shape[0], :] = b[:, 0:span]
        at += b.shape[0]


def weight_copies(part, weights, w_ref, sems):
    span = w_ref.shape[0]
    step = span // PIECES
    copies = []
    for j in range(PIECES):
        at = 0
        for w in weights:
            n = w.shape[1]
            copies.append(
                pltpu.make_async_copy(
                    w.at[pl.ds(part * span + j * step, step), :],
                    w_ref.at[pl.ds(j * step, step), pl.ds(at, n)],
                    sems.at[len(copies)],
                )
            )
            at += n
    return copies


def project_kernel(part, count, last, *refs):
    blocks = refs[:count]
    weights = refs[count : count + 3]
    rest = refs[count + 3 :]
    x_ref, w_ref, total_ref, sems = rest[-4:]
    span = x_ref.shape[1]
    step = span // PIECES
    copies = weight_copies(part, weights, w_ref, sems)
    for copy in copies:
        copy.start()
    gather_rows(blocks, x_ref)
    for j in range(PIECES):
        for copy in copies[3 * j : 3 * j + 3]:
            copy.wait()
        at = slice(j * step, (j + 1) * step)
        value = dot(x_ref[:, at], w_ref[at, :], ((1,), (0,)))
        if j > 0:
            value += total_ref[...]
        elif last:
            value += rest[0][...]
        total_ref[...] = value
    if not last:
        return
    _, grad_ref, out_ref, ext_ref = rest[:4]
    total = total_ref[...].astype(BF16)
    cols = total.shape[1]
    slots = out_ref.shape[0]
    both, near, nears, far, fars = [e[:, span : span + EXT] for e in blocks]
    ext = jnp.concatenate([both, near, nears, far, fars], axis=0)

    def hot(ext):
        return (ext[:, 0:1].astype(F32) == iota((ext.shape[0], slots), 1).astype(F32)).astype(BF16)

    spread = hot(ext)
    out_ref[:, 0:cols] = dot(spread, total, ((0,), (0,))).astype(BF16)
    out_ref[:, cols : cols + EXT] = dot(spread, ext, ((0,), (0,))).astype(BF16)
    n = grad_ref.shape[1] - EXT
    out_ref[:, cols + EXT :] = dot(hot(grad_ref[:, n:]), grad_ref[:, 0:n], ((0,), (0,))).astype(BF16)
    half = both.shape[0] // 2
    ext_ref[...] = jnp.concatenate([both[:half], nears, far, both[half:], near, fars], axis=0)


def project(part, blocks, weights, before, grads, slots):
    rows = sum(b.shape[0] for b in blocks)
    width = weights[0].shape[0]
    span = width // PARTS
    cols = sum(w.shape[1] for w in weights)
    last = before is not None
    sums = jax.ShapeDtypeStruct((rows, cols), F32)
    out = sums
    if last:
        out = [
            jax.ShapeDtypeStruct((slots, cols + grads.shape[1]), BF16),
            jax.ShapeDtypeStruct((rows, EXT), BF16),
        ]
    scratch = [pltpu.VMEM((rows, span), BF16), pltpu.VMEM((span, cols), BF16)]
    if last:
        scratch.append(pltpu.VMEM((rows, cols), F32))
    scratch.append(pltpu.SemaphoreType.DMA((3 * PIECES,)))

    def body(*refs):
        refs = list(refs)
        if not last:
            sums_ref = refs.pop(len(blocks) + 3)
            refs.insert(len(refs) - 1, sums_ref)
        project_kernel(part, len(blocks), last, *refs)

    return pl.pallas_call(
        body,
        in_specs=[VMEM] * len(blocks) + [ANY] * 3 + ([VMEM] * 2 if last else []),
        out_specs=[VMEM] * 2 if last else VMEM,
        out_shape=out,
        scratch_shapes=scratch,
        compiler_params=params(20),
        cost_estimate=pl.CostEstimate(
            flops=2 * rows * span * cols, bytes_accessed=2 * span * cols, transcendentals=0
        ),
        name="project",
    )(*blocks, *[in_hbm(w) for w in weights], *([before, grads] if last else []))


def attend_kernel(got_ref, rewards_ref, out_ref):
    slots = got_ref.shape[0]
    heads = out_ref.shape[1] // HD - 2
    kcol = heads * HD
    vcol = kcol + HD
    ecol = vcol + HD
    gcol = ecol + EXT
    factor = HD**-0.5
    ext = got_ref[:, ecol : ecol + EXT].astype(F32)
    label = ext[:, 1:2]
    label_row = jnp.transpose(ext)[1:2, :]
    rows, cols = iota((slots, slots), 0), iota((slots, slots), 1)
    same = label == label_row
    bias = jnp.where(same & (rows <= cols), 0.0, -1e30)
    position = jnp.sum(jnp.where(same & (cols < rows), 1.0, 0.0), axis=1, keepdims=True)
    lane = iota((slots, HD), 1)
    half = HD // 2
    index = jnp.where(lane < half, lane, lane - half).astype(F32)
    freq = jnp.exp(index * (-2.0 / HD * jnp.log(F32(BASE))))
    angle = position * freq
    cosine = jnp.cos(angle)
    sine = jnp.sin(angle)
    sine = jnp.where(lane < half, -sine, sine)

    def rope(u):
        return u * cosine + pltpu.roll(u, half, 1) * sine

    def rope_back(u):
        return u * cosine - pltpu.roll(u, half, 1) * sine

    scaled = rewards_ref[...].astype(F32) / 256.0
    advantage = scaled - (jnp.sum(scaled) - scaled) / (KC - 1)
    advantage = jnp.concatenate([advantage, jnp.zeros((1, EXT - KC), F32)], axis=1)
    weight = jnp.sum(jnp.where(label - 1.0 == lane.astype(F32), advantage, 0.0), axis=1, keepdims=True)

    key = rope(got_ref[:, kcol : kcol + HD].astype(F32)).astype(BF16)
    value = got_ref[:, vcol : vcol + HD]
    grad_key = jnp.zeros((slots, HD), F32)
    grad_value = jnp.zeros((slots, HD), F32)
    for h in range(heads):
        at = slice(h * HD, (h + 1) * HD)
        query = rope(got_ref[:, at].astype(F32)).astype(BF16)
        grad = (got_ref[:, gcol + h * HD : gcol + (h + 1) * HD].astype(F32) * weight).astype(BF16)
        scores = dot(key, query, ((1,), (1,))) * factor + bias
        highest = jnp.max(scores, axis=0, keepdims=True)
        weights = jnp.exp(scores - highest)
        probs = weights * (1.0 / jnp.sum(weights, axis=0, keepdims=True))
        grad_value = grad_value + dot(probs.astype(BF16), grad, ((1,), (0,)))
        grad_probs = dot(value, grad, ((1,), (1,)))
        inner = jnp.sum(probs * grad_probs, axis=0, keepdims=True)
        grad_scores = (probs * (grad_probs - inner) * factor).astype(BF16)
        grad_query = dot(grad_scores, key, ((0,), (0,)))
        grad_key = grad_key + dot(grad_scores, query, ((1,), (0,)))
        out_ref[:, at] = rope_back(grad_query).astype(BF16)
    out_ref[:, kcol : kcol + HD] = rope_back(grad_key).astype(BF16)
    out_ref[:, vcol : vcol + HD] = grad_value.astype(BF16)


def back_kernel(part, ext_ref, slots_ref, wq_hbm, wk_hbm, wv_hbm, keep_ref, send_ref, w_ref, sems):
    span = w_ref.shape[0]
    step = span // PIECES
    copies = weight_copies(part, (wq_hbm, wk_hbm, wv_hbm), w_ref, sems)
    for copy in copies:
        copy.start()
    half = keep_ref.shape[0]
    slots = slots_ref.shape[0]
    hot = (ext_ref[:, 0:1].astype(F32) == iota((ext_ref.shape[0], slots), 1).astype(F32)).astype(BF16)
    held = dot(hot, slots_ref[...], ((1,), (0,))).astype(BF16)
    for j in range(PIECES):
        for copy in copies[3 * j : 3 * j + 3]:
            copy.wait()
        at = slice(j * step, (j + 1) * step)
        term = dot(held, w_ref[at, :], ((1,), (1,))).astype(BF16)
        keep_ref[:, at] = term[0:half]
        send_ref[:, at] = term[half:]


def back(part, ext, slot_grads, weights):
    rows = ext.shape[0]
    width = weights[0].shape[0]
    span = width // PARTS
    cols = sum(w.shape[1] for w in weights)
    out = jax.ShapeDtypeStruct((rows // 2, span), BF16)
    return pl.pallas_call(
        lambda *refs: back_kernel(part, *refs),
        in_specs=[VMEM, VMEM] + [ANY] * 3,
        out_specs=[VMEM] * 2,
        out_shape=[out, out],
        scratch_shapes=[pltpu.VMEM((span, cols), BF16), pltpu.SemaphoreType.DMA((3 * PIECES,))],
        compiler_params=params(20),
        cost_estimate=pl.CostEstimate(
            flops=2 * rows * span * cols, bytes_accessed=2 * span * cols, transcendentals=0
        ),
        name="back",
    )(ext, slot_grads, *[in_hbm(w) for w in weights])


def finish_kernel(hidden_ref, gain_ref, *refs):
    out_ref = refs[-1]
    wide = hidden_ref[...].astype(F32)
    inverse = lax.rsqrt(jnp.mean(wide * wide, axis=1, keepdims=True) + EPSILON)
    parts = []
    for i in range(PARTS):
        a, b, c = refs[3 * i : 3 * i + 3]
        parts.append(a[...].astype(F32) + b[...].astype(F32) + c[...].astype(F32))
    scaled = jnp.concatenate(parts, axis=1) * gain_ref[...]
    inner = jnp.mean(scaled * wide, axis=1, keepdims=True)
    out_ref[...] = (inverse * scaled - wide * inverse * inverse * inverse * inner).astype(BF16)


def on_device(hidden, gain, w_query, w_key, w_value, out_grad, owner, completion, rewards):
    groups = lax.axis_size("dp")
    ranks = lax.axis_size("tensor")
    chips = ranks // 2
    count, width = hidden.shape
    query_cols = w_query.shape[1]
    slots = 2 * groups * ranks
    span = width // PARTS

    swap_pairs = [(t, t ^ 1) for t in range(ranks)]
    flow_pairs = [(t, (t // 2 + (1 if t % 2 == 0 else chips - 1)) % chips * 2 + t % 2) for t in range(ranks)]

    def swap(x):
        return lax.ppermute(x, "tensor", swap_pairs)

    def flow(x):
        return lax.ppermute(x, "tensor", flow_pairs)

    mine = pl.pallas_call(
        norm_kernel,
        in_specs=[ANY] * 4,
        out_specs=VMEM,
        out_shape=jax.ShapeDtypeStruct((count, width + EXT), BF16),
        scratch_shapes=[
            pltpu.VMEM((count, width), BF16),
            pltpu.VMEM((1, width), F32),
            pltpu.VMEM((1, count), jnp.int32),
            pltpu.VMEM((1, count), jnp.int32),
            pltpu.SemaphoreType.DMA((4,)),
        ],
        compiler_params=params(),
        name="norm",
    )(*[in_hbm(x) for x in (hidden, gain.reshape(1, width), owner.reshape(1, count), completion.reshape(1, count))])
    other = swap(mine)
    sent = pl.pallas_call(
        join_kernel,
        in_specs=[VMEM] * 2,
        out_specs=[VMEM] * PARTS,
        out_shape=[
            jax.ShapeDtypeStruct((2 * count, span + (EXT if i == PARTS - 1 else 0)), BF16)
            for i in range(PARTS)
        ],
        compiler_params=params(),
        name="join",
    )(mine, other)

    weights = (w_query, w_key, w_value)
    blocks = []
    for i in range(PARTS):
        near = flow(sent[i])
        passed = pl.pallas_call(
            relay_kernel,
            in_specs=[VMEM],
            out_specs=VMEM,
            out_shape=jax.ShapeDtypeStruct((count, near.shape[1]), BF16),
            compiler_params=params(),
            name="relay",
        )(near)
        far = flow(passed)
        blocks.append((sent[i], near, swap(near), far, swap(far)))

    by_head = pl.pallas_call(
        pack_kernel,
        in_specs=[VMEM, VMEM, ANY],
        out_specs=VMEM,
        out_shape=jax.ShapeDtypeStruct((ranks * count, query_cols + EXT), BF16),
        compiler_params=params(),
        name="pack",
    )(out_grad, mine, blocks[PARTS - 1][1])
    head_rows = lax.all_to_all(by_head, "tensor", split_axis=0, concat_axis=0, tiled=True)

    before = None
    for i in range(PARTS):
        before = project(i, blocks[i], weights, before, head_rows, slots)
    total, ext = before
    got = lax.all_to_all(
        total.reshape(groups, 2 * ranks, total.shape[1]), "dp", split_axis=0, concat_axis=0, tiled=True
    ).reshape(total.shape)

    cols = sum(w.shape[1] for w in weights)
    grads = pl.pallas_call(
        attend_kernel,
        in_specs=[VMEM] * 2,
        out_specs=VMEM,
        out_shape=jax.ShapeDtypeStruct((slots, cols), BF16),
        compiler_params=params(),
        name="attend",
    )(got, rewards)
    slot_grads = lax.all_to_all(
        grads.reshape(groups, 2 * ranks, cols), "dp", split_axis=0, concat_axis=0, tiled=True
    ).reshape(grads.shape)

    pieces = []
    for i in range(PARTS):
        keep, send = back(i, ext, slot_grads, weights)
        both = (keep.astype(F32) + swap(send).astype(F32)).astype(BF16)
        passed = flow(both[3 * count :])
        onward = both[count : 3 * count]
        onward = jnp.concatenate(
            [onward[:count], (onward[count:].astype(F32) + passed.astype(F32)).astype(BF16)], axis=0
        )
        came = flow(onward)
        pieces += [both[:count], came[count:], swap(came[:count])]

    return pl.pallas_call(
        finish_kernel,
        in_specs=[VMEM] * (2 + len(pieces)),
        out_specs=VMEM,
        out_shape=jax.ShapeDtypeStruct((count, width), BF16),
        compiler_params=params(),
        name="finish",
    )(hidden, gain.reshape(1, width), *pieces)


def solution(mesh):
    return jax.shard_map(
        on_device,
        mesh=mesh,
        in_specs=(
            P(("dp", "tensor"), None),
            P(),
            P(None, "tensor"),
            P(None, "tensor"),
            P(None, "tensor"),
            P(("dp", "tensor"), None),
            P(("dp", "tensor"), None),
            P(("dp", "tensor")),
            P("dp", None),
        ),
        out_specs=P(("dp", "tensor"), None),
        check_vma=False,
    )
```

time: 140 us -> 112 us (0.80)
  local copies, waits for them, and re-layouts: 13 us -> 1.06 us
  starting transfers between devices: 42.9 us -> 34.7 us
  waiting for transfers between devices: 14.5 us -> 8.16 us
  Pallas kernels: 35.3 us -> 29 us
  blocking collectives: 32.2 us -> 38.4 us
    all_to_all x2 -> x1, starting transfers between devices: 13.6 us -> 3.83 us  [on_device(): lax.all_to_all(by_head, 'tensor', split_axis=0, concat_axis=0, tiled=True)]
    ppermute x8, waiting for transfers between devices: 11.6 us -> 4.32 us  [flow(): return lax.ppermute(x, 'tensor', flow_pairs)]
    all_to_all x1, blocking collectives: 17.8 us -> 25.1 us  [on_device(): lax.all_to_all(total.reshape(groups, 2 * ranks, total.shape[1]), 'dp', sp...]
    pallas_call x6 -> x10, Pallas kernels: 34.2 us -> 27.9 us  [the longest x2 11.6 us: back(): pl.pallas_call(lambda *refs: back_kernel(part, *refs), in_specs=[VMEM, VM...]
    unnamed x29 -> x8, local copies, waits for them, and re-layouts: 6.53 us -> 0.97 us
    ppermute x8, starting transfers between devices: 14.8 us -> 19.3 us  [flow(): return lax.ppermute(x, 'tensor', flow_pairs)]
    reshape x3 -> x0, local copies, waits for them, and re-layouts: 4.17 us -> none  [the longest x1 2.26 us: on_device(): by_group.reshape(2 * groups, ranks, query_cols).transpose(1, 0, 2)]
    ppermute x10 -> x9, starting transfers between devices: 14.5 us -> 11.5 us  [swap(): return lax.ppermute(x, 'tensor', swap_pairs)]
  transfers between devices with their start and end apart: 20 -> 18, of which waited for: 8 -> 6; matrix products, arithmetic and copies ran while one was open for 5% -> 0% of each run, Pallas kernels for 14% -> 10%
where the time goes in v2:
time: 112 us
  blocking collectives  38.4 us (34%)
  starting transfers between devices  34.7 us (31%)
  Pallas kernels  29 us (26%)
  waiting for transfers between devices  8.16 us (7%)
    all_to_all x1, blocking collectives, on_device(): lax.all_to_all(total.reshape(groups, 2 * ranks, total.shape[1]), 'dp', sp...  25.1 us
    ppermute x8, starting transfers between devices, flow(): return lax.ppermute(x, 'tensor', flow_pairs)  19.3 us
    all_to_all x1, blocking collectives, on_device(): lax.all_to_all(grads.reshape(groups, 2 * ranks, cols), 'dp', split_axis=0...  13.3 us
    pallas_call x2, Pallas kernels, back(): pl.pallas_call(lambda *refs: back_kernel(part, *refs), in_specs=[VMEM, VM...  11.6 us
    ppermute x9, starting transfers between devices, swap(): return lax.ppermute(x, 'tensor', swap_pairs)  11.5 us
    pallas_call x2, Pallas kernels, project(): pl.pallas_call(body, in_specs=[VMEM] * len(blocks) + [ANY] * 3 + ([VMEM]...  9.72 us
    pallas_call x1, Pallas kernels, on_device(): pl.pallas_call(attend_kernel, in_specs=[VMEM] * 2, out_specs=VMEM, out_sh...  4.55 us
    ppermute x8, waiting for transfers between devices, flow(): return lax.ppermute(x, 'tensor', flow_pairs)  4.32 us
  transfers between devices with their start and end apart: 18, of which 6 were waited for; matrix products, arithmetic and copies ran while one was open for 0% of the time, Pallas kernels for 10%

profile of v2, /device:TPU:1, one launch (start us, length us, event | category | flops | bytes accessed | tf_op | source)
XLA Modules:
  0.0 111.7 jit_solution(3414134461662321397)
XLA Ops:
  0.0 1.2 %norm.1.mine_ref = bf16[16,8320]{1,0:T(8,128)(2,1)S(1)} custom-call(bf16[16,8192]{1,0:T(8,128)(2,1)} %hidden_ref.1, f32[1,8192]{1,0:T(1,128)} %bitcast.15, s32[1,16]{1,0:T(1,128)} %bitcast.17, s32[1,16]{1,0:T(1,128)} %bitcast.18), custom_call_target="tpu_custom_call" | custom-call | tf_op jit(solution)/shard_map/norm/pallas_call | solution.py:333
  1.2 1.5 %collective-permute-start = (bf16[16,8320]{1,0:T(8,128)(2,1)S(1)}, bf16[16,8320]{1,0:T(8,128)(2,1)S(1)}, u32[]{:S(2)}, u32[]{:S(2)}) collective-permute-start(bf16[16,8320]{1,0:T(8,128)(2,1)S(1)} %norm.1.mine_ref), channel_id=1, source_target_pairs={{0,1},{1,0},{2,3},{3,2},{4,5},{5,4},{6,7},{7,6},{8,9},{9,8},{10,11... | collective-permute-start | bytes 798728 | tf_op jit(solution)/shard_map/ppermute | solution.py:328
  2.7 1.2 %collective-permute-done.other_ref = bf16[16,8320]{1,0:T(8,128)(2,1)S(1)} collective-permute-done((bf16[16,8320]{1,0:T(8,128)(2,1)S(1)}, bf16[16,8320]{1,0:T(8,128)(2,1)S(1)}, u32[]{:S(2)}, u32[]{:S(2)}) %collective-permute-start) | collective-permute-done | bytes 266272 | tf_op jit(solution)/shard_map/ppermute | solution.py:328
  3.9 2.9 %collective-permute-start.5 = (bf16[32,4096]{1,0:T(8,128)(2,1)S(1)}, bf16[32,4096]{1,0:T(8,128)(2,1)S(1)}, u32[]{:S(2)}, u32[]{:S(2)}) collective-permute-start(bf16[32,4096]{1,0:T(8,128)(2,1)S(1)} %get-tuple-element.14.refs_0_), channel_id=1, source_target_pairs={{0,2},{1,7},{2,4},{3,1},{4,6},{5,3},{6,0},{7,5},{8,10},{9,15},{10,... | collective-permute-start | bytes 786440 | tf_op jit(solution)/shard_map/ppermute | solution.py:331
  6.8 0.5 collective-permute-start.1
  7.3 2.9 %collective-permute-done.5.near_ref.refs_1_ = bf16[32,4096]{1,0:T(8,128)(2,1)S(1)} collective-permute-done((bf16[32,4096]{1,0:T(8,128)(2,1)S(1)}, bf16[32,4096]{1,0:T(8,128)(2,1)S(1)}, u32[]{:S(2)}, u32[]{:S(2)}) %collective-permute-start.5) | collective-permute-done | bytes 262176 | tf_op jit(solution)/shard_map/ppermute | solution.py:331
  10.2 3.2 %collective-permute-start.7 = (bf16[16,4096]{1,0:T(8,128)(2,1)S(1)}, bf16[16,4096]{1,0:T(8,128)(2,1)S(1)}, u32[]{:S(2)}, u32[]{:S(2)}) collective-permute-start(bf16[16,4096]{1,0:T(8,128)(2,1)S(1)} %relay.3), channel_id=1, source_target_pairs={{0,2},{1,7},{2,4},{3,1},{4,6},{5,3},{6,0},{7,5},{8,10},{9,15},{10,... | collective-permute-start | bytes 393224 | tf_op jit(solution)/shard_map/ppermute | solution.py:331
  13.3 0.0 collective-permute-start.6
  13.3 0.0 collective-permute-done.1.near_ref._.refs_1_
  13.4 2.9 %collective-permute-start.3 = (bf16[16,4224]{1,0:T(8,128)(2,1)S(1)}, bf16[16,4224]{1,0:T(8,128)(2,1)S(1)}, u32[]{:S(2)}, u32[]{:S(2)}) collective-permute-start(bf16[16,4224]{1,0:T(8,128)(2,1)S(1)} %relay.2), channel_id=1, source_target_pairs={{0,2},{1,7},{2,4},{3,1},{4,6},{5,3},{6,0},{7,5},{8,10},{9,15},{10,... | collective-permute-start | bytes 405512 | tf_op jit(solution)/shard_map/ppermute | solution.py:331
  16.2 0.0 collective-permute-start.2
  16.2 0.9 copy-done.1
  17.2 0.7 pack.1
  17.9 3.8 %all-to-all-start = ((bf16[8,16,1152]{2,1,0:T(8,128)(2,1)}), bf16[8,16,1152]{2,1,0:T(8,128)(2,1)S(1)}, u32[]{:S(2)}, u32[]{:S(2)}) async-start(bf16[8,16,1152]{2,1,0:T(8,128)(2,1)} %bitcast.3), calls=%async_computation | async-start | bytes 589824 | tf_op jit(solution)/shard_map/all_to_all | solution.py:384
  21.8 0.0 collective-permute-done.7.refs_3_
  21.8 0.2 collective-permute-start.8
  22.0 0.3 collective-permute-start.4
  22.3 0.8 collective-permute-done.8.refs_4_
  23.1 4.6 %project.2.refs_8_ = f32[128,1280]{1,0:T(8,128)S(1)} custom-call(bf16[32,4096]{1,0:T(8,128)(2,1)S(1)} %get-tuple-element.14.refs_0_, bf16[32,4096]{1,0:T(8,128)(2,1)S(1)} %collective-permute-done.5.near_ref.refs_1_, bf16[32,4096]{1,0:T(8,128)(2,1)S(1)} %collective-permute-done.6.refs_2_, bf16[16,4096]{1,0:T(8,128)(2,1)S(1)} %collective-permute-done.7.refs_3_, ...), custom_call_target="tpu_custom_call" | custom-call | flops 1342177280 | bytes 10485760 | tf_op jit(solution)/shard_map/project/pallas_call | solution.py:191
  27.7 0.8 all-to-all-done
  28.6 0.0 collective-permute-done.4.refs_4_
  28.6 0.0 collective-permute-done.2.refs_2_
  28.6 5.1 %project.3 = (bf16[256,2432]{1,0:T(8,128)(2,1)S(1)}, bf16[128,128]{1,0:T(8,128)(2,1)S(1)}) custom-call(bf16[32,4224]{1,0:T(8,128)(2,1)S(1)} %get-tuple-element.13.refs_0_, bf16[32,4224]{1,0:T(8,128)(2,1)S(1)} %collective-permute-done.1.near_ref._.refs_1_, bf16[32,4224]{1,0:T(8,128)(2,1)S(1)} %collective-permute-done.2.refs_2_, ...), custom_call_target="tpu_custom_call" | custom-call | flops 1342177280 | bytes 10485760 | tf_op jit(solution)/shard_map/project/pallas_call | solution.py:191
  33.7 0.0 copy-start.3
  33.7 25.1 %all_to_all.21 = bf16[16,16,2432]{2,1,0:T(8,128)(2,1)S(1)} all-to-all(bf16[16,16,2432]{2,1,0:T(8,128)(2,1)S(1)} %bitcast.13), channel_id=1, replica_groups=mesh['dp'=16,'tensor'=8] {'dp'}, dimensions={0} | all-to-all | bytes 2490368 | tf_op jit(solution)/shard_map/all_to_all | solution.py:390
  58.8 4.6 %attend.1 = bf16[256,1280]{1,0:T(8,128)(2,1)S(1)} custom-call(bf16[256,2432]{1,0:T(8,128)(2,1)S(1)} %bitcast.11, s32[1,16]{1,0:T(1,128)S(1)} %copy-done.3), custom_call_target="tpu_custom_call" | custom-call | tf_op jit(solution)/shard_map/attend/pallas_call | solution.py:395
  63.3 13.3 %all_to_all.22 = bf16[16,16,1280]{2,1,0:T(8,128)(2,1)S(1)} all-to-all(bf16[16,16,1280]{2,1,0:T(8,128)(2,1)S(1)} %bitcast.12), channel_id=1, replica_groups=mesh['dp'=16,'tensor'=8] {'dp'}, dimensions={0} | all-to-all | bytes 1310720 | tf_op jit(solution)/shard_map/all_to_all | solution.py:403
  76.6 5.8 %back.2 = (bf16[64,4096]{1,0:T(8,128)(2,1)S(1)}, bf16[64,4096]{1,0:T(8,128)(2,1)S(1)}) custom-call(bf16[128,128]{1,0:T(8,128)(2,1)S(1)} %get-tuple-element.15.refs_0_, bf16[256,1280]{1,0:T(8,128)(2,1)S(1)} %bitcast.9, bf16[8192,1024]{1,0:T(8,128)(2,1)} %refs_2_.3, bf16[8192,128]{1,0:T(8,128)(2,1)} %refs_3_.3, bf16[8192,128]{1,0:T(8,128)(2,1)} %refs_4_.3), custom_call_target="tpu_custom_call" | custom-call | flops 1342177280 | bytes 10485760 | tf_op jit(solution)/shard_map/back/pallas_call | solution.py:288
  82.4 3.6 %collective-permute-start.9 = (bf16[64,4096]{1,0:T(8,128)(2,1)S(1)}, bf16[64,4096]{1,0:T(8,128)(2,1)S(1)}, u32[]{:S(2)}, u32[]{:S(2)}) collective-permute-start(bf16[64,4096]{1,0:T(8,128)(2,1)S(1)} %get-tuple-element.18), channel_id=1, source_target_pairs={{0,1},{1,0},{2,3},{3,2},{4,5},{5,4},{6,7},{7,6},{8,9},{9,8},{10,11... | collective-permute-start | bytes 1572872 | tf_op jit(solution)/shard_map/ppermute | solution.py:328
  86.0 5.8 %back.3 = (bf16[64,4096]{1,0:T(8,128)(2,1)S(1)}, bf16[64,4096]{1,0:T(8,128)(2,1)S(1)}) custom-call(bf16[128,128]{1,0:T(8,128)(2,1)S(1)} %get-tuple-element.15.refs_0_, bf16[256,1280]{1,0:T(8,128)(2,1)S(1)} %bitcast.10, bf16[8192,1024]{1,0:T(8,128)(2,1)} %refs_2_.3, bf16[8192,128]{1,0:T(8,128)(2,1)} %refs_3_.3, bf16[8192,128]{1,0:T(8,128)(2,1)} %refs_4_.3), custom_call_target="tpu_custom_call" | custom-call | flops 1342177280 | bytes 10485760 | tf_op jit(solution)/shard_map/back/pallas_call | solution.py:288
  91.8 0.1 collective-permute-start.13
  91.9 0.1 add_convert_fusion.1
  92.1 3.2 %collective-permute-start.10 = (bf16[16,4096]{1,0:T(8,128)(2,1)S(1)}, bf16[16,4096]{1,0:T(8,128)(2,1)S(1)}, u32[]{:S(2)}, u32[]{:S(2)}) collective-permute-start(bf16[16,4096]{1,0:T(8,128)(2,1)S(1)} %get-tuple-element.25), channel_id=1, source_target_pairs={{0,2},{1,7},{2,4},{3,1},{4,6},{5,3},{6,0},{7,5},{8,10},{9,15},{10,... | collective-permute-start | bytes 393224 | tf_op jit(solution)/shard_map/ppermute | solution.py:331
  95.3 0.0 collective-permute-done.13
  95.3 0.1 add_convert_fusion
  95.4 0.0 copy-start
  95.4 0.0 copy-start.2
  95.5 1.7 %collective-permute-start.14 = (bf16[16,4096]{1,0:T(8,128)(2,1)S(1)}, bf16[16,4096]{1,0:T(8,128)(2,1)S(1)}, u32[]{:S(2)}, u32[]{:S(2)}) collective-permute-start(bf16[16,4096]{1,0:T(8,128)(2,1)S(1)} %get-tuple-element.22), channel_id=1, source_target_pairs={{0,2},{1,7},{2,4},{3,1},{4,6},{5,3},{6,0},{7,5},{8,10},{9,15},{10,... | collective-permute-start | bytes 393224 | tf_op jit(solution)/shard_map/ppermute | solution.py:331
  97.2 0.0 collective-permute-done.10
  97.3 3.1 %collective-permute-start.11 = (bf16[32,4096]{1,0:T(8,128)(2,1)S(1)}, bf16[32,4096]{1,0:T(8,128)(2,1)S(1)}, u32[]{:S(2)}, u32[]{:S(2)}) collective-permute-start(bf16[32,4096]{1,0:T(8,128)(2,1)S(1)} %pad_maximum_fusion), channel_id=1, source_target_pairs={{0,2},{1,7},{2,4},{3,1},{4,6},{5,3},{6,0},{7,5},{8,10},{9,15},{10,... | collective-permute-start | bytes 786440 | tf_op jit(solution)/shard_map/ppermute | solution.py:331
  100.4 0.0 collective-permute-done.14
  100.5 1.8 %collective-permute-start.15 = (bf16[32,4096]{1,0:T(8,128)(2,1)S(1)}, bf16[32,4096]{1,0:T(8,128)(2,1)S(1)}, u32[]{:S(2)}, u32[]{:S(2)}) collective-permute-start(bf16[32,4096]{1,0:T(8,128)(2,1)S(1)} %pad_maximum_fusion.1), channel_id=1, source_target_pairs={{0,2},{1,7},{2,4},{3,1},{4,6},{5,3},{6,0},{7,5},{8,10},{9,15},{10,... | collective-permute-start | bytes 786440 | tf_op jit(solution)/shard_map/ppermute | solution.py:331
  102.3 1.4 %collective-permute-done.11 = bf16[32,4096]{1,0:T(8,128)(2,1)S(1)} collective-permute-done((bf16[32,4096]{1,0:T(8,128)(2,1)S(1)}, bf16[32,4096]{1,0:T(8,128)(2,1)S(1)}, u32[]{:S(2)}, u32[]{:S(2)}) %collective-permute-start.11) | collective-permute-done | bytes 262176 | tf_op jit(solution)/shard_map/ppermute | solution.py:331
  103.8 3.0 %collective-permute-start.12 = (bf16[16,4096]{1,0:T(8,128)(2,1)S(1)}, bf16[16,4096]{1,0:T(8,128)(2,1)S(1)}, u32[]{:S(2)}, u32[]{:S(2)}) collective-permute-start(bf16[16,4096]{1,0:T(8,128)(2,1)S(1)} %get-tuple-element.29), channel_id=1, source_target_pairs={{0,1},{1,0},{2,3},{3,2},{4,5},{5,4},{6,7},{7,6},{8,9},{9,8},{10,11... | collective-permute-start | bytes 393224 | tf_op jit(solution)/shard_map/ppermute | solution.py:328
  106.8 0.0 collective-permute-done.15
  106.8 2.8 %collective-permute-start.16 = (bf16[16,4096]{1,0:T(8,128)(2,1)S(1)}, bf16[16,4096]{1,0:T(8,128)(2,1)S(1)}, u32[]{:S(2)}, u32[]{:S(2)}) collective-permute-start(bf16[16,4096]{1,0:T(8,128)(2,1)S(1)} %get-tuple-element.27), channel_id=1, source_target_pairs={{0,1},{1,0},{2,3},{3,2},{4,5},{5,4},{6,7},{7,6},{8,9},{9,8},{10,11... | collective-permute-start | bytes 393224 | tf_op jit(solution)/shard_map/ppermute | solution.py:328
  109.6 1.0 collective-permute-done.16.refs_5_
  110.6 1.1 %finish.1 = bf16[16,8192]{1,0:T(8,128)(2,1)} custom-call(bf16[16,8192]{1,0:T(8,128)(2,1)S(1)} %copy-done, f32[1,8192]{1,0:T(1,128)S(1)} %bitcast.16, bf16[16,4096]{1,0:T(8,128)(2,1)S(1)} %get-tuple-element.26.refs_0_, bf16[16,4096]{1,0:T(8,128)(2,1)S(1)} %get-tuple-element.30.refs_1_, bf16[16,4096]{1,0:T(8,128)(2,1)S(1)} %collective-permute-done.12.refs_2_, ...), custom_call_target="tpu_custom_call" | custom-call | tf_op jit(solution)/shard_map/finish/pallas_call | solution.py:419
  (19 shorter events, 0.3 us)
Async XLA Ops:
  1.2 2.7 %collective-permute-start = (bf16[16,8320]{1,0:T(8,128)(2,1)S(1)}, bf16[16,8320]{1,0:T(8,128)(2,1)S(1)}, u32[]{:S(2)}, u32[]{:S(2)}) collective-permute-start(bf16[16,8320]{1,0:T(8,128)(2,1)S(1)} %norm.1.mine_ref), channel_id=1, source_target_pairs={{0,1},{1,0},{2,3},{3,2},{4,5},{5,4},{6,7},{7,6},{8,9},{9,8},{10,11... | collective-permute-start | bytes 798728 | tf_op jit(solution)/shard_map/ppermute | solution.py:328
  3.9 6.2 %collective-permute-start.5 = (bf16[32,4096]{1,0:T(8,128)(2,1)S(1)}, bf16[32,4096]{1,0:T(8,128)(2,1)S(1)}, u32[]{:S(2)}, u32[]{:S(2)}) collective-permute-start(bf16[32,4096]{1,0:T(8,128)(2,1)S(1)} %get-tuple-element.14.refs_0_), channel_id=1, source_target_pairs={{0,2},{1,7},{2,4},{3,1},{4,6},{5,3},{6,0},{7,5},{8,10},{9,15},{10,... | collective-permute-start | bytes 786440 | tf_op jit(solution)/shard_map/ppermute | solution.py:331
  6.8 6.5 %collective-permute-start.1 = (bf16[32,4224]{1,0:T(8,128)(2,1)S(1)}, bf16[32,4224]{1,0:T(8,128)(2,1)S(1)}, u32[]{:S(2)}, u32[]{:S(2)}) collective-permute-start(bf16[32,4224]{1,0:T(8,128)(2,1)S(1)} %get-tuple-element.13.refs_0_), channel_id=1, source_target_pairs={{0,2},{1,7},{2,4},{3,1},{4,6},{5,3},{6,0},{7,5},{8,10},{9,15},{10,... | collective-permute-start | bytes 811016 | tf_op jit(solution)/shard_map/ppermute | solution.py:331
  10.2 11.6 %collective-permute-start.7 = (bf16[16,4096]{1,0:T(8,128)(2,1)S(1)}, bf16[16,4096]{1,0:T(8,128)(2,1)S(1)}, u32[]{:S(2)}, u32[]{:S(2)}) collective-permute-start(bf16[16,4096]{1,0:T(8,128)(2,1)S(1)} %relay.3), channel_id=1, source_target_pairs={{0,2},{1,7},{2,4},{3,1},{4,6},{5,3},{6,0},{7,5},{8,10},{9,15},{10,... | collective-permute-start | bytes 393224 | tf_op jit(solution)/shard_map/ppermute | solution.py:331
  13.3 9.8 %collective-permute-start.6 = (bf16[32,4096]{1,0:T(8,128)(2,1)S(1)}, bf16[32,4096]{1,0:T(8,128)(2,1)S(1)}, u32[]{:S(2)}, u32[]{:S(2)}) collective-permute-start(bf16[32,4096]{1,0:T(8,128)(2,1)S(1)} %collective-permute-done.5.near_ref.refs_1_), channel_id=1, source_target_pairs={{0,1},{1,0},{2,3},{3,2},{4,5},{5,4},{6,7},{7,6},{8,9},{9,8},{10,11... | collective-permute-start | bytes 786440 | tf_op jit(solution)/shard_map/ppermute | solution.py:328
  13.4 8.6 %collective-permute-start.3 = (bf16[16,4224]{1,0:T(8,128)(2,1)S(1)}, bf16[16,4224]{1,0:T(8,128)(2,1)S(1)}, u32[]{:S(2)}, u32[]{:S(2)}) collective-permute-start(bf16[16,4224]{1,0:T(8,128)(2,1)S(1)} %relay.2), channel_id=1, source_target_pairs={{0,2},{1,7},{2,4},{3,1},{4,6},{5,3},{6,0},{7,5},{8,10},{9,15},{10,... | collective-permute-start | bytes 405512 | tf_op jit(solution)/shard_map/ppermute | solution.py:331
  16.2 12.3 %collective-permute-start.2 = (bf16[32,4224]{1,0:T(8,128)(2,1)S(1)}, bf16[32,4224]{1,0:T(8,128)(2,1)S(1)}, u32[]{:S(2)}, u32[]{:S(2)}) collective-permute-start(bf16[32,4224]{1,0:T(8,128)(2,1)S(1)} %collective-permute-done.1.near_ref._.refs_1_), channel_id=1, source_target_pairs={{0,1},{1,0},{2,3},{3,2},{4,5},{5,4},{6,7},{7,6},{8,9},{9,8},{10,11... | collective-permute-start | bytes 811016 | tf_op jit(solution)/shard_map/ppermute | solution.py:328
  16.2 1.0 copy-start.1
  17.9 10.7 %all-to-all-start = ((bf16[8,16,1152]{2,1,0:T(8,128)(2,1)}), bf16[8,16,1152]{2,1,0:T(8,128)(2,1)S(1)}, u32[]{:S(2)}, u32[]{:S(2)}) async-start(bf16[8,16,1152]{2,1,0:T(8,128)(2,1)} %bitcast.3), calls=%async_computation | async-start | bytes 589824 | tf_op jit(solution)/shard_map/all_to_all | solution.py:384
  21.8 1.3 %collective-permute-start.8 = (bf16[16,4096]{1,0:T(8,128)(2,1)S(1)}, bf16[16,4096]{1,0:T(8,128)(2,1)S(1)}, u32[]{:S(2)}, u32[]{:S(2)}) collective-permute-start(bf16[16,4096]{1,0:T(8,128)(2,1)S(1)} %collective-permute-done.7.refs_3_), channel_id=1, source_target_pairs={{0,1},{1,0},{2,3},{3,2},{4,5},{5,4},{6,7},{7,6},{8,9},{9,8},{10,11... | collective-permute-start | bytes 393224 | tf_op jit(solution)/shard_map/ppermute | solution.py:328
  22.0 6.6 %collective-permute-start.4 = (bf16[16,4224]{1,0:T(8,128)(2,1)S(1)}, bf16[16,4224]{1,0:T(8,128)(2,1)S(1)}, u32[]{:S(2)}, u32[]{:S(2)}) collective-permute-start(bf16[16,4224]{1,0:T(8,128)(2,1)S(1)} %collective-permute-done.3.refs_3_), channel_id=1, source_target_pairs={{0,1},{1,0},{2,3},{3,2},{4,5},{5,4},{6,7},{7,6},{8,9},{9,8},{10,11... | collective-permute-start | bytes 405512 | tf_op jit(solution)/shard_map/ppermute | solution.py:328
  33.7 25.1 %copy-start.3 = (s32[1,16]{1,0:T(1,128)S(1)}, s32[1,16]{1,0:T(1,128)}, u32[]{:S(2)}) copy-start(s32[1,16]{1,0:T(1,128)} %rewards_ref.1) | copy-start | bytes 196
  82.4 9.5 %collective-permute-start.9 = (bf16[64,4096]{1,0:T(8,128)(2,1)S(1)}, bf16[64,4096]{1,0:T(8,128)(2,1)S(1)}, u32[]{:S(2)}, u32[]{:S(2)}) collective-permute-start(bf16[64,4096]{1,0:T(8,128)(2,1)S(1)} %get-tuple-element.18), channel_id=1, source_target_pairs={{0,1},{1,0},{2,3},{3,2},{4,5},{5,4},{6,7},{7,6},{8,9},{9,8},{10,11... | collective-permute-start | bytes 1572872 | tf_op jit(solution)/shard_map/ppermute | solution.py:328
  91.8 3.5 %collective-permute-start.13 = (bf16[64,4096]{1,0:T(8,128)(2,1)S(1)}, bf16[64,4096]{1,0:T(8,128)(2,1)S(1)}, u32[]{:S(2)}, u32[]{:S(2)}) collective-permute-start(bf16[64,4096]{1,0:T(8,128)(2,1)S(1)} %get-tuple-element.20), channel_id=1, source_target_pairs={{0,1},{1,0},{2,3},{3,2},{4,5},{5,4},{6,7},{7,6},{8,9},{9,8},{10,11... | collective-permute-start | bytes 1572872 | tf_op jit(solution)/shard_map/ppermute | solution.py:328
  92.1 5.2 %collective-permute-start.10 = (bf16[16,4096]{1,0:T(8,128)(2,1)S(1)}, bf16[16,4096]{1,0:T(8,128)(2,1)S(1)}, u32[]{:S(2)}, u32[]{:S(2)}) collective-permute-start(bf16[16,4096]{1,0:T(8,128)(2,1)S(1)} %get-tuple-element.25), channel_id=1, source_target_pairs={{0,2},{1,7},{2,4},{3,1},{4,6},{5,3},{6,0},{7,5},{8,10},{9,15},{10,... | collective-permute-start | bytes 393224 | tf_op jit(solution)/shard_map/ppermute | solution.py:331
  95.4 15.2 %copy-start = (bf16[16,8192]{1,0:T(8,128)(2,1)S(1)}, bf16[16,8192]{1,0:T(8,128)(2,1)}, u32[]{:S(2)}) copy-start(bf16[16,8192]{1,0:T(8,128)(2,1)} %hidden_ref.1) | copy-start | bytes 786436
  95.4 15.2 %copy-start.2 = (f32[8192]{0:T(1024)S(1)}, f32[8192]{0:T(1024)}, u32[]{:S(2)}) copy-start(f32[8192]{0:T(1024)} %param.10) | copy-start | bytes 98308
  95.5 5.0 %collective-permute-start.14 = (bf16[16,4096]{1,0:T(8,128)(2,1)S(1)}, bf16[16,4096]{1,0:T(8,128)(2,1)S(1)}, u32[]{:S(2)}, u32[]{:S(2)}) collective-permute-start(bf16[16,4096]{1,0:T(8,128)(2,1)S(1)} %get-tuple-element.22), channel_id=1, source_target_pairs={{0,2},{1,7},{2,4},{3,1},{4,6},{5,3},{6,0},{7,5},{8,10},{9,15},{10,... | collective-permute-start | bytes 393224 | tf_op jit(solution)/shard_map/ppermute | solution.py:331
  97.3 6.5 %collective-permute-start.11 = (bf16[32,4096]{1,0:T(8,128)(2,1)S(1)}, bf16[32,4096]{1,0:T(8,128)(2,1)S(1)}, u32[]{:S(2)}, u32[]{:S(2)}) collective-permute-start(bf16[32,4096]{1,0:T(8,128)(2,1)S(1)} %pad_maximum_fusion), channel_id=1, source_target_pairs={{0,2},{1,7},{2,4},{3,1},{4,6},{5,3},{6,0},{7,5},{8,10},{9,15},{10,... | collective-permute-start | bytes 786440 | tf_op jit(solution)/shard_map/ppermute | solution.py:331
  100.5 6.3 %collective-permute-start.15 = (bf16[32,4096]{1,0:T(8,128)(2,1)S(1)}, bf16[32,4096]{1,0:T(8,128)(2,1)S(1)}, u32[]{:S(2)}, u32[]{:S(2)}) collective-permute-start(bf16[32,4096]{1,0:T(8,128)(2,1)S(1)} %pad_maximum_fusion.1), channel_id=1, source_target_pairs={{0,2},{1,7},{2,4},{3,1},{4,6},{5,3},{6,0},{7,5},{8,10},{9,15},{10,... | collective-permute-start | bytes 786440 | tf_op jit(solution)/shard_map/ppermute | solution.py:331
  103.8 5.8 %collective-permute-start.12 = (bf16[16,4096]{1,0:T(8,128)(2,1)S(1)}, bf16[16,4096]{1,0:T(8,128)(2,1)S(1)}, u32[]{:S(2)}, u32[]{:S(2)}) collective-permute-start(bf16[16,4096]{1,0:T(8,128)(2,1)S(1)} %get-tuple-element.29), channel_id=1, source_target_pairs={{0,1},{1,0},{2,3},{3,2},{4,5},{5,4},{6,7},{7,6},{8,9},{9,8},{10,11... | collective-permute-start | bytes 393224 | tf_op jit(solution)/shard_map/ppermute | solution.py:328
  106.8 3.8 %collective-permute-start.16 = (bf16[16,4096]{1,0:T(8,128)(2,1)S(1)}, bf16[16,4096]{1,0:T(8,128)(2,1)S(1)}, u32[]{:S(2)}, u32[]{:S(2)}) collective-permute-start(bf16[16,4096]{1,0:T(8,128)(2,1)S(1)} %get-tuple-element.27), channel_id=1, source_target_pairs={{0,1},{1,0},{2,3},{3,2},{4,5},{5,4},{6,7},{7,6},{8,9},{9,8},{10,11... | collective-permute-start | bytes 393224 | tf_op jit(solution)/shard_map/ppermute | solution.py:328

commit v3 on v2

--- a/solution.py
+++ b/solution.py
@@ -9,6 +9,7 @@
 KC = 16
 PARTS = 2
 EXT = 128
+HEADS_AT = 8192 + EXT
 STEP = 1024
 PIECES = 4
 EPSILON = 1e-05
@@ -16,6 +17,7 @@
 F32 = jnp.float32
 BF16 = jnp.bfloat16
 
+TOKEN = jax.ShapeDtypeStruct((8, 128), F32)
 VMEM = pl.BlockSpec(memory_space=pltpu.VMEM)
 ANY = pl.BlockSpec(memory_space=pl.ANY)
 
@@ -28,6 +30,10 @@
     return pltpu.with_memory_space_constraint(x, pltpu.HBM)
 
 
+def in_vmem(x):
+    return pltpu.with_memory_space_constraint(x, pltpu.VMEM)
+
+
 def dot(a, b, dims):
     return lax.dot_general(a, b, (dims, ((), ())), preferred_element_type=F32)
 
@@ -36,8 +42,13 @@
     return lax.broadcasted_iota(jnp.int32, shape, axis)
 
 
-def norm_kernel(hidden_hbm, gain_hbm, owner_hbm, completion_hbm, out_ref, *rest):
-    hidden_ref, gain_ref, owner_ref, completion_ref, sems = rest
+def chip_and_core():
+    here = lax.axis_index("tensor")
+    return here // 2, here % 2, lax.axis_size("tensor") // 2
+
+
+def norm_kernel(hidden_hbm, gain_hbm, owner_hbm, completion_hbm, grad_hbm, leave_ref, cross_ref, own_ref, *rest):
+    hidden_ref, gain_ref, owner_ref, completion_ref, grad_ref, sems = rest
     copies = [
         pltpu.make_async_copy(src, dst, sems.at[i])
         for i, (src, dst) in enumerate(
@@ -46,6 +57,7 @@
                 (gain_hbm, gain_ref),
                 (owner_hbm, owner_ref),
                 (completion_hbm, completion_ref),
+                (grad_hbm, grad_ref),
             )
         )
     ]
@@ -66,140 +78,145 @@
     here = lax.axis_index("tensor").astype(F32)
     slot = owner * 16.0 + here * 2.0 + rank
     lane = iota((count, EXT), 1)
-    ext = jnp.where(lane == 0, slot, jnp.where(lane == 1, label, 0.0))
-    out_ref[:, 0:width] = (wide * inverse * gain_ref[...]).astype(BF16)
-    out_ref[:, width:] = ext.astype(BF16)
-
-
-def join_kernel(mine_ref, other_ref, *part_refs):
-    count = mine_ref.shape[0]
-    at = 0
-    for ref in part_refs:
-        n = ref.shape[1]
-        ref[0:count, :] = mine_ref[:, at : at + n]
-        ref[count:, :] = other_ref[:, at : at + n]
-        at += n
-
-
-def pack_kernel(grad_ref, mine_ref, _, out_ref):
-    count = grad_ref.shape[0]
-    n = out_ref.shape[1] - EXT
-    for t in range(grad_ref.shape[1] // n):
-        at = slice(t * count, (t + 1) * count)
-        out_ref[at, 0:n] = grad_ref[:, t * n : (t + 1) * n]
-        out_ref[at, n:] = mine_ref[:, mine_ref.shape[1] - EXT :]
-
-
-def relay_kernel(near_ref, out_ref):
-    out_ref[...] = near_ref[0 : out_ref.shape[0], :]
-
-
-def gather_rows(blocks, x_ref):
-    at = 0
-    span = x_ref.shape[1]
-    for b in blocks:
-        x_ref[at : at + b.shape[0], :] = b[:, 0:span]
-        at += b.shape[0]
-
-
-def weight_copies(part, weights, w_ref, sems):
-    span = w_ref.shape[0]
+    ext = jnp.where(lane == 0, slot, jnp.where(lane == 1, label, 0.0)).astype(BF16)
+    normed = (wide * inverse * gain_ref[...]).astype(BF16)
+    for ref in (leave_ref, cross_ref):
+        ref[:, 0:width] = normed
+        ref[:, width : width + EXT] = ext
+    chip, core, chips = chip_and_core()
+    each = own_ref.shape[1]
+
+    def heads(at, n):
+        return grad_ref[:, pl.ds(pl.multiple_of(at * each, each), n * each)]
+
+    up, down = (chip + 1) % chips, (chip + chips - 1) % chips
+    at = width + EXT
+    leave_ref[:, at : at + 2 * each] = heads(2 * jnp.where(core == 0, up, down), 2)
+    leave_ref[:, at + 2 * each :] = heads(2 * ((chip + 2) % chips), 2)
+    cross_ref[:, at : at + 2 * each] = heads(2 * jnp.where(core == 0, down, up), 2)
+    cross_ref[:, at + 2 * each :] = heads(2 * chip + 1 - core, 1)
+    own_ref[...] = heads(2 * chip + core, 1)
+
+
+def join_kernel(mine_ref, other_ref, mine_out, other_out):
+    mine_out[...] = mine_ref[...]
+    other_out[...] = other_ref[:, 0 : other_out.shape[1]]
+
+
+def half(rows_ref, out_ref):
+    n = HEADS_AT
+    each = out_ref.shape[1] - n
+    _, core, _ = chip_and_core()
+    out_ref[:, 0:n] = rows_ref[:, 0:n]
+    first, second = rows_ref[:, n : n + each], rows_ref[:, n + each : n + 2 * each]
+    out_ref[:, n:] = jnp.where(core == 0, second, first)
+
+
+def half_kernel(rows_ref, _, out_ref):
+    half(rows_ref, out_ref)
+
+
+def relay_kernel(near_ref, _, pass_ref, half_ref):
+    n = HEADS_AT
+    each = half_ref.shape[1] - n
+    pass_ref[:, 0:n] = near_ref[:, 0:n]
+    pass_ref[:, n:] = near_ref[:, n + 2 * each :]
+    half(near_ref, half_ref)
+
+
+def load_kernel(part, wq_hbm, wk_hbm, wv_hbm, _, out_ref, token_ref, sems):
+    token_ref[...] = jnp.zeros_like(token_ref)
+    span = out_ref.shape[0]
     step = span // PIECES
     copies = []
-    for j in range(PIECES):
-        at = 0
-        for w in weights:
-            n = w.shape[1]
+    at = 0
+    for w in (wq_hbm, wk_hbm, wv_hbm):
+        n = w.shape[1]
+        for j in range(PIECES):
             copies.append(
                 pltpu.make_async_copy(
                     w.at[pl.ds(part * span + j * step, step), :],
-                    w_ref.at[pl.ds(j * step, step), pl.ds(at, n)],
+                    out_ref.at[pl.ds(j * step, step), pl.ds(at, n)],
                     sems.at[len(copies)],
                 )
             )
-            at += n
-    return copies
-
-
-def project_kernel(part, count, last, *refs):
-    blocks = refs[:count]
-    weights = refs[count : count + 3]
-    rest = refs[count + 3 :]
-    x_ref, w_ref, total_ref, sems = rest[-4:]
-    span = x_ref.shape[1]
-    step = span // PIECES
-    copies = weight_copies(part, weights, w_ref, sems)
+        at += n
     for copy in copies:
         copy.start()
-    gather_rows(blocks, x_ref)
-    for j in range(PIECES):
-        for copy in copies[3 * j : 3 * j + 3]:
-            copy.wait()
-        at = slice(j * step, (j + 1) * step)
-        value = dot(x_ref[:, at], w_ref[at, :], ((1,), (0,)))
-        if j > 0:
-            value += total_ref[...]
-        elif last:
-            value += rest[0][...]
-        total_ref[...] = value
-    if not last:
-        return
-    _, grad_ref, out_ref, ext_ref = rest[:4]
-    total = total_ref[...].astype(BF16)
+    for copy in copies:
+        copy.wait()
+
+
+def load(part, weights, after):
+    span = weights[0].shape[0] // PARTS
+    cols = sum(w.shape[1] for w in weights)
+    return pl.pallas_call(
+        lambda *refs: load_kernel(part, *refs),
+        in_specs=[ANY] * 3 + [VMEM],
+        out_specs=[VMEM] * 2,
+        out_shape=[pltpu.VMEM((span, cols), BF16), TOKEN],
+        scratch_shapes=[pltpu.SemaphoreType.DMA((3 * PIECES,))],
+        compiler_params=params(),
+        cost_estimate=pl.CostEstimate(flops=0, bytes_accessed=2 * span * cols, transcendentals=0),
+        name="load",
+    )(*[in_hbm(w) for w in weights], after)
+
+
+def project_kernel(count, *refs):
+    blocks = refs[:count]
+    parts = refs[count : count + PARTS]
+    own_ref, out_ref, ext_ref, x_ref = refs[count + PARTS :]
+    width = x_ref.shape[1]
+    rows = blocks[0].shape[0]
+    for i, b in enumerate(blocks):
+        x_ref[i * rows : (i + 1) * rows, :] = b[:, 0:width]
+    exts = [b[:, width : width + EXT] for b in blocks]
+    mine, other, near, near_o, across, across_o, far, far_o = exts
+    ext_ref[...] = jnp.concatenate([mine, across, across_o, far, other, near, near_o, far_o], axis=0)
+    total = None
+    for i, w in enumerate(parts):
+        span = w.shape[0]
+        value = dot(x_ref[:, i * span : (i + 1) * span], w[...], ((1,), (0,)))
+        total = value if total is None else total + value
+    total = total.astype(BF16)
     cols = total.shape[1]
     slots = out_ref.shape[0]
-    both, near, nears, far, fars = [e[:, span : span + EXT] for e in blocks]
-    ext = jnp.concatenate([both, near, nears, far, fars], axis=0)
-
-    def hot(ext):
-        return (ext[:, 0:1].astype(F32) == iota((ext.shape[0], slots), 1).astype(F32)).astype(BF16)
-
-    spread = hot(ext)
+    ext = jnp.concatenate(exts, axis=0)
+    spread = (ext[:, 0:1].astype(F32) == iota((ext.shape[0], slots), 1).astype(F32)).astype(BF16)
     out_ref[:, 0:cols] = dot(spread, total, ((0,), (0,))).astype(BF16)
     out_ref[:, cols : cols + EXT] = dot(spread, ext, ((0,), (0,))).astype(BF16)
-    n = grad_ref.shape[1] - EXT
-    out_ref[:, cols + EXT :] = dot(hot(grad_ref[:, n:]), grad_ref[:, 0:n], ((0,), (0,))).astype(BF16)
-    half = both.shape[0] // 2
-    ext_ref[...] = jnp.concatenate([both[:half], nears, far, both[half:], near, fars], axis=0)
-
-
-def project(part, blocks, weights, before, grads, slots):
+    _, core, _ = chip_and_core()
+    n = HEADS_AT
+    each = own_ref.shape[1]
+
+    def heads(b):
+        return jnp.where(core == 0, b[:, n : n + each], b[:, n + each : n + 2 * each])
+
+    mine, other, near, near_o, across, across_o, far, far_o = blocks
+    grads = [own_ref[...], other[:, n + 2 * each :], heads(near), heads(near_o)]
+    grads += [across[:, n:], across_o[:, n:], heads(far), far_o[:, n:]]
+    out_ref[:, cols + EXT :] = dot(spread, jnp.concatenate(grads, axis=0), ((0,), (0,))).astype(BF16)
+
+
+def project(blocks, loaded, own, slots):
     rows = sum(b.shape[0] for b in blocks)
-    width = weights[0].shape[0]
-    span = width // PARTS
-    cols = sum(w.shape[1] for w in weights)
-    last = before is not None
-    sums = jax.ShapeDtypeStruct((rows, cols), F32)
-    out = sums
-    if last:
-        out = [
-            jax.ShapeDtypeStruct((slots, cols + grads.shape[1]), BF16),
+    span, cols = loaded[0].shape
+    width = span * PARTS
+    return pl.pallas_call(
+        lambda *refs: project_kernel(len(blocks), *refs),
+        in_specs=[VMEM] * (len(blocks) + PARTS + 1),
+        out_specs=[VMEM] * 2,
+        out_shape=[
+            jax.ShapeDtypeStruct((slots, cols + EXT + own.shape[1]), BF16),
             jax.ShapeDtypeStruct((rows, EXT), BF16),
-        ]
-    scratch = [pltpu.VMEM((rows, span), BF16), pltpu.VMEM((span, cols), BF16)]
-    if last:
-        scratch.append(pltpu.VMEM((rows, cols), F32))
-    scratch.append(pltpu.SemaphoreType.DMA((3 * PIECES,)))
-
-    def body(*refs):
-        refs = list(refs)
-        if not last:
-            sums_ref = refs.pop(len(blocks) + 3)
-            refs.insert(len(refs) - 1, sums_ref)
-        project_kernel(part, len(blocks), last, *refs)
-
-    return pl.pallas_call(
-        body,
-        in_specs=[VMEM] * len(blocks) + [ANY] * 3 + ([VMEM] * 2 if last else []),
-        out_specs=[VMEM] * 2 if last else VMEM,
-        out_shape=out,
-        scratch_shapes=scratch,
-        compiler_params=params(20),
+        ],
+        scratch_shapes=[pltpu.VMEM((rows, width), BF16)],
+        compiler_params=params(),
         cost_estimate=pl.CostEstimate(
-            flops=2 * rows * span * cols, bytes_accessed=2 * span * cols, transcendentals=0
+            flops=2 * rows * width * cols, bytes_accessed=2 * width * cols, transcendentals=0
         ),
         name="project",
-    )(*blocks, *[in_hbm(w) for w in weights], *([before, grads] if last else []))
+    )(*blocks, *[in_vmem(w) for w in loaded], own)
 
 
 def attend_kernel(got_ref, rewards_ref, out_ref):
@@ -260,6 +277,25 @@
     out_ref[:, vcol : vcol + HD] = grad_value.astype(BF16)
 
 
+def weight_copies(part, weights, w_ref, sems):
+    span = w_ref.shape[0]
+    step = span // PIECES
+    copies = []
+    for j in range(PIECES):
+        at = 0
+        for w in weights:
+            n = w.shape[1]
+            copies.append(
+                pltpu.make_async_copy(
+                    w.at[pl.ds(part * span + j * step, step), :],
+                    w_ref.at[pl.ds(j * step, step), pl.ds(at, n)],
+                    sems.at[len(copies)],
+                )
+            )
+            at += n
+    return copies
+
+
 def back_kernel(part, ext_ref, slots_ref, wq_hbm, wk_hbm, wv_hbm, keep_ref, send_ref, w_ref, sems):
     span = w_ref.shape[0]
     step = span // PIECES
@@ -330,63 +366,74 @@
     def flow(x):
         return lax.ppermute(x, "tensor", flow_pairs)
 
-    mine = pl.pallas_call(
+    near_cols = HEADS_AT + 2 * query_cols
+
+    def rows_of(cols):
+        return jax.ShapeDtypeStruct((count, cols), BF16)
+
+    leave, cross, own = pl.pallas_call(
         norm_kernel,
-        in_specs=[ANY] * 4,
-        out_specs=VMEM,
-        out_shape=jax.ShapeDtypeStruct((count, width + EXT), BF16),
+        in_specs=[ANY] * 5,
+        out_specs=[VMEM] * 3,
+        out_shape=[rows_of(near_cols + 2 * query_cols), rows_of(near_cols + query_cols), rows_of(query_cols)],
         scratch_shapes=[
             pltpu.VMEM((count, width), BF16),
             pltpu.VMEM((1, width), F32),
             pltpu.VMEM((1, count), jnp.int32),
             pltpu.VMEM((1, count), jnp.int32),
-            pltpu.SemaphoreType.DMA((4,)),
+            pltpu.VMEM((count, width), BF16),
+            pltpu.SemaphoreType.DMA((5,)),
         ],
         compiler_params=params(),
         name="norm",
-    )(*[in_hbm(x) for x in (hidden, gain.reshape(1, width), owner.reshape(1, count), completion.reshape(1, count))])
-    other = swap(mine)
-    sent = pl.pallas_call(
+    )(
+        *[
+            in_hbm(x)
+            for x in (hidden, gain.reshape(1, width), owner.reshape(1, count), completion.reshape(1, count), out_grad)
+        ]
+    )
+    other = swap(cross)
+    mine, leave_o = pl.pallas_call(
         join_kernel,
         in_specs=[VMEM] * 2,
-        out_specs=[VMEM] * PARTS,
-        out_shape=[
-            jax.ShapeDtypeStruct((2 * count, span + (EXT if i == PARTS - 1 else 0)), BF16)
-            for i in range(PARTS)
-        ],
+        out_specs=[VMEM] * 2,
+        out_shape=[rows_of(near_cols + 2 * query_cols), rows_of(near_cols)],
         compiler_params=params(),
         name="join",
-    )(mine, other)
+    )(leave, other)
 
     weights = (w_query, w_key, w_value)
-    blocks = []
-    for i in range(PARTS):
-        near = flow(sent[i])
-        passed = pl.pallas_call(
-            relay_kernel,
-            in_specs=[VMEM],
+    near = flow(mine)
+    near_o = flow(leave_o)
+    first, ready = load(0, weights, leave_o)
+    half_rows = rows_of(HEADS_AT + query_cols)
+    passed, half_near = pl.pallas_call(
+        relay_kernel,
+        in_specs=[VMEM] * 2,
+        out_specs=[VMEM] * 2,
+        out_shape=[rows_of(near_cols), half_rows],
+        compiler_params=params(),
+        name="relay",
+    )(near, ready)
+    far = flow(passed)
+    second, ready_too = load(1, weights, passed)
+
+    def half_of(rows, after):
+        return pl.pallas_call(
+            half_kernel,
+            in_specs=[VMEM] * 2,
             out_specs=VMEM,
-            out_shape=jax.ShapeDtypeStruct((count, near.shape[1]), BF16),
+            out_shape=half_rows,
             compiler_params=params(),
-            name="relay",
-        )(near)
-        far = flow(passed)
-        blocks.append((sent[i], near, swap(near), far, swap(far)))
-
-    by_head = pl.pallas_call(
-        pack_kernel,
-        in_specs=[VMEM, VMEM, ANY],
-        out_specs=VMEM,
-        out_shape=jax.ShapeDtypeStruct((ranks * count, query_cols + EXT), BF16),
-        compiler_params=params(),
-        name="pack",
-    )(out_grad, mine, blocks[PARTS - 1][1])
-    head_rows = lax.all_to_all(by_head, "tensor", split_axis=0, concat_axis=0, tiled=True)
-
-    before = None
-    for i in range(PARTS):
-        before = project(i, blocks[i], weights, before, head_rows, slots)
-    total, ext = before
+            name="half",
+        )(rows, after)
+
+    across = swap(half_near)
+    across_o = swap(half_of(near_o, ready))
+    far_o = swap(half_of(far, ready_too))
+    blocks = (mine, other, near, near_o, across, across_o, far, far_o)
+    loaded = (first, second)
+    total, ext = project(blocks, loaded, own, slots)
     got = lax.all_to_all(
         total.reshape(groups, 2 * ranks, total.shape[1]), "dp", split_axis=0, concat_axis=0, tiled=True
     ).reshape(total.shape)

time: 112 us -> 107 us (0.955)
  starting transfers between devices: 34.7 us -> 28.4 us
  blocking collectives: 38.4 us -> 40.8 us
  waiting for transfers between devices: 8.16 us -> 6.06 us
  Pallas kernels: 29 us -> 30.8 us
    ppermute x8 -> x7, starting transfers between devices: 19.3 us -> 14.4 us  [flow(): return lax.ppermute(x, 'tensor', flow_pairs)]
    all_to_all x1 -> x0, starting transfers between devices: 3.83 us -> none  [on_device(): lax.all_to_all(by_head, 'tensor', split_axis=0, concat_axis=0, tiled=True)]
    ppermute x9 -> x8, starting transfers between devices: 11.5 us -> 14.1 us  [swap(): return lax.ppermute(x, 'tensor', swap_pairs)]
    ppermute x8 -> x7, waiting for transfers between devices: 4.32 us -> 2.39 us  [flow(): return lax.ppermute(x, 'tensor', flow_pairs)]
    pallas_call x7 -> x8, Pallas kernels: 11.7 us -> 13.5 us  [the longest x2 8.08 us: load(): pl.pallas_call(lambda *refs: load_kernel(part, *refs), in_specs=[ANY] * 3...]
    all_to_all x1, blocking collectives: 13.3 us -> 14.6 us  [on_device(): lax.all_to_all(grads.reshape(groups, 2 * ranks, cols), 'dp', split_axis=0...]
    all_to_all x1, blocking collectives: 25.1 us -> 26.3 us  [on_device(): lax.all_to_all(total.reshape(groups, 2 * ranks, total.shape[1]), 'dp', sp...]
    ppermute x9 -> x8, waiting for transfers between devices: 3 us -> 3.67 us  [swap(): return lax.ppermute(x, 'tensor', swap_pairs)]
  transfers between devices with their start and end apart: 18 -> 15, of which waited for: 6 -> 9; matrix products, arithmetic and copies ran while one was open for 0% -> 0% of each run, Pallas kernels for 10% -> 13%
where the time goes in v3:
time: 107 us
  blocking collectives  40.8 us (38%)
  Pallas kernels  30.8 us (29%)
  starting transfers between devices  28.4 us (27%)
  waiting for transfers between devices  6.06 us (6%)
    all_to_all x1, blocking collectives, on_device(): lax.all_to_all(total.reshape(groups, 2 * ranks, total.shape[1]), 'dp', sp...  26.3 us
    all_to_all x1, blocking collectives, on_device(): lax.all_to_all(grads.reshape(groups, 2 * ranks, cols), 'dp', split_axis=0...  14.6 us
    ppermute x7, starting transfers between devices, flow(): return lax.ppermute(x, 'tensor', flow_pairs)  14.4 us
    ppermute x8, starting transfers between devices, swap(): return lax.ppermute(x, 'tensor', swap_pairs)  14.1 us
    pallas_call x2, Pallas kernels, back(): pl.pallas_call(lambda *refs: back_kernel(part, *refs), in_specs=[VMEM, VM...  11.6 us
    pallas_call x2, Pallas kernels, load(): pl.pallas_call(lambda *refs: load_kernel(part, *refs), in_specs=[ANY] * 3...  8.08 us
    pallas_call x1, Pallas kernels, on_device(): pl.pallas_call(attend_kernel, in_specs=[VMEM] * 2, out_specs=VMEM, out_sh...  4.55 us
    pallas_call x1, Pallas kernels, project(): pl.pallas_call(lambda *refs: project_kernel(len(blocks), *refs), in_specs...  3.93 us
  transfers between devices with their start and end apart: 15, of which 9 were waited for; matrix products, arithmetic and copies ran while one was open for 0% of the time, Pallas kernels for 13%

profile of v3, /device:TPU:1, one launch (start us, length us, event | category | flops | bytes accessed | tf_op | source)
XLA Modules:
  0.0 106.7 jit_solution(420414060278455478)
XLA Ops:
  0.0 1.4 %norm.1 = (bf16[16,12416]{1,0:T(8,128)(2,1)S(1)}, bf16[16,11392]{1,0:T(8,128)(2,1)S(1)}, bf16[16,1024]{1,0:T(8,128)(2,1)S(1)}) custom-call(bf16[16,8192]{1,0:T(8,128)(2,1)} %hidden_ref.1, f32[1,8192]{1,0:T(1,128)} %bitcast.12, s32[1,16]{1,0:T(1,128)} %bitcast.14, s32[1,16]{1,0:T(1,128)} %bitcast.15, bf16[16,8192]{1,0:T(8,128)(2,1)} %grad_hbm.1), custom_call_target="tpu_custom_call" | custom-call | tf_op jit(solution)/shard_map/norm/pallas_call | solution.py:374
  1.4 1.5 %collective-permute-start = (bf16[16,11392]{1,0:T(8,128)(2,1)S(1)}, bf16[16,11392]{1,0:T(8,128)(2,1)S(1)}, u32[]{:S(2)}, u32[]{:S(2)}) collective-permute-start(bf16[16,11392]{1,0:T(8,128)(2,1)S(1)} %get-tuple-element.23), channel_id=1, source_target_pairs={{0,1},{1,0},{2,3},{3,2},{4,5},{5,4},{6,7},{7,6},{8,9},{9,8},{10,11... | collective-permute-start | bytes 1093640 | tf_op jit(solution)/shard_map/ppermute | solution.py:364
  2.9 1.3 %collective-permute-done.other_ref.refs_1_ = bf16[16,11392]{1,0:T(8,128)(2,1)S(1)} collective-permute-done((bf16[16,11392]{1,0:T(8,128)(2,1)S(1)}, bf16[16,11392]{1,0:T(8,128)(2,1)S(1)}, u32[]{:S(2)}, u32[]{:S(2)}) %collective-permute-start) | collective-permute-done | bytes 364576 | tf_op jit(solution)/shard_map/ppermute | solution.py:364
  4.3 2.9 %collective-permute-start.1 = (bf16[16,12416]{1,0:T(8,128)(2,1)S(1)}, bf16[16,12416]{1,0:T(8,128)(2,1)S(1)}, u32[]{:S(2)}, u32[]{:S(2)}) collective-permute-start(bf16[16,12416]{1,0:T(8,128)(2,1)S(1)} %get-tuple-element.24.refs_0_), channel_id=1, source_target_pairs={{0,2},{1,7},{2,4},{3,1},{4,6},{5,3},{6,0},{7,5},{8,10},{9,15},{10,... | collective-permute-start | bytes 1191944 | tf_op jit(solution)/shard_map/ppermute | solution.py:367
  7.1 0.5 collective-permute-start.2
  7.6 4.0 %load.2 = (bf16[4096,1280]{1,0:T(8,128)(2,1)S(1)}, f32[8,128]{1,0:T(8,128)S(1)}) custom-call(bf16[8192,1024]{1,0:T(8,128)(2,1)} %refs_2_.7, bf16[8192,128]{1,0:T(8,128)(2,1)} %refs_3_.3, bf16[8192,128]{1,0:T(8,128)(2,1)} %refs_4_.3, bf16[16,10368]{1,0:T(8,128)(2,1)S(1)} %get-tuple-element.25.refs_3_), custom_call_target="tpu_custom_call" | custom-call | bytes 10485760 | tf_op jit(solution)/shard_map/load/pallas_call | solution.py:153
  11.7 0.3 collective-permute-done.1.near_ref.refs_2_
  12.0 3.2 %collective-permute-start.5 = (bf16[16,10368]{1,0:T(8,128)(2,1)S(1)}, bf16[16,10368]{1,0:T(8,128)(2,1)S(1)}, u32[]{:S(2)}, u32[]{:S(2)}) collective-permute-start(bf16[16,10368]{1,0:T(8,128)(2,1)S(1)} %get-tuple-element.28.refs_3_), channel_id=1, source_target_pairs={{0,2},{1,7},{2,4},{3,1},{4,6},{5,3},{6,0},{7,5},{8,10},{9,15},{10,... | collective-permute-start | bytes 995336 | tf_op jit(solution)/shard_map/ppermute | solution.py:367
  15.1 0.3 collective-permute-done.2.rows_ref.refs_3_
  15.5 1.9 %collective-permute-start.4 = (bf16[16,9344]{1,0:T(8,128)(2,1)S(1)}, bf16[16,9344]{1,0:T(8,128)(2,1)S(1)}, u32[]{:S(2)}, u32[]{:S(2)}) collective-permute-start(bf16[16,9344]{1,0:T(8,128)(2,1)S(1)} %half.2), channel_id=1, source_target_pairs={{0,1},{1,0},{2,3},{3,2},{4,5},{5,4},{6,7},{7,6},{8,9},{9,8},{10,11... | collective-permute-start | bytes 897032 | tf_op jit(solution)/shard_map/ppermute | solution.py:364
  17.4 4.0 %load.3 = (bf16[4096,1280]{1,0:T(8,128)(2,1)S(1)}, f32[8,128]{1,0:T(8,128)S(1)}) custom-call(bf16[8192,1024]{1,0:T(8,128)(2,1)} %refs_2_.7, bf16[8192,128]{1,0:T(8,128)(2,1)} %refs_3_.3, bf16[8192,128]{1,0:T(8,128)(2,1)} %refs_4_.3, bf16[16,10368]{1,0:T(8,128)(2,1)S(1)} %get-tuple-element.28.refs_3_), custom_call_target="tpu_custom_call" | custom-call | bytes 10485760 | tf_op jit(solution)/shard_map/load/pallas_call | solution.py:153
  21.4 0.1 collective-permute-start.3
  21.5 0.0 collective-permute-done.5.rows_ref.refs_6_
  21.6 0.7 collective-permute-start.6
  22.3 0.0 collective-permute-done.4.refs_5_
  22.3 0.8 collective-permute-done.3.refs_4_
  23.1 0.4 collective-permute-done.6.refs_7_
  23.5 3.9 %project.1 = (bf16[256,2432]{1,0:T(8,128)(2,1)S(1)}, bf16[128,128]{1,0:T(8,128)(2,1)S(1)}) custom-call(bf16[16,12416]{1,0:T(8,128)(2,1)S(1)} %get-tuple-element.24.refs_0_, bf16[16,11392]{1,0:T(8,128)(2,1)S(1)} %collective-permute-done.other_ref.refs_1_, bf16[16,12416]{1,0:T(8,128)(2,1)S(1)} %collective-permute-done.1.near_ref.refs_2_, ...), custom_call_target="tpu_custom_call" | custom-call | flops 2684354560 | bytes 20971520 | tf_op jit(solution)/shard_map/project/pallas_call | solution.py:205
  27.5 0.0 copy-start.2
  27.5 26.3 %all_to_all.10 = bf16[16,16,2432]{2,1,0:T(8,128)(2,1)S(1)} all-to-all(bf16[16,16,2432]{2,1,0:T(8,128)(2,1)S(1)} %bitcast.11), channel_id=1, replica_groups=mesh['dp'=16,'tensor'=8] {'dp'}, dimensions={0} | all-to-all | bytes 2490368 | tf_op jit(solution)/shard_map/all_to_all | solution.py:437
  53.8 0.0 copy-done.2
  53.8 4.6 %attend.1 = bf16[256,1280]{1,0:T(8,128)(2,1)S(1)} custom-call(bf16[256,2432]{1,0:T(8,128)(2,1)S(1)} %bitcast.9, s32[1,16]{1,0:T(1,128)S(1)} %copy-done.2), custom_call_target="tpu_custom_call" | custom-call | tf_op jit(solution)/shard_map/attend/pallas_call | solution.py:442
  58.3 14.6 %all_to_all.11 = bf16[16,16,1280]{2,1,0:T(8,128)(2,1)S(1)} all-to-all(bf16[16,16,1280]{2,1,0:T(8,128)(2,1)S(1)} %bitcast.10), channel_id=1, replica_groups=mesh['dp'=16,'tensor'=8] {'dp'}, dimensions={0} | all-to-all | bytes 1310720 | tf_op jit(solution)/shard_map/all_to_all | solution.py:450
  72.9 5.8 %back.2 = (bf16[64,4096]{1,0:T(8,128)(2,1)S(1)}, bf16[64,4096]{1,0:T(8,128)(2,1)S(1)}) custom-call(bf16[128,128]{1,0:T(8,128)(2,1)S(1)} %get-tuple-element.33.refs_0_, bf16[256,1280]{1,0:T(8,128)(2,1)S(1)} %bitcast.7, bf16[8192,1024]{1,0:T(8,128)(2,1)} %refs_2_.7, bf16[8192,128]{1,0:T(8,128)(2,1)} %refs_3_.3, bf16[8192,128]{1,0:T(8,128)(2,1)} %refs_4_.3), custom_call_target="tpu_custom_call" | custom-call | flops 1342177280 | bytes 10485760 | tf_op jit(solution)/shard_map/back/pallas_call | solution.py:324
  78.7 2.5 %collective-permute-start.7 = (bf16[64,4096]{1,0:T(8,128)(2,1)S(1)}, bf16[64,4096]{1,0:T(8,128)(2,1)S(1)}, u32[]{:S(2)}, u32[]{:S(2)}) collective-permute-start(bf16[64,4096]{1,0:T(8,128)(2,1)S(1)} %get-tuple-element.36), channel_id=1, source_target_pairs={{0,1},{1,0},{2,3},{3,2},{4,5},{5,4},{6,7},{7,6},{8,9},{9,8},{10,11... | collective-permute-start | bytes 1572872 | tf_op jit(solution)/shard_map/ppermute | solution.py:364
  81.2 5.8 %back.3 = (bf16[64,4096]{1,0:T(8,128)(2,1)S(1)}, bf16[64,4096]{1,0:T(8,128)(2,1)S(1)}) custom-call(bf16[128,128]{1,0:T(8,128)(2,1)S(1)} %get-tuple-element.33.refs_0_, bf16[256,1280]{1,0:T(8,128)(2,1)S(1)} %bitcast.8, bf16[8192,1024]{1,0:T(8,128)(2,1)} %refs_2_.7, bf16[8192,128]{1,0:T(8,128)(2,1)} %refs_3_.3, bf16[8192,128]{1,0:T(8,128)(2,1)} %refs_4_.3), custom_call_target="tpu_custom_call" | custom-call | flops 1342177280 | bytes 10485760 | tf_op jit(solution)/shard_map/back/pallas_call | solution.py:324
  87.0 0.1 collective-permute-start.11
  87.1 0.0 collective-permute-done.7
  87.1 0.1 add_convert_fusion.1
  87.3 1.6 %collective-permute-start.8 = (bf16[16,4096]{1,0:T(8,128)(2,1)S(1)}, bf16[16,4096]{1,0:T(8,128)(2,1)S(1)}, u32[]{:S(2)}, u32[]{:S(2)}) collective-permute-start(bf16[16,4096]{1,0:T(8,128)(2,1)S(1)} %get-tuple-element.43), channel_id=1, source_target_pairs={{0,2},{1,7},{2,4},{3,1},{4,6},{5,3},{6,0},{7,5},{8,10},{9,15},{10,... | collective-permute-start | bytes 393224 | tf_op jit(solution)/shard_map/ppermute | solution.py:367
  88.8 0.1 collective-permute-done.11
  89.0 0.1 add_convert_fusion
  89.1 0.0 copy-start
  89.1 0.0 copy-start.1
  89.2 1.6 %collective-permute-start.12 = (bf16[16,4096]{1,0:T(8,128)(2,1)S(1)}, bf16[16,4096]{1,0:T(8,128)(2,1)S(1)}, u32[]{:S(2)}, u32[]{:S(2)}) collective-permute-start(bf16[16,4096]{1,0:T(8,128)(2,1)S(1)} %get-tuple-element.40), channel_id=1, source_target_pairs={{0,2},{1,7},{2,4},{3,1},{4,6},{5,3},{6,0},{7,5},{8,10},{9,15},{10,... | collective-permute-start | bytes 393224 | tf_op jit(solution)/shard_map/ppermute | solution.py:367
  90.8 0.4 collective-permute-done.8
  91.2 2.8 %collective-permute-start.9 = (bf16[32,4096]{1,0:T(8,128)(2,1)S(1)}, bf16[32,4096]{1,0:T(8,128)(2,1)S(1)}, u32[]{:S(2)}, u32[]{:S(2)}) collective-permute-start(bf16[32,4096]{1,0:T(8,128)(2,1)S(1)} %pad_maximum_fusion), channel_id=1, source_target_pairs={{0,2},{1,7},{2,4},{3,1},{4,6},{5,3},{6,0},{7,5},{8,10},{9,15},{10,... | collective-permute-start | bytes 786440 | tf_op jit(solution)/shard_map/ppermute | solution.py:367
  94.0 0.0 collective-permute-done.12
  94.1 1.8 %collective-permute-start.13 = (bf16[32,4096]{1,0:T(8,128)(2,1)S(1)}, bf16[32,4096]{1,0:T(8,128)(2,1)S(1)}, u32[]{:S(2)}, u32[]{:S(2)}) collective-permute-start(bf16[32,4096]{1,0:T(8,128)(2,1)S(1)} %pad_maximum_fusion.1), channel_id=1, source_target_pairs={{0,2},{1,7},{2,4},{3,1},{4,6},{5,3},{6,0},{7,5},{8,10},{9,15},{10,... | collective-permute-start | bytes 786440 | tf_op jit(solution)/shard_map/ppermute | solution.py:367
  95.9 1.4 %collective-permute-done.9 = bf16[32,4096]{1,0:T(8,128)(2,1)S(1)} collective-permute-done((bf16[32,4096]{1,0:T(8,128)(2,1)S(1)}, bf16[32,4096]{1,0:T(8,128)(2,1)S(1)}, u32[]{:S(2)}, u32[]{:S(2)}) %collective-permute-start.9) | collective-permute-done | bytes 262176 | tf_op jit(solution)/shard_map/ppermute | solution.py:367
  97.3 4.5 %collective-permute-start.10 = (bf16[16,4096]{1,0:T(8,128)(2,1)S(1)}, bf16[16,4096]{1,0:T(8,128)(2,1)S(1)}, u32[]{:S(2)}, u32[]{:S(2)}) collective-permute-start(bf16[16,4096]{1,0:T(8,128)(2,1)S(1)} %get-tuple-element.47), channel_id=1, source_target_pairs={{0,1},{1,0},{2,3},{3,2},{4,5},{5,4},{6,7},{7,6},{8,9},{9,8},{10,11... | collective-permute-start | bytes 393224 | tf_op jit(solution)/shard_map/ppermute | solution.py:364
  101.8 0.0 collective-permute-done.13
  101.8 2.8 %collective-permute-start.14 = (bf16[16,4096]{1,0:T(8,128)(2,1)S(1)}, bf16[16,4096]{1,0:T(8,128)(2,1)S(1)}, u32[]{:S(2)}, u32[]{:S(2)}) collective-permute-start(bf16[16,4096]{1,0:T(8,128)(2,1)S(1)} %get-tuple-element.45), channel_id=1, source_target_pairs={{0,1},{1,0},{2,3},{3,2},{4,5},{5,4},{6,7},{7,6},{8,9},{9,8},{10,11... | collective-permute-start | bytes 393224 | tf_op jit(solution)/shard_map/ppermute | solution.py:364
  104.6 0.0 collective-permute-done.10.refs_2_
  104.6 1.0 collective-permute-done.14.refs_5_
  105.6 0.0 copy-done
  105.6 0.0 copy-done.1
  105.6 1.1 %finish.1 = bf16[16,8192]{1,0:T(8,128)(2,1)} custom-call(bf16[16,8192]{1,0:T(8,128)(2,1)S(1)} %copy-done, f32[1,8192]{1,0:T(1,128)S(1)} %bitcast.13, bf16[16,4096]{1,0:T(8,128)(2,1)S(1)} %get-tuple-element.44.refs_0_, bf16[16,4096]{1,0:T(8,128)(2,1)S(1)} %get-tuple-element.48.refs_1_, bf16[16,4096]{1,0:T(8,128)(2,1)S(1)} %collective-permute-done.10.refs_2_, ...), custom_call_target="tpu_custom_call" | custom-call | tf_op jit(solution)/shard_map/finish/pallas_call | solution.py:466
  (12 shorter events, 0.3 us)
Async XLA Ops:
  1.4 2.8 %collective-permute-start = (bf16[16,11392]{1,0:T(8,128)(2,1)S(1)}, bf16[16,11392]{1,0:T(8,128)(2,1)S(1)}, u32[]{:S(2)}, u32[]{:S(2)}) collective-permute-start(bf16[16,11392]{1,0:T(8,128)(2,1)S(1)} %get-tuple-element.23), channel_id=1, source_target_pairs={{0,1},{1,0},{2,3},{3,2},{4,5},{5,4},{6,7},{7,6},{8,9},{9,8},{10,11... | collective-permute-start | bytes 1093640 | tf_op jit(solution)/shard_map/ppermute | solution.py:364
  4.3 7.7 %collective-permute-start.1 = (bf16[16,12416]{1,0:T(8,128)(2,1)S(1)}, bf16[16,12416]{1,0:T(8,128)(2,1)S(1)}, u32[]{:S(2)}, u32[]{:S(2)}) collective-permute-start(bf16[16,12416]{1,0:T(8,128)(2,1)S(1)} %get-tuple-element.24.refs_0_), channel_id=1, source_target_pairs={{0,2},{1,7},{2,4},{3,1},{4,6},{5,3},{6,0},{7,5},{8,10},{9,15},{10,... | collective-permute-start | bytes 1191944 | tf_op jit(solution)/shard_map/ppermute | solution.py:367
  7.1 8.3 %collective-permute-start.2 = (bf16[16,10368]{1,0:T(8,128)(2,1)S(1)}, bf16[16,10368]{1,0:T(8,128)(2,1)S(1)}, u32[]{:S(2)}, u32[]{:S(2)}) collective-permute-start(bf16[16,10368]{1,0:T(8,128)(2,1)S(1)} %get-tuple-element.25.refs_3_), channel_id=1, source_target_pairs={{0,2},{1,7},{2,4},{3,1},{4,6},{5,3},{6,0},{7,5},{8,10},{9,15},{10,... | collective-permute-start | bytes 995336 | tf_op jit(solution)/shard_map/ppermute | solution.py:367
  12.0 9.6 %collective-permute-start.5 = (bf16[16,10368]{1,0:T(8,128)(2,1)S(1)}, bf16[16,10368]{1,0:T(8,128)(2,1)S(1)}, u32[]{:S(2)}, u32[]{:S(2)}) collective-permute-start(bf16[16,10368]{1,0:T(8,128)(2,1)S(1)} %get-tuple-element.28.refs_3_), channel_id=1, source_target_pairs={{0,2},{1,7},{2,4},{3,1},{4,6},{5,3},{6,0},{7,5},{8,10},{9,15},{10,... | collective-permute-start | bytes 995336 | tf_op jit(solution)/shard_map/ppermute | solution.py:367
  15.5 6.8 %collective-permute-start.4 = (bf16[16,9344]{1,0:T(8,128)(2,1)S(1)}, bf16[16,9344]{1,0:T(8,128)(2,1)S(1)}, u32[]{:S(2)}, u32[]{:S(2)}) collective-permute-start(bf16[16,9344]{1,0:T(8,128)(2,1)S(1)} %half.2), channel_id=1, source_target_pairs={{0,1},{1,0},{2,3},{3,2},{4,5},{5,4},{6,7},{7,6},{8,9},{9,8},{10,11... | collective-permute-start | bytes 897032 | tf_op jit(solution)/shard_map/ppermute | solution.py:364
  21.4 1.7 %collective-permute-start.3 = (bf16[16,9344]{1,0:T(8,128)(2,1)S(1)}, bf16[16,9344]{1,0:T(8,128)(2,1)S(1)}, u32[]{:S(2)}, u32[]{:S(2)}) collective-permute-start(bf16[16,9344]{1,0:T(8,128)(2,1)S(1)} %get-tuple-element.27), channel_id=1, source_target_pairs={{0,1},{1,0},{2,3},{3,2},{4,5},{5,4},{6,7},{7,6},{8,9},{9,8},{10,11... | collective-permute-start | bytes 897032 | tf_op jit(solution)/shard_map/ppermute | solution.py:364
  21.6 2.0 %collective-permute-start.6 = (bf16[16,9344]{1,0:T(8,128)(2,1)S(1)}, bf16[16,9344]{1,0:T(8,128)(2,1)S(1)}, u32[]{:S(2)}, u32[]{:S(2)}) collective-permute-start(bf16[16,9344]{1,0:T(8,128)(2,1)S(1)} %half.3), channel_id=1, source_target_pairs={{0,1},{1,0},{2,3},{3,2},{4,5},{5,4},{6,7},{7,6},{8,9},{9,8},{10,11... | collective-permute-start | bytes 897032 | tf_op jit(solution)/shard_map/ppermute | solution.py:364
  27.5 26.3 %copy-start.2 = (s32[1,16]{1,0:T(1,128)S(1)}, s32[1,16]{1,0:T(1,128)}, u32[]{:S(2)}) copy-start(s32[1,16]{1,0:T(1,128)} %rewards_ref.1) | copy-start | bytes 196
  78.7 8.4 %collective-permute-start.7 = (bf16[64,4096]{1,0:T(8,128)(2,1)S(1)}, bf16[64,4096]{1,0:T(8,128)(2,1)S(1)}, u32[]{:S(2)}, u32[]{:S(2)}) collective-permute-start(bf16[64,4096]{1,0:T(8,128)(2,1)S(1)} %get-tuple-element.36), channel_id=1, source_target_pairs={{0,1},{1,0},{2,3},{3,2},{4,5},{5,4},{6,7},{7,6},{8,9},{9,8},{10,11... | collective-permute-start | bytes 1572872 | tf_op jit(solution)/shard_map/ppermute | solution.py:364
  87.0 2.0 %collective-permute-start.11 = (bf16[64,4096]{1,0:T(8,128)(2,1)S(1)}, bf16[64,4096]{1,0:T(8,128)(2,1)S(1)}, u32[]{:S(2)}, u32[]{:S(2)}) collective-permute-start(bf16[64,4096]{1,0:T(8,128)(2,1)S(1)} %get-tuple-element.38), channel_id=1, source_target_pairs={{0,1},{1,0},{2,3},{3,2},{4,5},{5,4},{6,7},{7,6},{8,9},{9,8},{10,11... | collective-permute-start | bytes 1572872 | tf_op jit(solution)/shard_map/ppermute | solution.py:364
  87.3 3.9 %collective-permute-start.8 = (bf16[16,4096]{1,0:T(8,128)(2,1)S(1)}, bf16[16,4096]{1,0:T(8,128)(2,1)S(1)}, u32[]{:S(2)}, u32[]{:S(2)}) collective-permute-start(bf16[16,4096]{1,0:T(8,128)(2,1)S(1)} %get-tuple-element.43), channel_id=1, source_target_pairs={{0,2},{1,7},{2,4},{3,1},{4,6},{5,3},{6,0},{7,5},{8,10},{9,15},{10,... | collective-permute-start | bytes 393224 | tf_op jit(solution)/shard_map/ppermute | solution.py:367
  89.1 16.5 %copy-start = (bf16[16,8192]{1,0:T(8,128)(2,1)S(1)}, bf16[16,8192]{1,0:T(8,128)(2,1)}, u32[]{:S(2)}) copy-start(bf16[16,8192]{1,0:T(8,128)(2,1)} %hidden_ref.1) | copy-start | bytes 786436
  89.1 16.5 %copy-start.1 = (f32[8192]{0:T(1024)S(1)}, f32[8192]{0:T(1024)}, u32[]{:S(2)}) copy-start(f32[8192]{0:T(1024)} %param.10) | copy-start | bytes 98308
  89.2 4.9 %collective-permute-start.12 = (bf16[16,4096]{1,0:T(8,128)(2,1)S(1)}, bf16[16,4096]{1,0:T(8,128)(2,1)S(1)}, u32[]{:S(2)}, u32[]{:S(2)}) collective-permute-start(bf16[16,4096]{1,0:T(8,128)(2,1)S(1)} %get-tuple-element.40), channel_id=1, source_target_pairs={{0,2},{1,7},{2,4},{3,1},{4,6},{5,3},{6,0},{7,5},{8,10},{9,15},{10,... | collective-permute-start | bytes 393224 | tf_op jit(solution)/shard_map/ppermute | solution.py:367
  91.2 6.1 %collective-permute-start.9 = (bf16[32,4096]{1,0:T(8,128)(2,1)S(1)}, bf16[32,4096]{1,0:T(8,128)(2,1)S(1)}, u32[]{:S(2)}, u32[]{:S(2)}) collective-permute-start(bf16[32,4096]{1,0:T(8,128)(2,1)S(1)} %pad_maximum_fusion), channel_id=1, source_target_pairs={{0,2},{1,7},{2,4},{3,1},{4,6},{5,3},{6,0},{7,5},{8,10},{9,15},{10,... | collective-permute-start | bytes 786440 | tf_op jit(solution)/shard_map/ppermute | solution.py:367
  94.1 7.7 %collective-permute-start.13 = (bf16[32,4096]{1,0:T(8,128)(2,1)S(1)}, bf16[32,4096]{1,0:T(8,128)(2,1)S(1)}, u32[]{:S(2)}, u32[]{:S(2)}) collective-permute-start(bf16[32,4096]{1,0:T(8,128)(2,1)S(1)} %pad_maximum_fusion.1), channel_id=1, source_target_pairs={{0,2},{1,7},{2,4},{3,1},{4,6},{5,3},{6,0},{7,5},{8,10},{9,15},{10,... | collective-permute-start | bytes 786440 | tf_op jit(solution)/shard_map/ppermute | solution.py:367
  97.3 7.3 %collective-permute-start.10 = (bf16[16,4096]{1,0:T(8,128)(2,1)S(1)}, bf16[16,4096]{1,0:T(8,128)(2,1)S(1)}, u32[]{:S(2)}, u32[]{:S(2)}) collective-permute-start(bf16[16,4096]{1,0:T(8,128)(2,1)S(1)} %get-tuple-element.47), channel_id=1, source_target_pairs={{0,1},{1,0},{2,3},{3,2},{4,5},{5,4},{6,7},{7,6},{8,9},{9,8},{10,11... | collective-permute-start | bytes 393224 | tf_op jit(solution)/shard_map/ppermute | solution.py:364
  101.8 3.8 %collective-permute-start.14 = (bf16[16,4096]{1,0:T(8,128)(2,1)S(1)}, bf16[16,4096]{1,0:T(8,128)(2,1)S(1)}, u32[]{:S(2)}, u32[]{:S(2)}) collective-permute-start(bf16[16,4096]{1,0:T(8,128)(2,1)S(1)} %get-tuple-element.45), channel_id=1, source_target_pairs={{0,1},{1,0},{2,3},{3,2},{4,5},{5,4},{6,7},{7,6},{8,9},{9,8},{10,11... | collective-permute-start | bytes 393224 | tf_op jit(solution)/shard_map/ppermute | solution.py:364

commit v4 on v3

--- a/solution.py
+++ b/solution.py
@@ -47,7 +47,7 @@
     return here // 2, here % 2, lax.axis_size("tensor") // 2
 
 
-def norm_kernel(hidden_hbm, gain_hbm, owner_hbm, completion_hbm, grad_hbm, leave_ref, cross_ref, own_ref, *rest):
+def norm_kernel(hidden_hbm, gain_hbm, owner_hbm, completion_hbm, grad_hbm, leave_ref, cross_ref, next_ref, own_ref, *rest):
     hidden_ref, gain_ref, owner_ref, completion_ref, grad_ref, sems = rest
     copies = [
         pltpu.make_async_copy(src, dst, sems.at[i])
@@ -91,37 +91,40 @@
 
     up, down = (chip + 1) % chips, (chip + chips - 1) % chips
     at = width + EXT
-    leave_ref[:, at : at + 2 * each] = heads(2 * jnp.where(core == 0, up, down), 2)
-    leave_ref[:, at + 2 * each :] = heads(2 * ((chip + 2) % chips), 2)
+    leave_ref[:, at:] = heads(2 * ((chip + 2) % chips), 2)
+    next_ref[...] = heads(2 * jnp.where(core == 0, up, down), 2)
     cross_ref[:, at : at + 2 * each] = heads(2 * jnp.where(core == 0, down, up), 2)
     cross_ref[:, at + 2 * each :] = heads(2 * chip + 1 - core, 1)
     own_ref[...] = heads(2 * chip + core, 1)
 
 
-def join_kernel(mine_ref, other_ref, mine_out, other_out):
-    mine_out[...] = mine_ref[...]
-    other_out[...] = other_ref[:, 0 : other_out.shape[1]]
-
-
-def half(rows_ref, out_ref):
+def join_kernel(other_ref, next_ref, out_ref):
+    n = out_ref.shape[1] - next_ref.shape[1]
+    out_ref[:, 0:n] = other_ref[:, 0:n]
+    out_ref[:, n:] = next_ref[...]
+
+
+def half(rows_ref, heads_ref, at, out_ref):
     n = HEADS_AT
     each = out_ref.shape[1] - n
     _, core, _ = chip_and_core()
     out_ref[:, 0:n] = rows_ref[:, 0:n]
-    first, second = rows_ref[:, n : n + each], rows_ref[:, n + each : n + 2 * each]
+    first, second = heads_ref[:, at : at + each], heads_ref[:, at + each : at + 2 * each]
     out_ref[:, n:] = jnp.where(core == 0, second, first)
 
 
-def half_kernel(rows_ref, _, out_ref):
-    half(rows_ref, out_ref)
-
-
-def relay_kernel(near_ref, _, pass_ref, half_ref):
-    n = HEADS_AT
-    each = half_ref.shape[1] - n
-    pass_ref[:, 0:n] = near_ref[:, 0:n]
-    pass_ref[:, n:] = near_ref[:, n + 2 * each :]
-    half(near_ref, half_ref)
+def half_near_kernel(near_ref, near_o_ref, _, out_ref, out_o_ref):
+    each = out_ref.shape[1] - HEADS_AT
+    half(near_ref, near_o_ref, HEADS_AT + 2 * each, out_ref)
+    half(near_o_ref, near_o_ref, HEADS_AT, out_o_ref)
+
+
+def half_far_kernel(far_ref, _, out_ref):
+    half(far_ref, far_ref, HEADS_AT, out_ref)
+
+
+def relay_kernel(near_ref, _, out_ref):
+    out_ref[...] = near_ref[...]
 
 
 def load_kernel(part, wq_hbm, wk_hbm, wv_hbm, _, out_ref, token_ref, sems):
@@ -189,12 +192,12 @@
     n = HEADS_AT
     each = own_ref.shape[1]
 
-    def heads(b):
-        return jnp.where(core == 0, b[:, n : n + each], b[:, n + each : n + 2 * each])
+    def heads(b, at):
+        return jnp.where(core == 0, b[:, at : at + each], b[:, at + each : at + 2 * each])
 
     mine, other, near, near_o, across, across_o, far, far_o = blocks
-    grads = [own_ref[...], other[:, n + 2 * each :], heads(near), heads(near_o)]
-    grads += [across[:, n:], across_o[:, n:], heads(far), far_o[:, n:]]
+    grads = [own_ref[...], other[:, n + 2 * each :], heads(near_o, n + 2 * each), heads(near_o, n)]
+    grads += [across[:, n:], across_o[:, n:], heads(far, n), far_o[:, n:]]
     out_ref[:, cols + EXT :] = dot(spread, jnp.concatenate(grads, axis=0), ((0,), (0,))).astype(BF16)
 
 
@@ -277,72 +280,44 @@
     out_ref[:, vcol : vcol + HD] = grad_value.astype(BF16)
 
 
-def weight_copies(part, weights, w_ref, sems):
-    span = w_ref.shape[0]
-    step = span // PIECES
-    copies = []
-    for j in range(PIECES):
-        at = 0
-        for w in weights:
-            n = w.shape[1]
-            copies.append(
-                pltpu.make_async_copy(
-                    w.at[pl.ds(part * span + j * step, step), :],
-                    w_ref.at[pl.ds(j * step, step), pl.ds(at, n)],
-                    sems.at[len(copies)],
-                )
-            )
-            at += n
-    return copies
-
-
-def back_kernel(part, ext_ref, slots_ref, wq_hbm, wk_hbm, wv_hbm, keep_ref, send_ref, w_ref, sems):
-    span = w_ref.shape[0]
-    step = span // PIECES
-    copies = weight_copies(part, (wq_hbm, wk_hbm, wv_hbm), w_ref, sems)
-    for copy in copies:
-        copy.start()
-    half = keep_ref.shape[0]
+def back_kernel(ext_ref, slots_ref, w_ref, keep_ref, send_ref):
+    half_rows, span = keep_ref.shape
     slots = slots_ref.shape[0]
     hot = (ext_ref[:, 0:1].astype(F32) == iota((ext_ref.shape[0], slots), 1).astype(F32)).astype(BF16)
     held = dot(hot, slots_ref[...], ((1,), (0,))).astype(BF16)
-    for j in range(PIECES):
-        for copy in copies[3 * j : 3 * j + 3]:
-            copy.wait()
-        at = slice(j * step, (j + 1) * step)
+    for j in range(span // STEP):
+        at = slice(j * STEP, (j + 1) * STEP)
         term = dot(held, w_ref[at, :], ((1,), (1,))).astype(BF16)
-        keep_ref[:, at] = term[0:half]
-        send_ref[:, at] = term[half:]
-
-
-def back(part, ext, slot_grads, weights):
+        keep_ref[:, at] = term[0:half_rows]
+        send_ref[:, at] = term[half_rows:]
+
+
+def back(ext, slot_grads, w):
     rows = ext.shape[0]
-    width = weights[0].shape[0]
-    span = width // PARTS
-    cols = sum(w.shape[1] for w in weights)
+    span, cols = w.shape
     out = jax.ShapeDtypeStruct((rows // 2, span), BF16)
     return pl.pallas_call(
-        lambda *refs: back_kernel(part, *refs),
-        in_specs=[VMEM, VMEM] + [ANY] * 3,
+        back_kernel,
+        in_specs=[VMEM] * 3,
         out_specs=[VMEM] * 2,
         out_shape=[out, out],
-        scratch_shapes=[pltpu.VMEM((span, cols), BF16), pltpu.SemaphoreType.DMA((3 * PIECES,))],
-        compiler_params=params(20),
+        compiler_params=params(),
         cost_estimate=pl.CostEstimate(
             flops=2 * rows * span * cols, bytes_accessed=2 * span * cols, transcendentals=0
         ),
         name="back",
-    )(ext, slot_grads, *[in_hbm(w) for w in weights])
-
-
-def finish_kernel(hidden_ref, gain_ref, *refs):
+    )(ext, slot_grads, in_vmem(w))
+
+
+def finish_kernel(counts, hidden_ref, gain_ref, *refs):
     out_ref = refs[-1]
     wide = hidden_ref[...].astype(F32)
     inverse = lax.rsqrt(jnp.mean(wide * wide, axis=1, keepdims=True) + EPSILON)
     parts = []
-    for i in range(PARTS):
-        a, b, c = refs[3 * i : 3 * i + 3]
-        parts.append(a[...].astype(F32) + b[...].astype(F32) + c[...].astype(F32))
+    at = 0
+    for n in counts:
+        parts.append(sum(ref[...].astype(F32) for ref in refs[at : at + n]))
+        at += n
     scaled = jnp.concatenate(parts, axis=1) * gain_ref[...]
     inner = jnp.mean(scaled * wide, axis=1, keepdims=True)
     out_ref[...] = (inverse * scaled - wide * inverse * inverse * inverse * inner).astype(BF16)
@@ -371,11 +346,11 @@
     def rows_of(cols):
         return jax.ShapeDtypeStruct((count, cols), BF16)
 
-    leave, cross, own = pl.pallas_call(
+    leave, cross, onto_next, own = pl.pallas_call(
         norm_kernel,
         in_specs=[ANY] * 5,
-        out_specs=[VMEM] * 3,
-        out_shape=[rows_of(near_cols + 2 * query_cols), rows_of(near_cols + query_cols), rows_of(query_cols)],
+        out_specs=[VMEM] * 4,
+        out_shape=[rows_of(n) for n in (near_cols, near_cols + query_cols, 2 * query_cols, query_cols)],
         scratch_shapes=[
             pltpu.VMEM((count, width), BF16),
             pltpu.VMEM((1, width), F32),
@@ -392,46 +367,49 @@
             for x in (hidden, gain.reshape(1, width), owner.reshape(1, count), completion.reshape(1, count), out_grad)
         ]
     )
+    near = flow(leave)
     other = swap(cross)
-    mine, leave_o = pl.pallas_call(
+    leave_o = pl.pallas_call(
         join_kernel,
         in_specs=[VMEM] * 2,
-        out_specs=[VMEM] * 2,
-        out_shape=[rows_of(near_cols + 2 * query_cols), rows_of(near_cols)],
+        out_specs=VMEM,
+        out_shape=rows_of(near_cols + 2 * query_cols),
         compiler_params=params(),
         name="join",
-    )(leave, other)
+    )(other, onto_next)
 
     weights = (w_query, w_key, w_value)
-    near = flow(mine)
     near_o = flow(leave_o)
     first, ready = load(0, weights, leave_o)
-    half_rows = rows_of(HEADS_AT + query_cols)
-    passed, half_near = pl.pallas_call(
+    passed = pl.pallas_call(
         relay_kernel,
         in_specs=[VMEM] * 2,
-        out_specs=[VMEM] * 2,
-        out_shape=[rows_of(near_cols), half_rows],
+        out_specs=VMEM,
+        out_shape=rows_of(near_cols),
         compiler_params=params(),
         name="relay",
     )(near, ready)
     far = flow(passed)
     second, ready_too = load(1, weights, passed)
 
-    def half_of(rows, after):
-        return pl.pallas_call(
-            half_kernel,
-            in_specs=[VMEM] * 2,
-            out_specs=VMEM,
-            out_shape=half_rows,
-            compiler_params=params(),
-            name="half",
-        )(rows, after)
-
-    across = swap(half_near)
-    across_o = swap(half_of(near_o, ready))
-    far_o = swap(half_of(far, ready_too))
-    blocks = (mine, other, near, near_o, across, across_o, far, far_o)
+    half_rows = rows_of(HEADS_AT + query_cols)
+    half_near, half_near_o = pl.pallas_call(
+        half_near_kernel,
+        in_specs=[VMEM] * 3,
+        out_specs=[VMEM] * 2,
+        out_shape=[half_rows] * 2,
+        compiler_params=params(),
+        name="half_near",
+    )(near, near_o, ready_too)
+    half_far = pl.pallas_call(
+        half_far_kernel,
+        in_specs=[VMEM] * 2,
+        out_specs=VMEM,
+        out_shape=half_rows,
+        compiler_params=params(),
+        name="half_far",
+    )(far, ready_too)
+    blocks = (leave, other, near, near_o, swap(half_near), swap(half_near_o), far, swap(half_far))
     loaded = (first, second)
     total, ext = project(blocks, loaded, own, slots)
     got = lax.all_to_all(
@@ -451,20 +429,27 @@
         grads.reshape(groups, 2 * ranks, cols), "dp", split_axis=0, concat_axis=0, tiled=True
     ).reshape(grads.shape)
 
+    def add(a, b):
+        return (a.astype(F32) + b.astype(F32)).astype(BF16)
+
     pieces = []
     for i in range(PARTS):
-        keep, send = back(i, ext, slot_grads, weights)
-        both = (keep.astype(F32) + swap(send).astype(F32)).astype(BF16)
+        keep, send = back(ext, slot_grads, loaded[i])
+        both = add(keep, swap(send))
+        mine, onward = both[:count], both[count : 3 * count]
         passed = flow(both[3 * count :])
-        onward = both[count : 3 * count]
-        onward = jnp.concatenate(
-            [onward[:count], (onward[count:].astype(F32) + passed.astype(F32)).astype(BF16)], axis=0
-        )
-        came = flow(onward)
-        pieces += [both[:count], came[count:], swap(came[:count])]
+        if i < PARTS - 1:
+            came = flow(onward)
+            mine = (mine, flow(passed))
+        else:
+            came = flow(jnp.concatenate([onward[:count], add(onward[count:], passed)], axis=0))
+            mine = (mine,)
+        pieces.append((*mine, came[count:], swap(came[:count])))
+    counts = [len(p) for p in pieces]
+    pieces = [x for p in pieces for x in p]
 
     return pl.pallas_call(
-        finish_kernel,
+        lambda *refs: finish_kernel(counts, *refs),
         in_specs=[VMEM] * (2 + len(pieces)),
         out_specs=VMEM,
         out_shape=jax.ShapeDtypeStruct((count, width), BF16),

time: 107 us -> 97.2 us (0.908)
  Pallas kernels: 30.8 us -> 25.4 us
  starting transfers between devices: 28.4 us -> 25 us
    pallas_call x8, Pallas kernels: 14.2 us -> 8.69 us  [the longest x2 6.04 us: back(): pl.pallas_call(back_kernel, in_specs=[VMEM] * 3, out_specs=[VMEM] * 2, ou...]
    ppermute x8, starting transfers between devices: 14.1 us -> 12 us  [swap(): return lax.ppermute(x, 'tensor', swap_pairs)]
    ppermute x7 -> x8, starting transfers between devices: 14.4 us -> 12.9 us  [flow(): return lax.ppermute(x, 'tensor', flow_pairs)]
    ppermute x7 -> x8, waiting for transfers between devices: 2.39 us -> 2.3 us  [flow(): return lax.ppermute(x, 'tensor', flow_pairs)]
  transfers between devices with their start and end apart: 15 -> 16, of which waited for: 9 -> 9; matrix products, arithmetic and copies ran while one was open for 0% -> 0% of each run, Pallas kernels for 13% -> 12%
where the time goes in v4:
time: 97.2 us; the launch traced here: 97 us
  blocking collectives  40.8 us (42%)
  Pallas kernels  25.4 us (26%)
  starting transfers between devices  25 us (26%)
  waiting for transfers between devices  5.25 us (5%)
    all_to_all x1, blocking collectives, on_device(): lax.all_to_all(total.reshape(groups, 2 * ranks, total.shape[1]), 'dp', sp...  26.3 us
    all_to_all x1, blocking collectives, on_device(): lax.all_to_all(grads.reshape(groups, 2 * ranks, cols), 'dp', split_axis=0...  14.5 us
    ppermute x8, starting transfers between devices, flow(): return lax.ppermute(x, 'tensor', flow_pairs)  12.9 us
    ppermute x8, starting transfers between devices, swap(): return lax.ppermute(x, 'tensor', swap_pairs)  12 us
    pallas_call x2, Pallas kernels, load(): pl.pallas_call(lambda *refs: load_kernel(part, *refs), in_specs=[ANY] * 3...  8.08 us
    pallas_call x2, Pallas kernels, back(): pl.pallas_call(back_kernel, in_specs=[VMEM] * 3, out_specs=[VMEM] * 2, ou...  6.04 us
    pallas_call x1, Pallas kernels, on_device(): pl.pallas_call(attend_kernel, in_specs=[VMEM] * 2, out_specs=VMEM, out_sh...  4.55 us
    pallas_call x1, Pallas kernels, project(): pl.pallas_call(lambda *refs: project_kernel(len(blocks), *refs), in_specs...  4.05 us
  transfers between devices with their start and end apart: 16, of which 9 were waited for; matrix products, arithmetic and copies ran while one was open for 0% of the time, Pallas kernels for 12%

profile of v4, /device:TPU:1, one launch (start us, length us, event | category | flops | bytes accessed | tf_op | source)
XLA Modules:
  0.0 97.0 jit_solution(10675733467795648537)
XLA Ops:
  0.0 1.4 %norm.1 = (bf16[16,10368]{1,0:T(8,128)(2,1)S(1)}, bf16[16,11392]{1,0:T(8,128)(2,1)S(1)}, bf16[16,2048]{1,0:T(8,128)(2,1)S(1)}, bf16[16,1024]{1,0:T(8,128)(2,1)S(1)}) custom-call(bf16[16,8192]{1,0:T(8,128)(2,1)} %refs_0_.5, f32[1,8192]{1,0:T(1,128)} %bitcast.12, s32[1,16]{1,0:T(1,128)} %bitcast.14, s32[1,16]{1,0:T(1,128)} %bitcast.15, bf16[16,8192]{1,0:T(8,128)(2,1)} %grad_hbm.1), custom_call_target="tpu_custom_call" | custom-call | tf_op jit(solution)/shard_map/norm/pallas_call | solution.py:349
  1.4 1.5 %collective-permute-start = (bf16[16,11392]{1,0:T(8,128)(2,1)S(1)}, bf16[16,11392]{1,0:T(8,128)(2,1)S(1)}, u32[]{:S(2)}, u32[]{:S(2)}) collective-permute-start(bf16[16,11392]{1,0:T(8,128)(2,1)S(1)} %get-tuple-element.22), channel_id=1, source_target_pairs={{0,1},{1,0},{2,3},{3,2},{4,5},{5,4},{6,7},{7,6},{8,9},{9,8},{10,11... | collective-permute-start | bytes 1093640 | tf_op jit(solution)/shard_map/ppermute | solution.py:339
  2.9 2.8 %collective-permute-start.1 = (bf16[16,10368]{1,0:T(8,128)(2,1)S(1)}, bf16[16,10368]{1,0:T(8,128)(2,1)S(1)}, u32[]{:S(2)}, u32[]{:S(2)}) collective-permute-start(bf16[16,10368]{1,0:T(8,128)(2,1)S(1)} %get-tuple-element.21.refs_0_), channel_id=1, source_target_pairs={{0,2},{1,7},{2,4},{3,1},{4,6},{5,3},{6,0},{7,5},{8,10},{9,15},{10,... | collective-permute-start | bytes 995336 | tf_op jit(solution)/shard_map/ppermute | solution.py:342
  5.7 0.0 collective-permute-done.other_ref.refs_1_
  5.7 1.4 %collective-permute-start.2 = (bf16[16,12416]{1,0:T(8,128)(2,1)S(1)}, bf16[16,12416]{1,0:T(8,128)(2,1)S(1)}, u32[]{:S(2)}, u32[]{:S(2)}) collective-permute-start(bf16[16,12416]{1,0:T(8,128)(2,1)S(1)} %join.1.refs_3_), channel_id=1, source_target_pairs={{0,2},{1,7},{2,4},{3,1},{4,6},{5,3},{6,0},{7,5},{8,10},{9,15},{10,... | collective-permute-start | bytes 1191944 | tf_op jit(solution)/shard_map/ppermute | solution.py:342
  7.1 4.0 %load.2 = (bf16[4096,1280]{1,0:T(8,128)(2,1)S(1)}, f32[8,128]{1,0:T(8,128)S(1)}) custom-call(bf16[8192,1024]{1,0:T(8,128)(2,1)} %refs_0_.4, bf16[8192,128]{1,0:T(8,128)(2,1)} %refs_1_.3, bf16[8192,128]{1,0:T(8,128)(2,1)} %refs_2_.3, bf16[16,12416]{1,0:T(8,128)(2,1)S(1)} %join.1.refs_3_), custom_call_target="tpu_custom_call" | custom-call | bytes 10485760 | tf_op jit(solution)/shard_map/load/pallas_call | solution.py:156
  11.2 0.0 collective-permute-done.1.near_ref.refs_2_
  11.2 1.8 %collective-permute-start.5 = (bf16[16,10368]{1,0:T(8,128)(2,1)S(1)}, bf16[16,10368]{1,0:T(8,128)(2,1)S(1)}, u32[]{:S(2)}, u32[]{:S(2)}) collective-permute-start(bf16[16,10368]{1,0:T(8,128)(2,1)S(1)} %relay.1.refs_3_), channel_id=1, source_target_pairs={{0,2},{1,7},{2,4},{3,1},{4,6},{5,3},{6,0},{7,5},{8,10},{9,15},{10,... | collective-permute-start | bytes 995336 | tf_op jit(solution)/shard_map/ppermute | solution.py:342
  13.0 4.0 %load.3 = (bf16[4096,1280]{1,0:T(8,128)(2,1)S(1)}, f32[8,128]{1,0:T(8,128)S(1)}) custom-call(bf16[8192,1024]{1,0:T(8,128)(2,1)} %refs_0_.4, bf16[8192,128]{1,0:T(8,128)(2,1)} %refs_1_.3, bf16[8192,128]{1,0:T(8,128)(2,1)} %refs_2_.3, bf16[16,10368]{1,0:T(8,128)(2,1)S(1)} %relay.1.refs_3_), custom_call_target="tpu_custom_call" | custom-call | bytes 10485760 | tf_op jit(solution)/shard_map/load/pallas_call | solution.py:156
  17.0 0.6 collective-permute-done.5.far_ref.refs_6_
  17.6 2.2 %collective-permute-start.6 = (bf16[16,9344]{1,0:T(8,128)(2,1)S(1)}, bf16[16,9344]{1,0:T(8,128)(2,1)S(1)}, u32[]{:S(2)}, u32[]{:S(2)}) collective-permute-start(bf16[16,9344]{1,0:T(8,128)(2,1)S(1)} %half_far.1), channel_id=1, source_target_pairs={{0,1},{1,0},{2,3},{3,2},{4,5},{5,4},{6,7},{7,6},{8,9},{9,8},{10,11... | collective-permute-start | bytes 897032 | tf_op jit(solution)/shard_map/ppermute | solution.py:339
  19.8 0.0 collective-permute-done.2.near_o_ref.refs_3_
  19.9 0.1 collective-permute-start.3
  20.0 0.5 collective-permute-start.4
  20.5 0.6 collective-permute-done.6.refs_7_
  21.1 0.5 collective-permute-done.3.refs_4_
  21.6 0.4 collective-permute-done.4.refs_5_
  22.0 4.1 %project.1 = (bf16[256,2432]{1,0:T(8,128)(2,1)S(1)}, bf16[128,128]{1,0:T(8,128)(2,1)S(1)}) custom-call(bf16[16,10368]{1,0:T(8,128)(2,1)S(1)} %get-tuple-element.21.refs_0_, bf16[16,11392]{1,0:T(8,128)(2,1)S(1)} %collective-permute-done.other_ref.refs_1_, bf16[16,10368]{1,0:T(8,128)(2,1)S(1)} %collective-permute-done.1.near_ref.refs_2_, ...), custom_call_target="tpu_custom_call" | custom-call | flops 2684354560 | bytes 20971520 | tf_op jit(solution)/shard_map/project/pallas_call | solution.py:208
  26.0 0.0 copy-start.2
  26.1 26.3 %all_to_all.10 = bf16[16,16,2432]{2,1,0:T(8,128)(2,1)S(1)} all-to-all(bf16[16,16,2432]{2,1,0:T(8,128)(2,1)S(1)} %bitcast.11), channel_id=1, replica_groups=mesh['dp'=16,'tensor'=8] {'dp'}, dimensions={0} | all-to-all | bytes 2490368 | tf_op jit(solution)/shard_map/all_to_all | solution.py:415
  52.3 0.0 copy-done.2
  52.3 4.6 %attend.1 = bf16[256,1280]{1,0:T(8,128)(2,1)S(1)} custom-call(bf16[256,2432]{1,0:T(8,128)(2,1)S(1)} %bitcast.9, s32[1,16]{1,0:T(1,128)S(1)} %copy-done.2), custom_call_target="tpu_custom_call" | custom-call | tf_op jit(solution)/shard_map/attend/pallas_call | solution.py:420
  56.9 14.5 %all_to_all.11 = bf16[16,16,1280]{2,1,0:T(8,128)(2,1)S(1)} all-to-all(bf16[16,16,1280]{2,1,0:T(8,128)(2,1)S(1)} %bitcast.10), channel_id=1, replica_groups=mesh['dp'=16,'tensor'=8] {'dp'}, dimensions={0} | all-to-all | bytes 1310720 | tf_op jit(solution)/shard_map/all_to_all | solution.py:428
  71.4 3.0 %back.3 = (bf16[64,4096]{1,0:T(8,128)(2,1)S(1)}, bf16[64,4096]{1,0:T(8,128)(2,1)S(1)}) custom-call(bf16[128,128]{1,0:T(8,128)(2,1)S(1)} %get-tuple-element.31.ext_ref, bf16[256,1280]{1,0:T(8,128)(2,1)S(1)} %bitcast.7, bf16[4096,1280]{1,0:T(8,128)(2,1)S(1)} %get-tuple-element.29.refs_9_.w_ref), custom_call_target="tpu_custom_call" | custom-call | flops 1342177280 | bytes 10485760 | tf_op jit(solution)/shard_map/back/pallas_call | solution.py:299
  74.5 2.5 %collective-permute-start.12 = (bf16[64,4096]{1,0:T(8,128)(2,1)S(1)}, bf16[64,4096]{1,0:T(8,128)(2,1)S(1)}, u32[]{:S(2)}, u32[]{:S(2)}) collective-permute-start(bf16[64,4096]{1,0:T(8,128)(2,1)S(1)} %get-tuple-element.36), channel_id=1, source_target_pairs={{0,1},{1,0},{2,3},{3,2},{4,5},{5,4},{6,7},{7,6},{8,9},{9,8},{10,11... | collective-permute-start | bytes 1572872 | tf_op jit(solution)/shard_map/ppermute | solution.py:339
  77.0 3.0 %back.2 = (bf16[64,4096]{1,0:T(8,128)(2,1)S(1)}, bf16[64,4096]{1,0:T(8,128)(2,1)S(1)}) custom-call(bf16[128,128]{1,0:T(8,128)(2,1)S(1)} %get-tuple-element.31.ext_ref, bf16[256,1280]{1,0:T(8,128)(2,1)S(1)} %bitcast.8, bf16[4096,1280]{1,0:T(8,128)(2,1)S(1)} %get-tuple-element.28.refs_8_.w_ref), custom_call_target="tpu_custom_call" | custom-call | flops 1342177280 | bytes 10485760 | tf_op jit(solution)/shard_map/back/pallas_call | solution.py:299
  80.0 0.1 collective-permute-start.7
  80.1 0.0 collective-permute-done.12
  80.1 0.1 add_convert_fusion
  80.3 1.3 %collective-permute-start.13 = (bf16[16,4096]{1,0:T(8,128)(2,1)S(1)}, bf16[16,4096]{1,0:T(8,128)(2,1)S(1)}, u32[]{:S(2)}, u32[]{:S(2)}) collective-permute-start(bf16[16,4096]{1,0:T(8,128)(2,1)S(1)} %get-tuple-element.38), channel_id=1, source_target_pairs={{0,2},{1,7},{2,4},{3,1},{4,6},{5,3},{6,0},{7,5},{8,10},{9,15},{10,... | collective-permute-start | bytes 393224 | tf_op jit(solution)/shard_map/ppermute | solution.py:342
  81.6 0.5 collective-permute-done.7
  82.0 0.1 add_convert_fusion.1
  82.2 1.3 %collective-permute-start.8 = (bf16[16,4096]{1,0:T(8,128)(2,1)S(1)}, bf16[16,4096]{1,0:T(8,128)(2,1)S(1)}, u32[]{:S(2)}, u32[]{:S(2)}) collective-permute-start(bf16[16,4096]{1,0:T(8,128)(2,1)S(1)} %get-tuple-element.40), channel_id=1, source_target_pairs={{0,2},{1,7},{2,4},{3,1},{4,6},{5,3},{6,0},{7,5},{8,10},{9,15},{10,... | collective-permute-start | bytes 393224 | tf_op jit(solution)/shard_map/ppermute | solution.py:342
  83.5 0.2 collective-permute-start.10
  83.6 0.5 collective-permute-done.13
  84.2 2.5 %collective-permute-start.14 = (bf16[32,4096]{1,0:T(8,128)(2,1)S(1)}, bf16[32,4096]{1,0:T(8,128)(2,1)S(1)}, u32[]{:S(2)}, u32[]{:S(2)}) collective-permute-start(bf16[32,4096]{1,0:T(8,128)(2,1)S(1)} %pad_maximum_fusion), channel_id=1, source_target_pairs={{0,2},{1,7},{2,4},{3,1},{4,6},{5,3},{6,0},{7,5},{8,10},{9,15},{10,... | collective-permute-start | bytes 786440 | tf_op jit(solution)/shard_map/ppermute | solution.py:342
  86.7 0.0 collective-permute-done.8
  86.7 1.8 %collective-permute-start.9 = (bf16[16,4096]{1,0:T(8,128)(2,1)S(1)}, bf16[16,4096]{1,0:T(8,128)(2,1)S(1)}, u32[]{:S(2)}, u32[]{:S(2)}) collective-permute-start(bf16[16,4096]{1,0:T(8,128)(2,1)S(1)} %collective-permute-done.8), channel_id=1, source_target_pairs={{0,2},{1,7},{2,4},{3,1},{4,6},{5,3},{6,0},{7,5},{8,10},{9,15},{10,... | collective-permute-start | bytes 393224 | tf_op jit(solution)/shard_map/ppermute | solution.py:342
  88.5 0.7 collective-permute-done.10
  89.2 2.3 %collective-permute-start.11 = (bf16[16,4096]{1,0:T(8,128)(2,1)S(1)}, bf16[16,4096]{1,0:T(8,128)(2,1)S(1)}, u32[]{:S(2)}, u32[]{:S(2)}) collective-permute-start(bf16[16,4096]{1,0:T(8,128)(2,1)S(1)} %get-tuple-element.44), channel_id=1, source_target_pairs={{0,1},{1,0},{2,3},{3,2},{4,5},{5,4},{6,7},{7,6},{8,9},{9,8},{10,11... | collective-permute-start | bytes 393224 | tf_op jit(solution)/shard_map/ppermute | solution.py:339
  91.5 0.5 collective-permute-done.14
  92.0 2.8 %collective-permute-start.15 = (bf16[16,4096]{1,0:T(8,128)(2,1)S(1)}, bf16[16,4096]{1,0:T(8,128)(2,1)S(1)}, u32[]{:S(2)}, u32[]{:S(2)}) collective-permute-start(bf16[16,4096]{1,0:T(8,128)(2,1)S(1)} %get-tuple-element.42), channel_id=1, source_target_pairs={{0,1},{1,0},{2,3},{3,2},{4,5},{5,4},{6,7},{7,6},{8,9},{9,8},{10,11... | collective-permute-start | bytes 393224 | tf_op jit(solution)/shard_map/ppermute | solution.py:339
  94.8 0.0 collective-permute-done.9.refs_3_
  94.9 0.0 collective-permute-done.11.refs_5_
  94.9 1.0 %collective-permute-done.15.refs_8_ = bf16[16,4096]{1,0:T(8,128)(2,1)S(1)} collective-permute-done((bf16[16,4096]{1,0:T(8,128)(2,1)S(1)}, bf16[16,4096]{1,0:T(8,128)(2,1)S(1)}, u32[]{:S(2)}, u32[]{:S(2)}) %collective-permute-start.15) | collective-permute-done | bytes 131104 | tf_op jit(solution)/shard_map/ppermute | solution.py:339
  95.8 0.0 copy-done
  95.8 0.0 copy-done.1
  95.8 1.1 %finish.1 = bf16[16,8192]{1,0:T(8,128)(2,1)} custom-call(bf16[16,8192]{1,0:T(8,128)(2,1)S(1)} %copy-done, f32[1,8192]{1,0:T(1,128)S(1)} %bitcast.13, bf16[16,4096]{1,0:T(8,128)(2,1)S(1)} %get-tuple-element.41.refs_2_, bf16[16,4096]{1,0:T(8,128)(2,1)S(1)} %collective-permute-done.9.refs_3_, bf16[16,4096]{1,0:T(8,128)(2,1)S(1)} %get-tuple-element.45.refs_4_, ...), custom_call_target="tpu_custom_call" | custom-call | tf_op jit(solution)/shard_map/finish/pallas_call | solution.py:451
  (13 shorter events, 0.3 us)
Async XLA Ops:
  1.4 4.3 %collective-permute-start = (bf16[16,11392]{1,0:T(8,128)(2,1)S(1)}, bf16[16,11392]{1,0:T(8,128)(2,1)S(1)}, u32[]{:S(2)}, u32[]{:S(2)}) collective-permute-start(bf16[16,11392]{1,0:T(8,128)(2,1)S(1)} %get-tuple-element.22), channel_id=1, source_target_pairs={{0,1},{1,0},{2,3},{3,2},{4,5},{5,4},{6,7},{7,6},{8,9},{9,8},{10,11... | collective-permute-start | bytes 1093640 | tf_op jit(solution)/shard_map/ppermute | solution.py:339
  2.9 8.3 %collective-permute-start.1 = (bf16[16,10368]{1,0:T(8,128)(2,1)S(1)}, bf16[16,10368]{1,0:T(8,128)(2,1)S(1)}, u32[]{:S(2)}, u32[]{:S(2)}) collective-permute-start(bf16[16,10368]{1,0:T(8,128)(2,1)S(1)} %get-tuple-element.21.refs_0_), channel_id=1, source_target_pairs={{0,2},{1,7},{2,4},{3,1},{4,6},{5,3},{6,0},{7,5},{8,10},{9,15},{10,... | collective-permute-start | bytes 995336 | tf_op jit(solution)/shard_map/ppermute | solution.py:342
  5.7 14.1 %collective-permute-start.2 = (bf16[16,12416]{1,0:T(8,128)(2,1)S(1)}, bf16[16,12416]{1,0:T(8,128)(2,1)S(1)}, u32[]{:S(2)}, u32[]{:S(2)}) collective-permute-start(bf16[16,12416]{1,0:T(8,128)(2,1)S(1)} %join.1.refs_3_), channel_id=1, source_target_pairs={{0,2},{1,7},{2,4},{3,1},{4,6},{5,3},{6,0},{7,5},{8,10},{9,15},{10,... | collective-permute-start | bytes 1191944 | tf_op jit(solution)/shard_map/ppermute | solution.py:342
  11.2 6.4 %collective-permute-start.5 = (bf16[16,10368]{1,0:T(8,128)(2,1)S(1)}, bf16[16,10368]{1,0:T(8,128)(2,1)S(1)}, u32[]{:S(2)}, u32[]{:S(2)}) collective-permute-start(bf16[16,10368]{1,0:T(8,128)(2,1)S(1)} %relay.1.refs_3_), channel_id=1, source_target_pairs={{0,2},{1,7},{2,4},{3,1},{4,6},{5,3},{6,0},{7,5},{8,10},{9,15},{10,... | collective-permute-start | bytes 995336 | tf_op jit(solution)/shard_map/ppermute | solution.py:342
  17.6 3.4 %collective-permute-start.6 = (bf16[16,9344]{1,0:T(8,128)(2,1)S(1)}, bf16[16,9344]{1,0:T(8,128)(2,1)S(1)}, u32[]{:S(2)}, u32[]{:S(2)}) collective-permute-start(bf16[16,9344]{1,0:T(8,128)(2,1)S(1)} %half_far.1), channel_id=1, source_target_pairs={{0,1},{1,0},{2,3},{3,2},{4,5},{5,4},{6,7},{7,6},{8,9},{9,8},{10,11... | collective-permute-start | bytes 897032 | tf_op jit(solution)/shard_map/ppermute | solution.py:339
  19.9 1.7 %collective-permute-start.3 = (bf16[16,9344]{1,0:T(8,128)(2,1)S(1)}, bf16[16,9344]{1,0:T(8,128)(2,1)S(1)}, u32[]{:S(2)}, u32[]{:S(2)}) collective-permute-start(bf16[16,9344]{1,0:T(8,128)(2,1)S(1)} %get-tuple-element.26), channel_id=1, source_target_pairs={{0,1},{1,0},{2,3},{3,2},{4,5},{5,4},{6,7},{7,6},{8,9},{9,8},{10,11... | collective-permute-start | bytes 897032 | tf_op jit(solution)/shard_map/ppermute | solution.py:339
  20.0 2.0 %collective-permute-start.4 = (bf16[16,9344]{1,0:T(8,128)(2,1)S(1)}, bf16[16,9344]{1,0:T(8,128)(2,1)S(1)}, u32[]{:S(2)}, u32[]{:S(2)}) collective-permute-start(bf16[16,9344]{1,0:T(8,128)(2,1)S(1)} %get-tuple-element.27), channel_id=1, source_target_pairs={{0,1},{1,0},{2,3},{3,2},{4,5},{5,4},{6,7},{7,6},{8,9},{9,8},{10,11... | collective-permute-start | bytes 897032 | tf_op jit(solution)/shard_map/ppermute | solution.py:339
  26.0 26.3 %copy-start.2 = (s32[1,16]{1,0:T(1,128)S(1)}, s32[1,16]{1,0:T(1,128)}, u32[]{:S(2)}) copy-start(s32[1,16]{1,0:T(1,128)} %rewards_ref.1) | copy-start | bytes 196
  74.5 5.7 %collective-permute-start.12 = (bf16[64,4096]{1,0:T(8,128)(2,1)S(1)}, bf16[64,4096]{1,0:T(8,128)(2,1)S(1)}, u32[]{:S(2)}, u32[]{:S(2)}) collective-permute-start(bf16[64,4096]{1,0:T(8,128)(2,1)S(1)} %get-tuple-element.36), channel_id=1, source_target_pairs={{0,1},{1,0},{2,3},{3,2},{4,5},{5,4},{6,7},{7,6},{8,9},{9,8},{10,11... | collective-permute-start | bytes 1572872 | tf_op jit(solution)/shard_map/ppermute | solution.py:339
  80.0 2.0 %collective-permute-start.7 = (bf16[64,4096]{1,0:T(8,128)(2,1)S(1)}, bf16[64,4096]{1,0:T(8,128)(2,1)S(1)}, u32[]{:S(2)}, u32[]{:S(2)}) collective-permute-start(bf16[64,4096]{1,0:T(8,128)(2,1)S(1)} %get-tuple-element.34), channel_id=1, source_target_pairs={{0,1},{1,0},{2,3},{3,2},{4,5},{5,4},{6,7},{7,6},{8,9},{9,8},{10,11... | collective-permute-start | bytes 1572872 | tf_op jit(solution)/shard_map/ppermute | solution.py:339
  80.3 3.9 %collective-permute-start.13 = (bf16[16,4096]{1,0:T(8,128)(2,1)S(1)}, bf16[16,4096]{1,0:T(8,128)(2,1)S(1)}, u32[]{:S(2)}, u32[]{:S(2)}) collective-permute-start(bf16[16,4096]{1,0:T(8,128)(2,1)S(1)} %get-tuple-element.38), channel_id=1, source_target_pairs={{0,2},{1,7},{2,4},{3,1},{4,6},{5,3},{6,0},{7,5},{8,10},{9,15},{10,... | collective-permute-start | bytes 393224 | tf_op jit(solution)/shard_map/ppermute | solution.py:342
  82.0 13.8 %copy-start = (bf16[16,8192]{1,0:T(8,128)(2,1)S(1)}, bf16[16,8192]{1,0:T(8,128)(2,1)}, u32[]{:S(2)}) copy-start(bf16[16,8192]{1,0:T(8,128)(2,1)} %refs_0_.5) | copy-start | bytes 786436
  82.0 13.8 %copy-start.1 = (f32[8192]{0:T(1024)S(1)}, f32[8192]{0:T(1024)}, u32[]{:S(2)}) copy-start(f32[8192]{0:T(1024)} %param.10) | copy-start | bytes 98308
  82.2 4.5 %collective-permute-start.8 = (bf16[16,4096]{1,0:T(8,128)(2,1)S(1)}, bf16[16,4096]{1,0:T(8,128)(2,1)S(1)}, u32[]{:S(2)}, u32[]{:S(2)}) collective-permute-start(bf16[16,4096]{1,0:T(8,128)(2,1)S(1)} %get-tuple-element.40), channel_id=1, source_target_pairs={{0,2},{1,7},{2,4},{3,1},{4,6},{5,3},{6,0},{7,5},{8,10},{9,15},{10,... | collective-permute-start | bytes 393224 | tf_op jit(solution)/shard_map/ppermute | solution.py:342
  83.5 5.7 %collective-permute-start.10 = (bf16[32,4096]{1,0:T(8,128)(2,1)S(1)}, bf16[32,4096]{1,0:T(8,128)(2,1)S(1)}, u32[]{:S(2)}, u32[]{:S(2)}) collective-permute-start(bf16[32,4096]{1,0:T(8,128)(2,1)S(1)} %slice.49), channel_id=1, source_target_pairs={{0,2},{1,7},{2,4},{3,1},{4,6},{5,3},{6,0},{7,5},{8,10},{9,15},{10,... | collective-permute-start | bytes 786440 | tf_op jit(solution)/shard_map/ppermute | solution.py:342
  84.2 7.8 %collective-permute-start.14 = (bf16[32,4096]{1,0:T(8,128)(2,1)S(1)}, bf16[32,4096]{1,0:T(8,128)(2,1)S(1)}, u32[]{:S(2)}, u32[]{:S(2)}) collective-permute-start(bf16[32,4096]{1,0:T(8,128)(2,1)S(1)} %pad_maximum_fusion), channel_id=1, source_target_pairs={{0,2},{1,7},{2,4},{3,1},{4,6},{5,3},{6,0},{7,5},{8,10},{9,15},{10,... | collective-permute-start | bytes 786440 | tf_op jit(solution)/shard_map/ppermute | solution.py:342
  86.7 8.1 %collective-permute-start.9 = (bf16[16,4096]{1,0:T(8,128)(2,1)S(1)}, bf16[16,4096]{1,0:T(8,128)(2,1)S(1)}, u32[]{:S(2)}, u32[]{:S(2)}) collective-permute-start(bf16[16,4096]{1,0:T(8,128)(2,1)S(1)} %collective-permute-done.8), channel_id=1, source_target_pairs={{0,2},{1,7},{2,4},{3,1},{4,6},{5,3},{6,0},{7,5},{8,10},{9,15},{10,... | collective-permute-start | bytes 393224 | tf_op jit(solution)/shard_map/ppermute | solution.py:342
  89.2 5.6 %collective-permute-start.11 = (bf16[16,4096]{1,0:T(8,128)(2,1)S(1)}, bf16[16,4096]{1,0:T(8,128)(2,1)S(1)}, u32[]{:S(2)}, u32[]{:S(2)}) collective-permute-start(bf16[16,4096]{1,0:T(8,128)(2,1)S(1)} %get-tuple-element.44), channel_id=1, source_target_pairs={{0,1},{1,0},{2,3},{3,2},{4,5},{5,4},{6,7},{7,6},{8,9},{9,8},{10,11... | collective-permute-start | bytes 393224 | tf_op jit(solution)/shard_map/ppermute | solution.py:339
  92.0 3.8 %collective-permute-start.15 = (bf16[16,4096]{1,0:T(8,128)(2,1)S(1)}, bf16[16,4096]{1,0:T(8,128)(2,1)S(1)}, u32[]{:S(2)}, u32[]{:S(2)}) collective-permute-start(bf16[16,4096]{1,0:T(8,128)(2,1)S(1)} %get-tuple-element.42), channel_id=1, source_target_pairs={{0,1},{1,0},{2,3},{3,2},{4,5},{5,4},{6,7},{7,6},{8,9},{9,8},{10,11... | collective-permute-start | bytes 393224 | tf_op jit(solution)/shard_map/ppermute | solution.py:339

commit v5 on v4

--- a/solution.py
+++ b/solution.py
@@ -12,6 +12,7 @@
 HEADS_AT = 8192 + EXT
 STEP = 1024
 PIECES = 4
+TURN = 512
 EPSILON = 1e-05
 BASE = 500000.0
 F32 = jnp.float32
@@ -22,7 +23,7 @@
 ANY = pl.BlockSpec(memory_space=pl.ANY)
 
 
-def params(mib=12):
+def params(mib=8):
     return pltpu.CompilerParams(vmem_limit_bytes=mib * 2**20)
 
 
@@ -127,15 +128,16 @@
     out_ref[...] = near_ref[...]
 
 
-def load_kernel(part, wq_hbm, wk_hbm, wv_hbm, _, out_ref, token_ref, sems):
+def load_kernel(part, wq_hbm, wk_hbm, wv_hbm, _, out_ref, token_ref, *rest):
+    turned_ref, sems = rest[0], rest[-1]
     token_ref[...] = jnp.zeros_like(token_ref)
     span = out_ref.shape[0]
     step = span // PIECES
     copies = []
-    at = 0
-    for w in (wq_hbm, wk_hbm, wv_hbm):
-        n = w.shape[1]
-        for j in range(PIECES):
+    for j in range(PIECES):
+        at = 0
+        for w in (wq_hbm, wk_hbm, wv_hbm):
+            n = w.shape[1]
             copies.append(
                 pltpu.make_async_copy(
                     w.at[pl.ds(part * span + j * step, step), :],
@@ -143,11 +145,19 @@
                     sems.at[len(copies)],
                 )
             )
-        at += n
+            at += n
     for copy in copies:
         copy.start()
-    for copy in copies:
-        copy.wait()
+    for j in range(PIECES):
+        for copy in copies[3 * j : 3 * j + 3]:
+            copy.wait()
+        if part == 0:
+            continue
+
+        @pl.loop(0, step // TURN)
+        def _(k):
+            at = pl.ds(pl.multiple_of(j * step + k * TURN, TURN), TURN)
+            turned_ref[:, at] = jnp.transpose(out_ref[at, :])
 
 
 def load(part, weights, after):
@@ -156,8 +166,8 @@
     return pl.pallas_call(
         lambda *refs: load_kernel(part, *refs),
         in_specs=[ANY] * 3 + [VMEM],
-        out_specs=[VMEM] * 2,
-        out_shape=[pltpu.VMEM((span, cols), BF16), TOKEN],
+        out_specs=[VMEM] * (2 + (part > 0)),
+        out_shape=[pltpu.VMEM((span, cols), BF16), TOKEN] + [pltpu.VMEM((cols, span), BF16)] * (part > 0),
         scratch_shapes=[pltpu.SemaphoreType.DMA((3 * PIECES,))],
         compiler_params=params(),
         cost_estimate=pl.CostEstimate(flops=0, bytes_accessed=2 * span * cols, transcendentals=0),
@@ -185,9 +195,10 @@
     cols = total.shape[1]
     slots = out_ref.shape[0]
     ext = jnp.concatenate(exts, axis=0)
-    spread = (ext[:, 0:1].astype(F32) == iota((ext.shape[0], slots), 1).astype(F32)).astype(BF16)
-    out_ref[:, 0:cols] = dot(spread, total, ((0,), (0,))).astype(BF16)
-    out_ref[:, cols : cols + EXT] = dot(spread, ext, ((0,), (0,))).astype(BF16)
+    place = jnp.transpose(ext.astype(F32))[0:1, :]
+    spread = (place == iota((slots, ext.shape[0]), 0).astype(F32)).astype(BF16)
+    out_ref[:, 0:cols] = dot(spread, total, ((1,), (0,))).astype(BF16)
+    out_ref[:, cols : cols + EXT] = dot(spread, ext, ((1,), (0,))).astype(BF16)
     _, core, _ = chip_and_core()
     n = HEADS_AT
     each = own_ref.shape[1]
@@ -198,7 +209,7 @@
     mine, other, near, near_o, across, across_o, far, far_o = blocks
     grads = [own_ref[...], other[:, n + 2 * each :], heads(near_o, n + 2 * each), heads(near_o, n)]
     grads += [across[:, n:], across_o[:, n:], heads(far, n), far_o[:, n:]]
-    out_ref[:, cols + EXT :] = dot(spread, jnp.concatenate(grads, axis=0), ((0,), (0,))).astype(BF16)
+    out_ref[:, cols + EXT :] = dot(spread, jnp.concatenate(grads, axis=0), ((1,), (0,))).astype(BF16)
 
 
 def project(blocks, loaded, own, slots):
@@ -280,24 +291,27 @@
     out_ref[:, vcol : vcol + HD] = grad_value.astype(BF16)
 
 
-def back_kernel(ext_ref, slots_ref, w_ref, keep_ref, send_ref):
+def back_kernel(is_turned, ext_ref, slots_ref, w_ref, keep_ref, send_ref):
     half_rows, span = keep_ref.shape
     slots = slots_ref.shape[0]
     hot = (ext_ref[:, 0:1].astype(F32) == iota((ext_ref.shape[0], slots), 1).astype(F32)).astype(BF16)
     held = dot(hot, slots_ref[...], ((1,), (0,))).astype(BF16)
     for j in range(span // STEP):
         at = slice(j * STEP, (j + 1) * STEP)
-        term = dot(held, w_ref[at, :], ((1,), (1,))).astype(BF16)
+        if is_turned:
+            term = dot(held, w_ref[:, at], ((1,), (0,))).astype(BF16)
+        else:
+            term = dot(held, w_ref[at, :], ((1,), (1,))).astype(BF16)
         keep_ref[:, at] = term[0:half_rows]
         send_ref[:, at] = term[half_rows:]
 
 
-def back(ext, slot_grads, w):
+def back(ext, slot_grads, w, is_turned):
     rows = ext.shape[0]
-    span, cols = w.shape
+    cols, span = w.shape if is_turned else w.shape[::-1]
     out = jax.ShapeDtypeStruct((rows // 2, span), BF16)
     return pl.pallas_call(
-        back_kernel,
+        lambda *refs: back_kernel(is_turned, *refs),
         in_specs=[VMEM] * 3,
         out_specs=[VMEM] * 2,
         out_shape=[out, out],
@@ -390,7 +404,7 @@
         name="relay",
     )(near, ready)
     far = flow(passed)
-    second, ready_too = load(1, weights, passed)
+    second, ready_too, turned = load(1, weights, passed)
 
     half_rows = rows_of(HEADS_AT + query_cols)
     half_near, half_near_o = pl.pallas_call(
@@ -434,7 +448,7 @@
 
     pieces = []
     for i in range(PARTS):
-        keep, send = back(ext, slot_grads, loaded[i])
+        keep, send = back(ext, slot_grads, first if i == 0 else turned, i > 0)
         both = add(keep, swap(send))
         mine, onward = both[:count], both[count : 3 * count]
         passed = flow(both[3 * count :])

time: 97.2 us -> 95.8 us (0.986)
    pallas_call x2, Pallas kernels: 6.04 us -> 4.72 us  [back(): pl.pallas_call(lambda *refs: back_kernel(is_turned, *refs), in_specs=[VME...]
    pallas_call x2, Pallas kernels: 8.08 us -> 9.21 us  [load(): pl.pallas_call(lambda *refs: load_kernel(part, *refs), in_specs=[ANY] * 3...]
  transfers between devices with their start and end apart: 16 -> 16, of which waited for: 9 -> 8; matrix products, arithmetic and copies ran while one was open for 0% -> 0% of each run, Pallas kernels for 12% -> 13%
where the time goes in v5:
time: 95.8 us; the launch traced here: 95.7 us
  blocking collectives  40.8 us (43%)
  Pallas kernels  25.1 us (26%)
  starting transfers between devices  24.4 us (25%)
  waiting for transfers between devices  4.7 us (5%)
    all_to_all x1, blocking collectives, on_device(): lax.all_to_all(total.reshape(groups, 2 * ranks, total.shape[1]), 'dp', sp...  26.3 us
    all_to_all x1, blocking collectives, on_device(): lax.all_to_all(grads.reshape(groups, 2 * ranks, cols), 'dp', split_axis=0...  14.5 us
    ppermute x8, starting transfers between devices, flow(): return lax.ppermute(x, 'tensor', flow_pairs)  12.9 us
    ppermute x8, starting transfers between devices, swap(): return lax.ppermute(x, 'tensor', swap_pairs)  11.5 us
    pallas_call x2, Pallas kernels, load(): pl.pallas_call(lambda *refs: load_kernel(part, *refs), in_specs=[ANY] * 3...  9.21 us
    pallas_call x2, Pallas kernels, back(): pl.pallas_call(lambda *refs: back_kernel(is_turned, *refs), in_specs=[VME...  4.72 us
    pallas_call x1, Pallas kernels, on_device(): pl.pallas_call(attend_kernel, in_specs=[VMEM] * 2, out_specs=VMEM, out_sh...  4.55 us
    pallas_call x1, Pallas kernels, project(): pl.pallas_call(lambda *refs: project_kernel(len(blocks), *refs), in_specs...  4 us
  transfers between devices with their start and end apart: 16, of which 8 were waited for; matrix products, arithmetic and copies ran while one was open for 0% of the time, Pallas kernels for 13%

profile of v5, /device:TPU:1, one launch (start us, length us, event | category | flops | bytes accessed | tf_op | source)
XLA Modules:
  0.0 95.7 jit_solution(10758767116106558743)
XLA Ops:
  0.0 1.4 %norm.1 = (bf16[16,10368]{1,0:T(8,128)(2,1)S(1)}, bf16[16,11392]{1,0:T(8,128)(2,1)S(1)}, bf16[16,2048]{1,0:T(8,128)(2,1)S(1)}, bf16[16,1024]{1,0:T(8,128)(2,1)S(1)}) custom-call(bf16[16,8192]{1,0:T(8,128)(2,1)} %refs_0_.5, f32[1,8192]{1,0:T(1,128)} %bitcast.12, s32[1,16]{1,0:T(1,128)} %bitcast.14, s32[1,16]{1,0:T(1,128)} %bitcast.15, bf16[16,8192]{1,0:T(8,128)(2,1)} %grad_hbm.1), custom_call_target="tpu_custom_call" | custom-call | tf_op jit(solution)/shard_map/norm/pallas_call | solution.py:363
  1.4 1.5 %collective-permute-start = (bf16[16,11392]{1,0:T(8,128)(2,1)S(1)}, bf16[16,11392]{1,0:T(8,128)(2,1)S(1)}, u32[]{:S(2)}, u32[]{:S(2)}) collective-permute-start(bf16[16,11392]{1,0:T(8,128)(2,1)S(1)} %get-tuple-element.23), channel_id=1, source_target_pairs={{0,1},{1,0},{2,3},{3,2},{4,5},{5,4},{6,7},{7,6},{8,9},{9,8},{10,11... | collective-permute-start | bytes 1093640 | tf_op jit(solution)/shard_map/ppermute | solution.py:353
  2.9 2.8 %collective-permute-start.1 = (bf16[16,10368]{1,0:T(8,128)(2,1)S(1)}, bf16[16,10368]{1,0:T(8,128)(2,1)S(1)}, u32[]{:S(2)}, u32[]{:S(2)}) collective-permute-start(bf16[16,10368]{1,0:T(8,128)(2,1)S(1)} %get-tuple-element.22.refs_0_), channel_id=1, source_target_pairs={{0,2},{1,7},{2,4},{3,1},{4,6},{5,3},{6,0},{7,5},{8,10},{9,15},{10,... | collective-permute-start | bytes 995336 | tf_op jit(solution)/shard_map/ppermute | solution.py:356
  5.7 0.0 collective-permute-done.other_ref.refs_1_
  5.7 1.4 %collective-permute-start.2 = (bf16[16,12416]{1,0:T(8,128)(2,1)S(1)}, bf16[16,12416]{1,0:T(8,128)(2,1)S(1)}, u32[]{:S(2)}, u32[]{:S(2)}) collective-permute-start(bf16[16,12416]{1,0:T(8,128)(2,1)S(1)} %join.1.refs_3_), channel_id=1, source_target_pairs={{0,2},{1,7},{2,4},{3,1},{4,6},{5,3},{6,0},{7,5},{8,10},{9,15},{10,... | collective-permute-start | bytes 1191944 | tf_op jit(solution)/shard_map/ppermute | solution.py:356
  7.1 4.0 %load.2 = (bf16[4096,1280]{1,0:T(8,128)(2,1)S(1)}, f32[8,128]{1,0:T(8,128)S(1)}) custom-call(bf16[8192,1024]{1,0:T(8,128)(2,1)} %refs_0_.4, bf16[8192,128]{1,0:T(8,128)(2,1)} %refs_1_.3, bf16[8192,128]{1,0:T(8,128)(2,1)} %refs_2_.3, bf16[16,12416]{1,0:T(8,128)(2,1)S(1)} %join.1.refs_3_), custom_call_target="tpu_custom_call" | custom-call | bytes 10485760 | tf_op jit(solution)/shard_map/load/pallas_call | solution.py:166
  11.2 0.0 collective-permute-done.1.near_ref.refs_2_
  11.2 1.8 %collective-permute-start.5 = (bf16[16,10368]{1,0:T(8,128)(2,1)S(1)}, bf16[16,10368]{1,0:T(8,128)(2,1)S(1)}, u32[]{:S(2)}, u32[]{:S(2)}) collective-permute-start(bf16[16,10368]{1,0:T(8,128)(2,1)S(1)} %relay.1.refs_3_), channel_id=1, source_target_pairs={{0,2},{1,7},{2,4},{3,1},{4,6},{5,3},{6,0},{7,5},{8,10},{9,15},{10,... | collective-permute-start | bytes 995336 | tf_op jit(solution)/shard_map/ppermute | solution.py:356
  13.0 5.2 %load.3 = (bf16[4096,1280]{1,0:T(8,128)(2,1)S(1)}, f32[8,128]{1,0:T(8,128)S(1)}, bf16[1280,4096]{1,0:T(8,128)(2,1)S(1)}) custom-call(bf16[8192,1024]{1,0:T(8,128)(2,1)} %refs_0_.4, bf16[8192,128]{1,0:T(8,128)(2,1)} %refs_1_.3, bf16[8192,128]{1,0:T(8,128)(2,1)} %refs_2_.3, bf16[16,10368]{1,0:T(8,128)(2,1)S(1)} %relay.1.refs_3_), custom_call_target="tpu_custom_call" | custom-call | bytes 10485760 | tf_op jit(solution)/shard_map/load/pallas_call | solution.py:166
  18.2 0.0 collective-permute-done.5.far_ref.refs_6_
  18.2 1.6 %collective-permute-start.6 = (bf16[16,9344]{1,0:T(8,128)(2,1)S(1)}, bf16[16,9344]{1,0:T(8,128)(2,1)S(1)}, u32[]{:S(2)}, u32[]{:S(2)}) collective-permute-start(bf16[16,9344]{1,0:T(8,128)(2,1)S(1)} %half_far.1), channel_id=1, source_target_pairs={{0,1},{1,0},{2,3},{3,2},{4,5},{5,4},{6,7},{7,6},{8,9},{9,8},{10,11... | collective-permute-start | bytes 897032 | tf_op jit(solution)/shard_map/ppermute | solution.py:353
  19.8 0.0 collective-permute-done.2.near_o_ref.refs_3_
  19.9 0.1 collective-permute-start.3
  20.0 0.5 collective-permute-start.4
  20.5 0.6 collective-permute-done.6.refs_7_
  21.1 0.5 collective-permute-done.3.refs_4_
  21.6 0.4 collective-permute-done.4.refs_5_
  22.0 4.0 %project.1 = (bf16[256,2432]{1,0:T(8,128)(2,1)S(1)}, bf16[128,128]{1,0:T(8,128)(2,1)S(1)}) custom-call(bf16[16,10368]{1,0:T(8,128)(2,1)S(1)} %get-tuple-element.22.refs_0_, bf16[16,11392]{1,0:T(8,128)(2,1)S(1)} %collective-permute-done.other_ref.refs_1_, bf16[16,10368]{1,0:T(8,128)(2,1)S(1)} %collective-permute-done.1.near_ref.refs_2_, ...), custom_call_target="tpu_custom_call" | custom-call | flops 2684354560 | bytes 20971520 | tf_op jit(solution)/shard_map/project/pallas_call | solution.py:219
  26.0 26.3 %all_to_all.10 = bf16[16,16,2432]{2,1,0:T(8,128)(2,1)S(1)} all-to-all(bf16[16,16,2432]{2,1,0:T(8,128)(2,1)S(1)} %bitcast.11), channel_id=1, replica_groups=mesh['dp'=16,'tensor'=8] {'dp'}, dimensions={0} | all-to-all | bytes 2490368 | tf_op jit(solution)/shard_map/all_to_all | solution.py:429
  52.3 0.0 copy-done.2
  52.3 4.6 %attend.1 = bf16[256,1280]{1,0:T(8,128)(2,1)S(1)} custom-call(bf16[256,2432]{1,0:T(8,128)(2,1)S(1)} %bitcast.9, s32[1,16]{1,0:T(1,128)S(1)} %copy-done.2), custom_call_target="tpu_custom_call" | custom-call | tf_op jit(solution)/shard_map/attend/pallas_call | solution.py:434
  56.9 14.5 %all_to_all.11 = bf16[16,16,1280]{2,1,0:T(8,128)(2,1)S(1)} all-to-all(bf16[16,16,1280]{2,1,0:T(8,128)(2,1)S(1)} %bitcast.10), channel_id=1, replica_groups=mesh['dp'=16,'tensor'=8] {'dp'}, dimensions={0} | all-to-all | bytes 1310720 | tf_op jit(solution)/shard_map/all_to_all | solution.py:442
  71.4 1.7 %back.3 = (bf16[64,4096]{1,0:T(8,128)(2,1)S(1)}, bf16[64,4096]{1,0:T(8,128)(2,1)S(1)}) custom-call(bf16[128,128]{1,0:T(8,128)(2,1)S(1)} %get-tuple-element.32.refs_0_, bf16[256,1280]{1,0:T(8,128)(2,1)S(1)} %bitcast.7, bf16[1280,4096]{1,0:T(8,128)(2,1)S(1)} %get-tuple-element.36.refs_2_), custom_call_target="tpu_custom_call" | custom-call | flops 1342177280 | bytes 10485760 | tf_op jit(solution)/shard_map/back/pallas_call | solution.py:313
  73.1 0.0 copy-start
  73.1 0.0 copy-start.1
  73.1 2.5 %collective-permute-start.12 = (bf16[64,4096]{1,0:T(8,128)(2,1)S(1)}, bf16[64,4096]{1,0:T(8,128)(2,1)S(1)}, u32[]{:S(2)}, u32[]{:S(2)}) collective-permute-start(bf16[64,4096]{1,0:T(8,128)(2,1)S(1)} %get-tuple-element.38), channel_id=1, source_target_pairs={{0,1},{1,0},{2,3},{3,2},{4,5},{5,4},{6,7},{7,6},{8,9},{9,8},{10,11... | collective-permute-start | bytes 1572872 | tf_op jit(solution)/shard_map/ppermute | solution.py:353
  75.7 3.0 %back.2 = (bf16[64,4096]{1,0:T(8,128)(2,1)S(1)}, bf16[64,4096]{1,0:T(8,128)(2,1)S(1)}) custom-call(bf16[128,128]{1,0:T(8,128)(2,1)S(1)} %get-tuple-element.32.refs_0_, bf16[256,1280]{1,0:T(8,128)(2,1)S(1)} %bitcast.8, bf16[4096,1280]{1,0:T(8,128)(2,1)S(1)} %get-tuple-element.29.refs_8_.refs_2_), custom_call_target="tpu_custom_call" | custom-call | flops 1342177280 | bytes 10485760 | tf_op jit(solution)/shard_map/back/pallas_call | solution.py:313
  78.7 0.1 collective-permute-start.7
  78.8 0.0 collective-permute-done.12
  78.8 0.1 add_convert_fusion
  78.9 1.3 %collective-permute-start.13 = (bf16[16,4096]{1,0:T(8,128)(2,1)S(1)}, bf16[16,4096]{1,0:T(8,128)(2,1)S(1)}, u32[]{:S(2)}, u32[]{:S(2)}) collective-permute-start(bf16[16,4096]{1,0:T(8,128)(2,1)S(1)} %get-tuple-element.40), channel_id=1, source_target_pairs={{0,2},{1,7},{2,4},{3,1},{4,6},{5,3},{6,0},{7,5},{8,10},{9,15},{10,... | collective-permute-start | bytes 393224 | tf_op jit(solution)/shard_map/ppermute | solution.py:356
  80.2 0.5 collective-permute-done.7
  80.7 0.1 add_convert_fusion.1
  80.8 1.3 %collective-permute-start.8 = (bf16[16,4096]{1,0:T(8,128)(2,1)S(1)}, bf16[16,4096]{1,0:T(8,128)(2,1)S(1)}, u32[]{:S(2)}, u32[]{:S(2)}) collective-permute-start(bf16[16,4096]{1,0:T(8,128)(2,1)S(1)} %get-tuple-element.42), channel_id=1, source_target_pairs={{0,2},{1,7},{2,4},{3,1},{4,6},{5,3},{6,0},{7,5},{8,10},{9,15},{10,... | collective-permute-start | bytes 393224 | tf_op jit(solution)/shard_map/ppermute | solution.py:356
  82.1 0.2 collective-permute-start.10
  82.3 0.5 collective-permute-done.13
  82.9 2.5 %collective-permute-start.14 = (bf16[32,4096]{1,0:T(8,128)(2,1)S(1)}, bf16[32,4096]{1,0:T(8,128)(2,1)S(1)}, u32[]{:S(2)}, u32[]{:S(2)}) collective-permute-start(bf16[32,4096]{1,0:T(8,128)(2,1)S(1)} %pad_maximum_fusion), channel_id=1, source_target_pairs={{0,2},{1,7},{2,4},{3,1},{4,6},{5,3},{6,0},{7,5},{8,10},{9,15},{10,... | collective-permute-start | bytes 786440 | tf_op jit(solution)/shard_map/ppermute | solution.py:356
  85.4 0.0 collective-permute-done.8
  85.4 1.8 %collective-permute-start.9 = (bf16[16,4096]{1,0:T(8,128)(2,1)S(1)}, bf16[16,4096]{1,0:T(8,128)(2,1)S(1)}, u32[]{:S(2)}, u32[]{:S(2)}) collective-permute-start(bf16[16,4096]{1,0:T(8,128)(2,1)S(1)} %collective-permute-done.8), channel_id=1, source_target_pairs={{0,2},{1,7},{2,4},{3,1},{4,6},{5,3},{6,0},{7,5},{8,10},{9,15},{10,... | collective-permute-start | bytes 393224 | tf_op jit(solution)/shard_map/ppermute | solution.py:356
  87.1 0.7 collective-permute-done.10
  87.9 2.3 %collective-permute-start.11 = (bf16[16,4096]{1,0:T(8,128)(2,1)S(1)}, bf16[16,4096]{1,0:T(8,128)(2,1)S(1)}, u32[]{:S(2)}, u32[]{:S(2)}) collective-permute-start(bf16[16,4096]{1,0:T(8,128)(2,1)S(1)} %get-tuple-element.46), channel_id=1, source_target_pairs={{0,1},{1,0},{2,3},{3,2},{4,5},{5,4},{6,7},{7,6},{8,9},{9,8},{10,11... | collective-permute-start | bytes 393224 | tf_op jit(solution)/shard_map/ppermute | solution.py:353
  90.1 0.5 collective-permute-done.14
  90.7 2.8 %collective-permute-start.15 = (bf16[16,4096]{1,0:T(8,128)(2,1)S(1)}, bf16[16,4096]{1,0:T(8,128)(2,1)S(1)}, u32[]{:S(2)}, u32[]{:S(2)}) collective-permute-start(bf16[16,4096]{1,0:T(8,128)(2,1)S(1)} %get-tuple-element.44), channel_id=1, source_target_pairs={{0,1},{1,0},{2,3},{3,2},{4,5},{5,4},{6,7},{7,6},{8,9},{9,8},{10,11... | collective-permute-start | bytes 393224 | tf_op jit(solution)/shard_map/ppermute | solution.py:353
  93.5 0.0 collective-permute-done.9.refs_3_
  93.5 0.0 collective-permute-done.11.refs_5_
  93.5 1.0 %collective-permute-done.15.refs_8_ = bf16[16,4096]{1,0:T(8,128)(2,1)S(1)} collective-permute-done((bf16[16,4096]{1,0:T(8,128)(2,1)S(1)}, bf16[16,4096]{1,0:T(8,128)(2,1)S(1)}, u32[]{:S(2)}, u32[]{:S(2)}) %collective-permute-start.15) | collective-permute-done | bytes 131104 | tf_op jit(solution)/shard_map/ppermute | solution.py:353
  94.5 0.0 copy-done.1
  94.5 1.2 %finish.1 = bf16[16,8192]{1,0:T(8,128)(2,1)} custom-call(bf16[16,8192]{1,0:T(8,128)(2,1)S(1)} %copy-done, f32[1,8192]{1,0:T(1,128)S(1)} %bitcast.13, bf16[16,4096]{1,0:T(8,128)(2,1)S(1)} %get-tuple-element.43.refs_2_, bf16[16,4096]{1,0:T(8,128)(2,1)S(1)} %collective-permute-done.9.refs_3_, bf16[16,4096]{1,0:T(8,128)(2,1)S(1)} %get-tuple-element.47.refs_4_, ...), custom_call_target="tpu_custom_call" | custom-call | tf_op jit(solution)/shard_map/finish/pallas_call | solution.py:465
  (13 shorter events, 0.3 us)
Async XLA Ops:
  1.4 4.3 %collective-permute-start = (bf16[16,11392]{1,0:T(8,128)(2,1)S(1)}, bf16[16,11392]{1,0:T(8,128)(2,1)S(1)}, u32[]{:S(2)}, u32[]{:S(2)}) collective-permute-start(bf16[16,11392]{1,0:T(8,128)(2,1)S(1)} %get-tuple-element.23), channel_id=1, source_target_pairs={{0,1},{1,0},{2,3},{3,2},{4,5},{5,4},{6,7},{7,6},{8,9},{9,8},{10,11... | collective-permute-start | bytes 1093640 | tf_op jit(solution)/shard_map/ppermute | solution.py:353
  2.9 8.3 %collective-permute-start.1 = (bf16[16,10368]{1,0:T(8,128)(2,1)S(1)}, bf16[16,10368]{1,0:T(8,128)(2,1)S(1)}, u32[]{:S(2)}, u32[]{:S(2)}) collective-permute-start(bf16[16,10368]{1,0:T(8,128)(2,1)S(1)} %get-tuple-element.22.refs_0_), channel_id=1, source_target_pairs={{0,2},{1,7},{2,4},{3,1},{4,6},{5,3},{6,0},{7,5},{8,10},{9,15},{10,... | collective-permute-start | bytes 995336 | tf_op jit(solution)/shard_map/ppermute | solution.py:356
  5.7 14.1 %collective-permute-start.2 = (bf16[16,12416]{1,0:T(8,128)(2,1)S(1)}, bf16[16,12416]{1,0:T(8,128)(2,1)S(1)}, u32[]{:S(2)}, u32[]{:S(2)}) collective-permute-start(bf16[16,12416]{1,0:T(8,128)(2,1)S(1)} %join.1.refs_3_), channel_id=1, source_target_pairs={{0,2},{1,7},{2,4},{3,1},{4,6},{5,3},{6,0},{7,5},{8,10},{9,15},{10,... | collective-permute-start | bytes 1191944 | tf_op jit(solution)/shard_map/ppermute | solution.py:356
  11.2 6.9 %collective-permute-start.5 = (bf16[16,10368]{1,0:T(8,128)(2,1)S(1)}, bf16[16,10368]{1,0:T(8,128)(2,1)S(1)}, u32[]{:S(2)}, u32[]{:S(2)}) collective-permute-start(bf16[16,10368]{1,0:T(8,128)(2,1)S(1)} %relay.1.refs_3_), channel_id=1, source_target_pairs={{0,2},{1,7},{2,4},{3,1},{4,6},{5,3},{6,0},{7,5},{8,10},{9,15},{10,... | collective-permute-start | bytes 995336 | tf_op jit(solution)/shard_map/ppermute | solution.py:356
  18.2 2.9 %collective-permute-start.6 = (bf16[16,9344]{1,0:T(8,128)(2,1)S(1)}, bf16[16,9344]{1,0:T(8,128)(2,1)S(1)}, u32[]{:S(2)}, u32[]{:S(2)}) collective-permute-start(bf16[16,9344]{1,0:T(8,128)(2,1)S(1)} %half_far.1), channel_id=1, source_target_pairs={{0,1},{1,0},{2,3},{3,2},{4,5},{5,4},{6,7},{7,6},{8,9},{9,8},{10,11... | collective-permute-start | bytes 897032 | tf_op jit(solution)/shard_map/ppermute | solution.py:353
  19.9 1.7 %collective-permute-start.3 = (bf16[16,9344]{1,0:T(8,128)(2,1)S(1)}, bf16[16,9344]{1,0:T(8,128)(2,1)S(1)}, u32[]{:S(2)}, u32[]{:S(2)}) collective-permute-start(bf16[16,9344]{1,0:T(8,128)(2,1)S(1)} %get-tuple-element.27), channel_id=1, source_target_pairs={{0,1},{1,0},{2,3},{3,2},{4,5},{5,4},{6,7},{7,6},{8,9},{9,8},{10,11... | collective-permute-start | bytes 897032 | tf_op jit(solution)/shard_map/ppermute | solution.py:353
  20.0 2.0 %collective-permute-start.4 = (bf16[16,9344]{1,0:T(8,128)(2,1)S(1)}, bf16[16,9344]{1,0:T(8,128)(2,1)S(1)}, u32[]{:S(2)}, u32[]{:S(2)}) collective-permute-start(bf16[16,9344]{1,0:T(8,128)(2,1)S(1)} %get-tuple-element.28), channel_id=1, source_target_pairs={{0,1},{1,0},{2,3},{3,2},{4,5},{5,4},{6,7},{7,6},{8,9},{9,8},{10,11... | collective-permute-start | bytes 897032 | tf_op jit(solution)/shard_map/ppermute | solution.py:353
  22.0 30.3 %copy-start.2 = (s32[1,16]{1,0:T(1,128)S(1)}, s32[1,16]{1,0:T(1,128)}, u32[]{:S(2)}) copy-start(s32[1,16]{1,0:T(1,128)} %rewards_ref.1) | copy-start | bytes 196
  73.1 21.4 %copy-start = (bf16[16,8192]{1,0:T(8,128)(2,1)S(1)}, bf16[16,8192]{1,0:T(8,128)(2,1)}, u32[]{:S(2)}) copy-start(bf16[16,8192]{1,0:T(8,128)(2,1)} %refs_0_.5) | copy-start | bytes 786436
  73.1 21.4 %copy-start.1 = (f32[8192]{0:T(1024)S(1)}, f32[8192]{0:T(1024)}, u32[]{:S(2)}) copy-start(f32[8192]{0:T(1024)} %param.10) | copy-start | bytes 98308
  73.1 5.7 %collective-permute-start.12 = (bf16[64,4096]{1,0:T(8,128)(2,1)S(1)}, bf16[64,4096]{1,0:T(8,128)(2,1)S(1)}, u32[]{:S(2)}, u32[]{:S(2)}) collective-permute-start(bf16[64,4096]{1,0:T(8,128)(2,1)S(1)} %get-tuple-element.38), channel_id=1, source_target_pairs={{0,1},{1,0},{2,3},{3,2},{4,5},{5,4},{6,7},{7,6},{8,9},{9,8},{10,11... | collective-permute-start | bytes 1572872 | tf_op jit(solution)/shard_map/ppermute | solution.py:353
  78.7 2.0 %collective-permute-start.7 = (bf16[64,4096]{1,0:T(8,128)(2,1)S(1)}, bf16[64,4096]{1,0:T(8,128)(2,1)S(1)}, u32[]{:S(2)}, u32[]{:S(2)}) collective-permute-start(bf16[64,4096]{1,0:T(8,128)(2,1)S(1)} %get-tuple-element.35), channel_id=1, source_target_pairs={{0,1},{1,0},{2,3},{3,2},{4,5},{5,4},{6,7},{7,6},{8,9},{9,8},{10,11... | collective-permute-start | bytes 1572872 | tf_op jit(solution)/shard_map/ppermute | solution.py:353
  78.9 3.9 %collective-permute-start.13 = (bf16[16,4096]{1,0:T(8,128)(2,1)S(1)}, bf16[16,4096]{1,0:T(8,128)(2,1)S(1)}, u32[]{:S(2)}, u32[]{:S(2)}) collective-permute-start(bf16[16,4096]{1,0:T(8,128)(2,1)S(1)} %get-tuple-element.40), channel_id=1, source_target_pairs={{0,2},{1,7},{2,4},{3,1},{4,6},{5,3},{6,0},{7,5},{8,10},{9,15},{10,... | collective-permute-start | bytes 393224 | tf_op jit(solution)/shard_map/ppermute | solution.py:356
  80.8 4.5 %collective-permute-start.8 = (bf16[16,4096]{1,0:T(8,128)(2,1)S(1)}, bf16[16,4096]{1,0:T(8,128)(2,1)S(1)}, u32[]{:S(2)}, u32[]{:S(2)}) collective-permute-start(bf16[16,4096]{1,0:T(8,128)(2,1)S(1)} %get-tuple-element.42), channel_id=1, source_target_pairs={{0,2},{1,7},{2,4},{3,1},{4,6},{5,3},{6,0},{7,5},{8,10},{9,15},{10,... | collective-permute-start | bytes 393224 | tf_op jit(solution)/shard_map/ppermute | solution.py:356
  82.1 5.7 %collective-permute-start.10 = (bf16[32,4096]{1,0:T(8,128)(2,1)S(1)}, bf16[32,4096]{1,0:T(8,128)(2,1)S(1)}, u32[]{:S(2)}, u32[]{:S(2)}) collective-permute-start(bf16[32,4096]{1,0:T(8,128)(2,1)S(1)} %slice.49), channel_id=1, source_target_pairs={{0,2},{1,7},{2,4},{3,1},{4,6},{5,3},{6,0},{7,5},{8,10},{9,15},{10,... | collective-permute-start | bytes 786440 | tf_op jit(solution)/shard_map/ppermute | solution.py:356
  82.9 7.7 %collective-permute-start.14 = (bf16[32,4096]{1,0:T(8,128)(2,1)S(1)}, bf16[32,4096]{1,0:T(8,128)(2,1)S(1)}, u32[]{:S(2)}, u32[]{:S(2)}) collective-permute-start(bf16[32,4096]{1,0:T(8,128)(2,1)S(1)} %pad_maximum_fusion), channel_id=1, source_target_pairs={{0,2},{1,7},{2,4},{3,1},{4,6},{5,3},{6,0},{7,5},{8,10},{9,15},{10,... | collective-permute-start | bytes 786440 | tf_op jit(solution)/shard_map/ppermute | solution.py:356
  85.4 8.1 %collective-permute-start.9 = (bf16[16,4096]{1,0:T(8,128)(2,1)S(1)}, bf16[16,4096]{1,0:T(8,128)(2,1)S(1)}, u32[]{:S(2)}, u32[]{:S(2)}) collective-permute-start(bf16[16,4096]{1,0:T(8,128)(2,1)S(1)} %collective-permute-done.8), channel_id=1, source_target_pairs={{0,2},{1,7},{2,4},{3,1},{4,6},{5,3},{6,0},{7,5},{8,10},{9,15},{10,... | collective-permute-start | bytes 393224 | tf_op jit(solution)/shard_map/ppermute | solution.py:356
  87.9 5.6 %collective-permute-start.11 = (bf16[16,4096]{1,0:T(8,128)(2,1)S(1)}, bf16[16,4096]{1,0:T(8,128)(2,1)S(1)}, u32[]{:S(2)}, u32[]{:S(2)}) collective-permute-start(bf16[16,4096]{1,0:T(8,128)(2,1)S(1)} %get-tuple-element.46), channel_id=1, source_target_pairs={{0,1},{1,0},{2,3},{3,2},{4,5},{5,4},{6,7},{7,6},{8,9},{9,8},{10,11... | collective-permute-start | bytes 393224 | tf_op jit(solution)/shard_map/ppermute | solution.py:353
  90.7 3.8 %collective-permute-start.15 = (bf16[16,4096]{1,0:T(8,128)(2,1)S(1)}, bf16[16,4096]{1,0:T(8,128)(2,1)S(1)}, u32[]{:S(2)}, u32[]{:S(2)}) collective-permute-start(bf16[16,4096]{1,0:T(8,128)(2,1)S(1)} %get-tuple-element.44), channel_id=1, source_target_pairs={{0,1},{1,0},{2,3},{3,2},{4,5},{5,4},{6,7},{7,6},{8,9},{9,8},{10,11... | collective-permute-start | bytes 393224 | tf_op jit(solution)/shard_map/ppermute | solution.py:353

commit v6 on v5

--- a/solution.py
+++ b/solution.py
@@ -12,6 +12,7 @@
 HEADS_AT = 8192 + EXT
 STEP = 1024
 PIECES = 4
+TURNED = (2, 4)
 TURN = 512
 EPSILON = 1e-05
 BASE = 500000.0
@@ -133,6 +134,7 @@
     token_ref[...] = jnp.zeros_like(token_ref)
     span = out_ref.shape[0]
     step = span // PIECES
+    skip = PIECES - turned_ref.shape[1] // step
     copies = []
     for j in range(PIECES):
         at = 0
@@ -151,13 +153,14 @@
     for j in range(PIECES):
         for copy in copies[3 * j : 3 * j + 3]:
             copy.wait()
-        if part == 0:
+        if j < skip:
             continue
 
         @pl.loop(0, step // TURN)
         def _(k):
             at = pl.ds(pl.multiple_of(j * step + k * TURN, TURN), TURN)
-            turned_ref[:, at] = jnp.transpose(out_ref[at, :])
+            to = pl.ds(pl.multiple_of((j - skip) * step + k * TURN, TURN), TURN)
+            turned_ref[:, to] = jnp.transpose(out_ref[at, :])
 
 
 def load(part, weights, after):
@@ -166,8 +169,8 @@
     return pl.pallas_call(
         lambda *refs: load_kernel(part, *refs),
         in_specs=[ANY] * 3 + [VMEM],
-        out_specs=[VMEM] * (2 + (part > 0)),
-        out_shape=[pltpu.VMEM((span, cols), BF16), TOKEN] + [pltpu.VMEM((cols, span), BF16)] * (part > 0),
+        out_specs=[VMEM] * 3,
+        out_shape=[pltpu.VMEM((span, cols), BF16), TOKEN] + [pltpu.VMEM((cols, span * TURNED[part] // PIECES), BF16)],
         scratch_shapes=[pltpu.SemaphoreType.DMA((3 * PIECES,))],
         compiler_params=params(),
         cost_estimate=pl.CostEstimate(flops=0, bytes_accessed=2 * span * cols, transcendentals=0),
@@ -291,28 +294,34 @@
     out_ref[:, vcol : vcol + HD] = grad_value.astype(BF16)
 
 
-def back_kernel(is_turned, ext_ref, slots_ref, w_ref, keep_ref, send_ref):
+def back_kernel(ext_ref, slots_ref, *refs):
+    weights, (keep_ref, send_ref) = refs[:-2], refs[-2:]
     half_rows, span = keep_ref.shape
     slots = slots_ref.shape[0]
     hot = (ext_ref[:, 0:1].astype(F32) == iota((ext_ref.shape[0], slots), 1).astype(F32)).astype(BF16)
     held = dot(hot, slots_ref[...], ((1,), (0,))).astype(BF16)
+    turned_ref = weights[-1]
+    plain = span - turned_ref.shape[1]
     for j in range(span // STEP):
         at = slice(j * STEP, (j + 1) * STEP)
-        if is_turned:
-            term = dot(held, w_ref[:, at], ((1,), (0,))).astype(BF16)
+        if j * STEP < plain:
+            term = dot(held, weights[0][at, :], ((1,), (1,)))
         else:
-            term = dot(held, w_ref[at, :], ((1,), (1,))).astype(BF16)
+            term = dot(held, turned_ref[:, j * STEP - plain : (j + 1) * STEP - plain], ((1,), (0,)))
+        term = term.astype(BF16)
         keep_ref[:, at] = term[0:half_rows]
         send_ref[:, at] = term[half_rows:]
 
 
-def back(ext, slot_grads, w, is_turned):
+def back(ext, slot_grads, w, turned):
     rows = ext.shape[0]
-    cols, span = w.shape if is_turned else w.shape[::-1]
+    cols = turned.shape[0]
+    span = turned.shape[1] if w is None else w.shape[0]
+    weights = [in_vmem(x) for x in (w, turned) if x is not None]
     out = jax.ShapeDtypeStruct((rows // 2, span), BF16)
     return pl.pallas_call(
-        lambda *refs: back_kernel(is_turned, *refs),
-        in_specs=[VMEM] * 3,
+        back_kernel,
+        in_specs=[VMEM] * (2 + len(weights)),
         out_specs=[VMEM] * 2,
         out_shape=[out, out],
         compiler_params=params(),
@@ -320,7 +329,7 @@
             flops=2 * rows * span * cols, bytes_accessed=2 * span * cols, transcendentals=0
         ),
         name="back",
-    )(ext, slot_grads, in_vmem(w))
+    )(ext, slot_grads, *weights)
 
 
 def finish_kernel(counts, hidden_ref, gain_ref, *refs):
@@ -394,7 +403,7 @@
 
     weights = (w_query, w_key, w_value)
     near_o = flow(leave_o)
-    first, ready = load(0, weights, leave_o)
+    first, ready, first_turned = load(0, weights, leave_o)
     passed = pl.pallas_call(
         relay_kernel,
         in_specs=[VMEM] * 2,
@@ -404,7 +413,7 @@
         name="relay",
     )(near, ready)
     far = flow(passed)
-    second, ready_too, turned = load(1, weights, passed)
+    second, ready_too, second_turned = load(1, weights, passed)
 
     half_rows = rows_of(HEADS_AT + query_cols)
     half_near, half_near_o = pl.pallas_call(
@@ -448,7 +457,7 @@
 
     pieces = []
     for i in range(PARTS):
-        keep, send = back(ext, slot_grads, first if i == 0 else turned, i > 0)
+        keep, send = back(ext, slot_grads, *((first, first_turned) if i == 0 else (None, second_turned)))
         both = add(keep, swap(send))
         mine, onward = both[:count], both[count : 3 * count]
         passed = flow(both[3 * count :])

time: 95.8 us -> 95.2 us (level)
  starting transfers between devices: 24.4 us -> 23.4 us
  transfers between devices with their start and end apart: 16 -> 16, of which waited for: 8 -> 9; matrix products, arithmetic and copies ran while one was open for 0% -> 0% of each run, Pallas kernels for 13% -> 13%
where the time goes in v6:
time: 95.2 us; the launch traced here: 95 us
  blocking collectives  40.8 us (43%)
  Pallas kernels  25.5 us (27%)
  starting transfers between devices  23.4 us (25%)
  waiting for transfers between devices  4.78 us (5%)
    all_to_all x1, blocking collectives, on_device(): lax.all_to_all(total.reshape(groups, 2 * ranks, total.shape[1]), 'dp', sp...  26.2 us
    all_to_all x1, blocking collectives, on_device(): lax.all_to_all(grads.reshape(groups, 2 * ranks, cols), 'dp', split_axis=0...  14.5 us
    ppermute x8, starting transfers between devices, flow(): return lax.ppermute(x, 'tensor', flow_pairs)  12.2 us
    ppermute x8, starting transfers between devices, swap(): return lax.ppermute(x, 'tensor', swap_pairs)  11.2 us
    pallas_call x2, Pallas kernels, load(): pl.pallas_call(lambda *refs: load_kernel(part, *refs), in_specs=[ANY] * 3...  10.2 us
    pallas_call x1, Pallas kernels, on_device(): pl.pallas_call(attend_kernel, in_specs=[VMEM] * 2, out_specs=VMEM, out_sh...  4.56 us
    pallas_call x2, Pallas kernels, back(): pl.pallas_call(back_kernel, in_specs=[VMEM] * (2 + len(weights)), out_spe...  4.06 us
    pallas_call x1, Pallas kernels, project(): pl.pallas_call(lambda *refs: project_kernel(len(blocks), *refs), in_specs...  4.05 us
  transfers between devices with their start and end apart: 16, of which 9 were waited for; matrix products, arithmetic and copies ran while one was open for 0% of the time, Pallas kernels for 13%

profile of v6, /device:TPU:1, one launch (start us, length us, event | category | flops | bytes accessed | tf_op | source)
XLA Modules:
  0.0 95.0 jit_solution(15983817665617271477)
XLA Ops:
  0.0 1.4 %norm.1 = (bf16[16,10368]{1,0:T(8,128)(2,1)S(1)}, bf16[16,11392]{1,0:T(8,128)(2,1)S(1)}, bf16[16,2048]{1,0:T(8,128)(2,1)S(1)}, bf16[16,1024]{1,0:T(8,128)(2,1)S(1)}) custom-call(bf16[16,8192]{1,0:T(8,128)(2,1)} %refs_0_.5, f32[1,8192]{1,0:T(1,128)} %bitcast.12, s32[1,16]{1,0:T(1,128)} %bitcast.14, s32[1,16]{1,0:T(1,128)} %bitcast.15, bf16[16,8192]{1,0:T(8,128)(2,1)} %grad_hbm.1), custom_call_target="tpu_custom_call" | custom-call | tf_op jit(solution)/shard_map/norm/pallas_call | solution.py:372
  1.4 1.5 %collective-permute-start = (bf16[16,11392]{1,0:T(8,128)(2,1)S(1)}, bf16[16,11392]{1,0:T(8,128)(2,1)S(1)}, u32[]{:S(2)}, u32[]{:S(2)}) collective-permute-start(bf16[16,11392]{1,0:T(8,128)(2,1)S(1)} %get-tuple-element.24), channel_id=1, source_target_pairs={{0,1},{1,0},{2,3},{3,2},{4,5},{5,4},{6,7},{7,6},{8,9},{9,8},{10,11... | collective-permute-start | bytes 1093640 | tf_op jit(solution)/shard_map/ppermute | solution.py:362
  2.9 2.8 %collective-permute-start.1 = (bf16[16,10368]{1,0:T(8,128)(2,1)S(1)}, bf16[16,10368]{1,0:T(8,128)(2,1)S(1)}, u32[]{:S(2)}, u32[]{:S(2)}) collective-permute-start(bf16[16,10368]{1,0:T(8,128)(2,1)S(1)} %get-tuple-element.23.refs_0_), channel_id=1, source_target_pairs={{0,2},{1,7},{2,4},{3,1},{4,6},{5,3},{6,0},{7,5},{8,10},{9,15},{10,... | collective-permute-start | bytes 995336 | tf_op jit(solution)/shard_map/ppermute | solution.py:365
  5.7 0.0 collective-permute-done.other_ref.refs_1_
  5.7 1.4 %collective-permute-start.2 = (bf16[16,12416]{1,0:T(8,128)(2,1)S(1)}, bf16[16,12416]{1,0:T(8,128)(2,1)S(1)}, u32[]{:S(2)}, u32[]{:S(2)}) collective-permute-start(bf16[16,12416]{1,0:T(8,128)(2,1)S(1)} %join.1.refs_3_), channel_id=1, source_target_pairs={{0,2},{1,7},{2,4},{3,1},{4,6},{5,3},{6,0},{7,5},{8,10},{9,15},{10,... | collective-permute-start | bytes 1191944 | tf_op jit(solution)/shard_map/ppermute | solution.py:365
  7.1 5.0 %load.2 = (bf16[4096,1280]{1,0:T(8,128)(2,1)S(1)}, f32[8,128]{1,0:T(8,128)S(1)}, bf16[1280,2048]{1,0:T(8,128)(2,1)S(1)}) custom-call(bf16[8192,1024]{1,0:T(8,128)(2,1)} %refs_0_.4, bf16[8192,128]{1,0:T(8,128)(2,1)} %refs_1_.3, bf16[8192,128]{1,0:T(8,128)(2,1)} %refs_2_.3, bf16[16,12416]{1,0:T(8,128)(2,1)S(1)} %join.1.refs_3_), custom_call_target="tpu_custom_call" | custom-call | bytes 10485760 | tf_op jit(solution)/shard_map/load/pallas_call | solution.py:169
  12.1 0.0 collective-permute-done.1.near_ref.refs_2_
  12.2 0.8 collective-permute-start.5
  13.0 5.2 %load.3 = (bf16[4096,1280]{1,0:T(8,128)(2,1)S(1)}, f32[8,128]{1,0:T(8,128)S(1)}, bf16[1280,4096]{1,0:T(8,128)(2,1)S(1)}) custom-call(bf16[8192,1024]{1,0:T(8,128)(2,1)} %refs_0_.4, bf16[8192,128]{1,0:T(8,128)(2,1)} %refs_1_.3, bf16[8192,128]{1,0:T(8,128)(2,1)} %refs_2_.3, bf16[16,10368]{1,0:T(8,128)(2,1)S(1)} %relay.1.refs_3_), custom_call_target="tpu_custom_call" | custom-call | bytes 10485760 | tf_op jit(solution)/shard_map/load/pallas_call | solution.py:169
  18.2 0.3 collective-permute-done.5.far_ref.refs_6_
  18.5 1.4 %collective-permute-start.6 = (bf16[16,9344]{1,0:T(8,128)(2,1)S(1)}, bf16[16,9344]{1,0:T(8,128)(2,1)S(1)}, u32[]{:S(2)}, u32[]{:S(2)}) collective-permute-start(bf16[16,9344]{1,0:T(8,128)(2,1)S(1)} %half_far.1), channel_id=1, source_target_pairs={{0,1},{1,0},{2,3},{3,2},{4,5},{5,4},{6,7},{7,6},{8,9},{9,8},{10,11... | collective-permute-start | bytes 897032 | tf_op jit(solution)/shard_map/ppermute | solution.py:362
  19.9 0.0 collective-permute-done.2.near_o_ref.refs_3_
  19.9 0.1 collective-permute-start.3
  20.0 0.5 collective-permute-start.4
  20.5 0.6 collective-permute-done.6.refs_7_
  21.1 0.5 collective-permute-done.3.refs_4_
  21.6 0.4 collective-permute-done.4.refs_5_
  22.0 4.0 %project.1 = (bf16[256,2432]{1,0:T(8,128)(2,1)S(1)}, bf16[128,128]{1,0:T(8,128)(2,1)S(1)}) custom-call(bf16[16,10368]{1,0:T(8,128)(2,1)S(1)} %get-tuple-element.23.refs_0_, bf16[16,11392]{1,0:T(8,128)(2,1)S(1)} %collective-permute-done.other_ref.refs_1_, bf16[16,10368]{1,0:T(8,128)(2,1)S(1)} %collective-permute-done.1.near_ref.refs_2_, ...), custom_call_target="tpu_custom_call" | custom-call | flops 2684354560 | bytes 20971520 | tf_op jit(solution)/shard_map/project/pallas_call | solution.py:222
  26.1 26.2 %all_to_all.10 = bf16[16,16,2432]{2,1,0:T(8,128)(2,1)S(1)} all-to-all(bf16[16,16,2432]{2,1,0:T(8,128)(2,1)S(1)} %bitcast.11), channel_id=1, replica_groups=mesh['dp'=16,'tensor'=8] {'dp'}, dimensions={0} | all-to-all | bytes 2490368 | tf_op jit(solution)/shard_map/all_to_all | solution.py:438
  52.3 0.0 copy-done.2
  52.3 4.6 %attend.1 = bf16[256,1280]{1,0:T(8,128)(2,1)S(1)} custom-call(bf16[256,2432]{1,0:T(8,128)(2,1)S(1)} %bitcast.9, s32[1,16]{1,0:T(1,128)S(1)} %copy-done.2), custom_call_target="tpu_custom_call" | custom-call | tf_op jit(solution)/shard_map/attend/pallas_call | solution.py:443
  56.9 14.5 %all_to_all.11 = bf16[16,16,1280]{2,1,0:T(8,128)(2,1)S(1)} all-to-all(bf16[16,16,1280]{2,1,0:T(8,128)(2,1)S(1)} %bitcast.10), channel_id=1, replica_groups=mesh['dp'=16,'tensor'=8] {'dp'}, dimensions={0} | all-to-all | bytes 1310720 | tf_op jit(solution)/shard_map/all_to_all | solution.py:451
  71.4 1.7 %back.3 = (bf16[64,4096]{1,0:T(8,128)(2,1)S(1)}, bf16[64,4096]{1,0:T(8,128)(2,1)S(1)}) custom-call(bf16[128,128]{1,0:T(8,128)(2,1)S(1)} %get-tuple-element.33.ext_ref, bf16[256,1280]{1,0:T(8,128)(2,1)S(1)} %bitcast.7, bf16[1280,4096]{1,0:T(8,128)(2,1)S(1)} %get-tuple-element.38.refs_0_), custom_call_target="tpu_custom_call" | custom-call | flops 1342177280 | bytes 10485760 | tf_op jit(solution)/shard_map/back/pallas_call | solution.py:322
  73.1 2.5 %collective-permute-start.12 = (bf16[64,4096]{1,0:T(8,128)(2,1)S(1)}, bf16[64,4096]{1,0:T(8,128)(2,1)S(1)}, u32[]{:S(2)}, u32[]{:S(2)}) collective-permute-start(bf16[64,4096]{1,0:T(8,128)(2,1)S(1)} %get-tuple-element.40), channel_id=1, source_target_pairs={{0,1},{1,0},{2,3},{3,2},{4,5},{5,4},{6,7},{7,6},{8,9},{9,8},{10,11... | collective-permute-start | bytes 1572872 | tf_op jit(solution)/shard_map/ppermute | solution.py:362
  75.7 2.4 %back.2 = (bf16[64,4096]{1,0:T(8,128)(2,1)S(1)}, bf16[64,4096]{1,0:T(8,128)(2,1)S(1)}) custom-call(bf16[128,128]{1,0:T(8,128)(2,1)S(1)} %get-tuple-element.33.ext_ref, bf16[256,1280]{1,0:T(8,128)(2,1)S(1)} %bitcast.8, bf16[4096,1280]{1,0:T(8,128)(2,1)S(1)} %get-tuple-element.30.refs_8_.refs_0_, bf16[1280,2048]{1,0:T(8,128)(2,1)S(1)} %get-tuple-element.35.refs_1_), custom_call_target="tpu_custom_call" | custom-call | flops 1342177280 | bytes 10485760 | tf_op jit(solution)/shard_map/back/pallas_call | solution.py:322
  78.0 0.0 copy-start
  78.1 0.0 copy-start.1
  78.1 0.1 collective-permute-start.7
  78.2 0.0 collective-permute-done.12
  78.2 0.1 add_convert_fusion
  78.3 1.3 %collective-permute-start.13 = (bf16[16,4096]{1,0:T(8,128)(2,1)S(1)}, bf16[16,4096]{1,0:T(8,128)(2,1)S(1)}, u32[]{:S(2)}, u32[]{:S(2)}) collective-permute-start(bf16[16,4096]{1,0:T(8,128)(2,1)S(1)} %get-tuple-element.42), channel_id=1, source_target_pairs={{0,2},{1,7},{2,4},{3,1},{4,6},{5,3},{6,0},{7,5},{8,10},{9,15},{10,... | collective-permute-start | bytes 393224 | tf_op jit(solution)/shard_map/ppermute | solution.py:365
  79.6 0.5 collective-permute-done.7
  80.1 0.1 add_convert_fusion.1
  80.2 1.3 %collective-permute-start.8 = (bf16[16,4096]{1,0:T(8,128)(2,1)S(1)}, bf16[16,4096]{1,0:T(8,128)(2,1)S(1)}, u32[]{:S(2)}, u32[]{:S(2)}) collective-permute-start(bf16[16,4096]{1,0:T(8,128)(2,1)S(1)} %get-tuple-element.44), channel_id=1, source_target_pairs={{0,2},{1,7},{2,4},{3,1},{4,6},{5,3},{6,0},{7,5},{8,10},{9,15},{10,... | collective-permute-start | bytes 393224 | tf_op jit(solution)/shard_map/ppermute | solution.py:365
  81.5 0.5 collective-permute-start.10
  82.0 0.3 collective-permute-done.13
  82.3 2.5 %collective-permute-start.14 = (bf16[32,4096]{1,0:T(8,128)(2,1)S(1)}, bf16[32,4096]{1,0:T(8,128)(2,1)S(1)}, u32[]{:S(2)}, u32[]{:S(2)}) collective-permute-start(bf16[32,4096]{1,0:T(8,128)(2,1)S(1)} %pad_maximum_fusion), channel_id=1, source_target_pairs={{0,2},{1,7},{2,4},{3,1},{4,6},{5,3},{6,0},{7,5},{8,10},{9,15},{10,... | collective-permute-start | bytes 786440 | tf_op jit(solution)/shard_map/ppermute | solution.py:365
  84.8 0.0 collective-permute-done.8
  84.8 1.8 %collective-permute-start.9 = (bf16[16,4096]{1,0:T(8,128)(2,1)S(1)}, bf16[16,4096]{1,0:T(8,128)(2,1)S(1)}, u32[]{:S(2)}, u32[]{:S(2)}) collective-permute-start(bf16[16,4096]{1,0:T(8,128)(2,1)S(1)} %collective-permute-done.8), channel_id=1, source_target_pairs={{0,2},{1,7},{2,4},{3,1},{4,6},{5,3},{6,0},{7,5},{8,10},{9,15},{10,... | collective-permute-start | bytes 393224 | tf_op jit(solution)/shard_map/ppermute | solution.py:365
  86.5 0.7 collective-permute-done.10
  87.2 2.3 %collective-permute-start.11 = (bf16[16,4096]{1,0:T(8,128)(2,1)S(1)}, bf16[16,4096]{1,0:T(8,128)(2,1)S(1)}, u32[]{:S(2)}, u32[]{:S(2)}) collective-permute-start(bf16[16,4096]{1,0:T(8,128)(2,1)S(1)} %get-tuple-element.48), channel_id=1, source_target_pairs={{0,1},{1,0},{2,3},{3,2},{4,5},{5,4},{6,7},{7,6},{8,9},{9,8},{10,11... | collective-permute-start | bytes 393224 | tf_op jit(solution)/shard_map/ppermute | solution.py:362
  89.5 0.5 collective-permute-done.14
  90.1 2.8 %collective-permute-start.15 = (bf16[16,4096]{1,0:T(8,128)(2,1)S(1)}, bf16[16,4096]{1,0:T(8,128)(2,1)S(1)}, u32[]{:S(2)}, u32[]{:S(2)}) collective-permute-start(bf16[16,4096]{1,0:T(8,128)(2,1)S(1)} %get-tuple-element.46), channel_id=1, source_target_pairs={{0,1},{1,0},{2,3},{3,2},{4,5},{5,4},{6,7},{7,6},{8,9},{9,8},{10,11... | collective-permute-start | bytes 393224 | tf_op jit(solution)/shard_map/ppermute | solution.py:362
  92.9 0.0 collective-permute-done.9.refs_3_
  92.9 0.0 collective-permute-done.11.refs_5_
  92.9 1.0 %collective-permute-done.15.refs_8_ = bf16[16,4096]{1,0:T(8,128)(2,1)S(1)} collective-permute-done((bf16[16,4096]{1,0:T(8,128)(2,1)S(1)}, bf16[16,4096]{1,0:T(8,128)(2,1)S(1)}, u32[]{:S(2)}, u32[]{:S(2)}) %collective-permute-start.15) | collective-permute-done | bytes 131104 | tf_op jit(solution)/shard_map/ppermute | solution.py:362
  93.9 0.0 copy-done
  93.9 1.2 %finish.1 = bf16[16,8192]{1,0:T(8,128)(2,1)} custom-call(bf16[16,8192]{1,0:T(8,128)(2,1)S(1)} %copy-done, f32[1,8192]{1,0:T(1,128)S(1)} %bitcast.13, bf16[16,4096]{1,0:T(8,128)(2,1)S(1)} %get-tuple-element.45.refs_2_, bf16[16,4096]{1,0:T(8,128)(2,1)S(1)} %collective-permute-done.9.refs_3_, bf16[16,4096]{1,0:T(8,128)(2,1)S(1)} %get-tuple-element.49.refs_4_, ...), custom_call_target="tpu_custom_call" | custom-call | tf_op jit(solution)/shard_map/finish/pallas_call | solution.py:474
  (13 shorter events, 0.3 us)
Async XLA Ops:
  1.4 4.3 %collective-permute-start = (bf16[16,11392]{1,0:T(8,128)(2,1)S(1)}, bf16[16,11392]{1,0:T(8,128)(2,1)S(1)}, u32[]{:S(2)}, u32[]{:S(2)}) collective-permute-start(bf16[16,11392]{1,0:T(8,128)(2,1)S(1)} %get-tuple-element.24), channel_id=1, source_target_pairs={{0,1},{1,0},{2,3},{3,2},{4,5},{5,4},{6,7},{7,6},{8,9},{9,8},{10,11... | collective-permute-start | bytes 1093640 | tf_op jit(solution)/shard_map/ppermute | solution.py:362
  2.9 9.2 %collective-permute-start.1 = (bf16[16,10368]{1,0:T(8,128)(2,1)S(1)}, bf16[16,10368]{1,0:T(8,128)(2,1)S(1)}, u32[]{:S(2)}, u32[]{:S(2)}) collective-permute-start(bf16[16,10368]{1,0:T(8,128)(2,1)S(1)} %get-tuple-element.23.refs_0_), channel_id=1, source_target_pairs={{0,2},{1,7},{2,4},{3,1},{4,6},{5,3},{6,0},{7,5},{8,10},{9,15},{10,... | collective-permute-start | bytes 995336 | tf_op jit(solution)/shard_map/ppermute | solution.py:365
  5.7 14.1 %collective-permute-start.2 = (bf16[16,12416]{1,0:T(8,128)(2,1)S(1)}, bf16[16,12416]{1,0:T(8,128)(2,1)S(1)}, u32[]{:S(2)}, u32[]{:S(2)}) collective-permute-start(bf16[16,12416]{1,0:T(8,128)(2,1)S(1)} %join.1.refs_3_), channel_id=1, source_target_pairs={{0,2},{1,7},{2,4},{3,1},{4,6},{5,3},{6,0},{7,5},{8,10},{9,15},{10,... | collective-permute-start | bytes 1191944 | tf_op jit(solution)/shard_map/ppermute | solution.py:365
  12.2 6.3 %collective-permute-start.5 = (bf16[16,10368]{1,0:T(8,128)(2,1)S(1)}, bf16[16,10368]{1,0:T(8,128)(2,1)S(1)}, u32[]{:S(2)}, u32[]{:S(2)}) collective-permute-start(bf16[16,10368]{1,0:T(8,128)(2,1)S(1)} %relay.1.refs_3_), channel_id=1, source_target_pairs={{0,2},{1,7},{2,4},{3,1},{4,6},{5,3},{6,0},{7,5},{8,10},{9,15},{10,... | collective-permute-start | bytes 995336 | tf_op jit(solution)/shard_map/ppermute | solution.py:365
  18.5 2.6 %collective-permute-start.6 = (bf16[16,9344]{1,0:T(8,128)(2,1)S(1)}, bf16[16,9344]{1,0:T(8,128)(2,1)S(1)}, u32[]{:S(2)}, u32[]{:S(2)}) collective-permute-start(bf16[16,9344]{1,0:T(8,128)(2,1)S(1)} %half_far.1), channel_id=1, source_target_pairs={{0,1},{1,0},{2,3},{3,2},{4,5},{5,4},{6,7},{7,6},{8,9},{9,8},{10,11... | collective-permute-start | bytes 897032 | tf_op jit(solution)/shard_map/ppermute | solution.py:362
  19.9 1.7 %collective-permute-start.3 = (bf16[16,9344]{1,0:T(8,128)(2,1)S(1)}, bf16[16,9344]{1,0:T(8,128)(2,1)S(1)}, u32[]{:S(2)}, u32[]{:S(2)}) collective-permute-start(bf16[16,9344]{1,0:T(8,128)(2,1)S(1)} %get-tuple-element.28), channel_id=1, source_target_pairs={{0,1},{1,0},{2,3},{3,2},{4,5},{5,4},{6,7},{7,6},{8,9},{9,8},{10,11... | collective-permute-start | bytes 897032 | tf_op jit(solution)/shard_map/ppermute | solution.py:362
  20.0 2.0 %collective-permute-start.4 = (bf16[16,9344]{1,0:T(8,128)(2,1)S(1)}, bf16[16,9344]{1,0:T(8,128)(2,1)S(1)}, u32[]{:S(2)}, u32[]{:S(2)}) collective-permute-start(bf16[16,9344]{1,0:T(8,128)(2,1)S(1)} %get-tuple-element.29), channel_id=1, source_target_pairs={{0,1},{1,0},{2,3},{3,2},{4,5},{5,4},{6,7},{7,6},{8,9},{9,8},{10,11... | collective-permute-start | bytes 897032 | tf_op jit(solution)/shard_map/ppermute | solution.py:362
  22.0 30.3 %copy-start.2 = (s32[1,16]{1,0:T(1,128)S(1)}, s32[1,16]{1,0:T(1,128)}, u32[]{:S(2)}) copy-start(s32[1,16]{1,0:T(1,128)} %rewards_ref.1) | copy-start | bytes 196
  73.1 5.0 %collective-permute-start.12 = (bf16[64,4096]{1,0:T(8,128)(2,1)S(1)}, bf16[64,4096]{1,0:T(8,128)(2,1)S(1)}, u32[]{:S(2)}, u32[]{:S(2)}) collective-permute-start(bf16[64,4096]{1,0:T(8,128)(2,1)S(1)} %get-tuple-element.40), channel_id=1, source_target_pairs={{0,1},{1,0},{2,3},{3,2},{4,5},{5,4},{6,7},{7,6},{8,9},{9,8},{10,11... | collective-permute-start | bytes 1572872 | tf_op jit(solution)/shard_map/ppermute | solution.py:362
  78.0 15.8 %copy-start = (bf16[16,8192]{1,0:T(8,128)(2,1)S(1)}, bf16[16,8192]{1,0:T(8,128)(2,1)}, u32[]{:S(2)}) copy-start(bf16[16,8192]{1,0:T(8,128)(2,1)} %refs_0_.5) | copy-start | bytes 786436
  78.1 15.8 %copy-start.1 = (f32[8192]{0:T(1024)S(1)}, f32[8192]{0:T(1024)}, u32[]{:S(2)}) copy-start(f32[8192]{0:T(1024)} %param.10) | copy-start | bytes 98308
  78.1 2.0 %collective-permute-start.7 = (bf16[64,4096]{1,0:T(8,128)(2,1)S(1)}, bf16[64,4096]{1,0:T(8,128)(2,1)S(1)}, u32[]{:S(2)}, u32[]{:S(2)}) collective-permute-start(bf16[64,4096]{1,0:T(8,128)(2,1)S(1)} %get-tuple-element.37), channel_id=1, source_target_pairs={{0,1},{1,0},{2,3},{3,2},{4,5},{5,4},{6,7},{7,6},{8,9},{9,8},{10,11... | collective-permute-start | bytes 1572872 | tf_op jit(solution)/shard_map/ppermute | solution.py:362
  78.3 3.9 %collective-permute-start.13 = (bf16[16,4096]{1,0:T(8,128)(2,1)S(1)}, bf16[16,4096]{1,0:T(8,128)(2,1)S(1)}, u32[]{:S(2)}, u32[]{:S(2)}) collective-permute-start(bf16[16,4096]{1,0:T(8,128)(2,1)S(1)} %get-tuple-element.42), channel_id=1, source_target_pairs={{0,2},{1,7},{2,4},{3,1},{4,6},{5,3},{6,0},{7,5},{8,10},{9,15},{10,... | collective-permute-start | bytes 393224 | tf_op jit(solution)/shard_map/ppermute | solution.py:365
  80.2 4.5 %collective-permute-start.8 = (bf16[16,4096]{1,0:T(8,128)(2,1)S(1)}, bf16[16,4096]{1,0:T(8,128)(2,1)S(1)}, u32[]{:S(2)}, u32[]{:S(2)}) collective-permute-start(bf16[16,4096]{1,0:T(8,128)(2,1)S(1)} %get-tuple-element.44), channel_id=1, source_target_pairs={{0,2},{1,7},{2,4},{3,1},{4,6},{5,3},{6,0},{7,5},{8,10},{9,15},{10,... | collective-permute-start | bytes 393224 | tf_op jit(solution)/shard_map/ppermute | solution.py:365
  81.5 5.7 %collective-permute-start.10 = (bf16[32,4096]{1,0:T(8,128)(2,1)S(1)}, bf16[32,4096]{1,0:T(8,128)(2,1)S(1)}, u32[]{:S(2)}, u32[]{:S(2)}) collective-permute-start(bf16[32,4096]{1,0:T(8,128)(2,1)S(1)} %slice.49), channel_id=1, source_target_pairs={{0,2},{1,7},{2,4},{3,1},{4,6},{5,3},{6,0},{7,5},{8,10},{9,15},{10,... | collective-permute-start | bytes 786440 | tf_op jit(solution)/shard_map/ppermute | solution.py:365
  82.3 7.7 %collective-permute-start.14 = (bf16[32,4096]{1,0:T(8,128)(2,1)S(1)}, bf16[32,4096]{1,0:T(8,128)(2,1)S(1)}, u32[]{:S(2)}, u32[]{:S(2)}) collective-permute-start(bf16[32,4096]{1,0:T(8,128)(2,1)S(1)} %pad_maximum_fusion), channel_id=1, source_target_pairs={{0,2},{1,7},{2,4},{3,1},{4,6},{5,3},{6,0},{7,5},{8,10},{9,15},{10,... | collective-permute-start | bytes 786440 | tf_op jit(solution)/shard_map/ppermute | solution.py:365
  84.8 8.1 %collective-permute-start.9 = (bf16[16,4096]{1,0:T(8,128)(2,1)S(1)}, bf16[16,4096]{1,0:T(8,128)(2,1)S(1)}, u32[]{:S(2)}, u32[]{:S(2)}) collective-permute-start(bf16[16,4096]{1,0:T(8,128)(2,1)S(1)} %collective-permute-done.8), channel_id=1, source_target_pairs={{0,2},{1,7},{2,4},{3,1},{4,6},{5,3},{6,0},{7,5},{8,10},{9,15},{10,... | collective-permute-start | bytes 393224 | tf_op jit(solution)/shard_map/ppermute | solution.py:365
  87.2 5.6 %collective-permute-start.11 = (bf16[16,4096]{1,0:T(8,128)(2,1)S(1)}, bf16[16,4096]{1,0:T(8,128)(2,1)S(1)}, u32[]{:S(2)}, u32[]{:S(2)}) collective-permute-start(bf16[16,4096]{1,0:T(8,128)(2,1)S(1)} %get-tuple-element.48), channel_id=1, source_target_pairs={{0,1},{1,0},{2,3},{3,2},{4,5},{5,4},{6,7},{7,6},{8,9},{9,8},{10,11... | collective-permute-start | bytes 393224 | tf_op jit(solution)/shard_map/ppermute | solution.py:362
  90.1 3.8 %collective-permute-start.15 = (bf16[16,4096]{1,0:T(8,128)(2,1)S(1)}, bf16[16,4096]{1,0:T(8,128)(2,1)S(1)}, u32[]{:S(2)}, u32[]{:S(2)}) collective-permute-start(bf16[16,4096]{1,0:T(8,128)(2,1)S(1)} %get-tuple-element.46), channel_id=1, source_target_pairs={{0,1},{1,0},{2,3},{3,2},{4,5},{5,4},{6,7},{7,6},{8,9},{9,8},{10,11... | collective-permute-start | bytes 393224 | tf_op jit(solution)/shard_map/ppermute | solution.py:362

commit v7 on v6

--- a/solution.py
+++ b/solution.py
@@ -12,7 +12,7 @@
 HEADS_AT = 8192 + EXT
 STEP = 1024
 PIECES = 4
-TURNED = (2, 4)
+TURNED = (3, 4)
 TURN = 512
 EPSILON = 1e-05
 BASE = 500000.0

time: 95.2 us -> 95 us (level)
  no operation moved by 1% of the time
where the time goes in v7:
time: 95 us; the launch traced here: 94.8 us
  blocking collectives  40.7 us (43%)
  Pallas kernels  25.3 us (27%)
  starting transfers between devices  23.2 us (24%)
  waiting for transfers between devices  4.97 us (5%)
    all_to_all x1, blocking collectives, on_device(): lax.all_to_all(total.reshape(groups, 2 * ranks, total.shape[1]), 'dp', sp...  26.2 us
    all_to_all x1, blocking collectives, on_device(): lax.all_to_all(grads.reshape(groups, 2 * ranks, cols), 'dp', split_axis=0...  14.5 us
    ppermute x8, starting transfers between devices, flow(): return lax.ppermute(x, 'tensor', flow_pairs)  12 us
    ppermute x8, starting transfers between devices, swap(): return lax.ppermute(x, 'tensor', swap_pairs)  11.2 us
    pallas_call x2, Pallas kernels, load(): pl.pallas_call(lambda *refs: load_kernel(part, *refs), in_specs=[ANY] * 3...  10.3 us
    pallas_call x1, Pallas kernels, on_device(): pl.pallas_call(attend_kernel, in_specs=[VMEM] * 2, out_specs=VMEM, out_sh...  4.55 us
    pallas_call x1, Pallas kernels, project(): pl.pallas_call(lambda *refs: project_kernel(len(blocks), *refs), in_specs...  4.05 us
    pallas_call x2, Pallas kernels, back(): pl.pallas_call(back_kernel, in_specs=[VMEM] * (2 + len(weights)), out_spe...  3.74 us
  transfers between devices with their start and end apart: 16, of which 9 were waited for; matrix products, arithmetic and copies ran while one was open for 0% of the time, Pallas kernels for 13%

profile of v7, /device:TPU:1, one launch (start us, length us, event | category | flops | bytes accessed | tf_op | source)
XLA Modules:
  0.0 94.8 jit_solution(2042837980515721493)
XLA Ops:
  0.0 1.4 %norm.1 = (bf16[16,10368]{1,0:T(8,128)(2,1)S(1)}, bf16[16,11392]{1,0:T(8,128)(2,1)S(1)}, bf16[16,2048]{1,0:T(8,128)(2,1)S(1)}, bf16[16,1024]{1,0:T(8,128)(2,1)S(1)}) custom-call(bf16[16,8192]{1,0:T(8,128)(2,1)} %refs_0_.5, f32[1,8192]{1,0:T(1,128)} %bitcast.12, s32[1,16]{1,0:T(1,128)} %bitcast.14, s32[1,16]{1,0:T(1,128)} %bitcast.15, bf16[16,8192]{1,0:T(8,128)(2,1)} %grad_hbm.1), custom_call_target="tpu_custom_call" | custom-call | tf_op jit(solution)/shard_map/norm/pallas_call | solution.py:372
  1.4 1.5 %collective-permute-start = (bf16[16,11392]{1,0:T(8,128)(2,1)S(1)}, bf16[16,11392]{1,0:T(8,128)(2,1)S(1)}, u32[]{:S(2)}, u32[]{:S(2)}) collective-permute-start(bf16[16,11392]{1,0:T(8,128)(2,1)S(1)} %get-tuple-element.24), channel_id=1, source_target_pairs={{0,1},{1,0},{2,3},{3,2},{4,5},{5,4},{6,7},{7,6},{8,9},{9,8},{10,11... | collective-permute-start | bytes 1093640 | tf_op jit(solution)/shard_map/ppermute | solution.py:362
  2.9 2.8 %collective-permute-start.1 = (bf16[16,10368]{1,0:T(8,128)(2,1)S(1)}, bf16[16,10368]{1,0:T(8,128)(2,1)S(1)}, u32[]{:S(2)}, u32[]{:S(2)}) collective-permute-start(bf16[16,10368]{1,0:T(8,128)(2,1)S(1)} %get-tuple-element.23.refs_0_), channel_id=1, source_target_pairs={{0,2},{1,7},{2,4},{3,1},{4,6},{5,3},{6,0},{7,5},{8,10},{9,15},{10,... | collective-permute-start | bytes 995336 | tf_op jit(solution)/shard_map/ppermute | solution.py:365
  5.7 0.0 collective-permute-done.other_ref.refs_1_
  5.7 1.4 %collective-permute-start.2 = (bf16[16,12416]{1,0:T(8,128)(2,1)S(1)}, bf16[16,12416]{1,0:T(8,128)(2,1)S(1)}, u32[]{:S(2)}, u32[]{:S(2)}) collective-permute-start(bf16[16,12416]{1,0:T(8,128)(2,1)S(1)} %join.1.refs_3_), channel_id=1, source_target_pairs={{0,2},{1,7},{2,4},{3,1},{4,6},{5,3},{6,0},{7,5},{8,10},{9,15},{10,... | collective-permute-start | bytes 1191944 | tf_op jit(solution)/shard_map/ppermute | solution.py:365
  7.1 5.1 %load.2 = (bf16[4096,1280]{1,0:T(8,128)(2,1)S(1)}, f32[8,128]{1,0:T(8,128)S(1)}, bf16[1280,3072]{1,0:T(8,128)(2,1)S(1)}) custom-call(bf16[8192,1024]{1,0:T(8,128)(2,1)} %refs_0_.4, bf16[8192,128]{1,0:T(8,128)(2,1)} %refs_1_.3, bf16[8192,128]{1,0:T(8,128)(2,1)} %refs_2_.3, bf16[16,12416]{1,0:T(8,128)(2,1)S(1)} %join.1.refs_3_), custom_call_target="tpu_custom_call" | custom-call | bytes 10485760 | tf_op jit(solution)/shard_map/load/pallas_call | solution.py:169
  12.2 0.0 collective-permute-done.1.near_ref.refs_2_
  12.3 0.7 collective-permute-start.5
  13.0 5.2 %load.3 = (bf16[4096,1280]{1,0:T(8,128)(2,1)S(1)}, f32[8,128]{1,0:T(8,128)S(1)}, bf16[1280,4096]{1,0:T(8,128)(2,1)S(1)}) custom-call(bf16[8192,1024]{1,0:T(8,128)(2,1)} %refs_0_.4, bf16[8192,128]{1,0:T(8,128)(2,1)} %refs_1_.3, bf16[8192,128]{1,0:T(8,128)(2,1)} %refs_2_.3, bf16[16,10368]{1,0:T(8,128)(2,1)S(1)} %relay.1.refs_3_), custom_call_target="tpu_custom_call" | custom-call | bytes 10485760 | tf_op jit(solution)/shard_map/load/pallas_call | solution.py:169
  18.2 0.4 collective-permute-done.5.far_ref.refs_6_
  18.6 1.4 %collective-permute-start.6 = (bf16[16,9344]{1,0:T(8,128)(2,1)S(1)}, bf16[16,9344]{1,0:T(8,128)(2,1)S(1)}, u32[]{:S(2)}, u32[]{:S(2)}) collective-permute-start(bf16[16,9344]{1,0:T(8,128)(2,1)S(1)} %half_far.1), channel_id=1, source_target_pairs={{0,1},{1,0},{2,3},{3,2},{4,5},{5,4},{6,7},{7,6},{8,9},{9,8},{10,11... | collective-permute-start | bytes 897032 | tf_op jit(solution)/shard_map/ppermute | solution.py:362
  20.0 0.0 collective-permute-done.2.near_o_ref.refs_3_
  20.0 0.1 collective-permute-start.3
  20.1 0.5 collective-permute-start.4
  20.6 0.6 collective-permute-done.6.refs_7_
  21.2 0.5 collective-permute-done.3.refs_4_
  21.7 0.4 collective-permute-done.4.refs_5_
  22.1 0.0 copy-start.2
  22.1 4.0 %project.1 = (bf16[256,2432]{1,0:T(8,128)(2,1)S(1)}, bf16[128,128]{1,0:T(8,128)(2,1)S(1)}) custom-call(bf16[16,10368]{1,0:T(8,128)(2,1)S(1)} %get-tuple-element.23.refs_0_, bf16[16,11392]{1,0:T(8,128)(2,1)S(1)} %collective-permute-done.other_ref.refs_1_, bf16[16,10368]{1,0:T(8,128)(2,1)S(1)} %collective-permute-done.1.near_ref.refs_2_, ...), custom_call_target="tpu_custom_call" | custom-call | flops 2684354560 | bytes 20971520 | tf_op jit(solution)/shard_map/project/pallas_call | solution.py:222
  26.2 26.2 %all_to_all.10 = bf16[16,16,2432]{2,1,0:T(8,128)(2,1)S(1)} all-to-all(bf16[16,16,2432]{2,1,0:T(8,128)(2,1)S(1)} %bitcast.11), channel_id=1, replica_groups=mesh['dp'=16,'tensor'=8] {'dp'}, dimensions={0} | all-to-all | bytes 2490368 | tf_op jit(solution)/shard_map/all_to_all | solution.py:438
  52.4 0.0 copy-done.2
  52.4 4.6 %attend.1 = bf16[256,1280]{1,0:T(8,128)(2,1)S(1)} custom-call(bf16[256,2432]{1,0:T(8,128)(2,1)S(1)} %bitcast.9, s32[1,16]{1,0:T(1,128)S(1)} %copy-done.2), custom_call_target="tpu_custom_call" | custom-call | tf_op jit(solution)/shard_map/attend/pallas_call | solution.py:443
  57.0 14.5 %all_to_all.11 = bf16[16,16,1280]{2,1,0:T(8,128)(2,1)S(1)} all-to-all(bf16[16,16,1280]{2,1,0:T(8,128)(2,1)S(1)} %bitcast.10), channel_id=1, replica_groups=mesh['dp'=16,'tensor'=8] {'dp'}, dimensions={0} | all-to-all | bytes 1310720 | tf_op jit(solution)/shard_map/all_to_all | solution.py:451
  71.5 1.7 %back.3 = (bf16[64,4096]{1,0:T(8,128)(2,1)S(1)}, bf16[64,4096]{1,0:T(8,128)(2,1)S(1)}) custom-call(bf16[128,128]{1,0:T(8,128)(2,1)S(1)} %get-tuple-element.33.ext_ref, bf16[256,1280]{1,0:T(8,128)(2,1)S(1)} %bitcast.7, bf16[1280,4096]{1,0:T(8,128)(2,1)S(1)} %get-tuple-element.38.refs_0_), custom_call_target="tpu_custom_call" | custom-call | flops 1342177280 | bytes 10485760 | tf_op jit(solution)/shard_map/back/pallas_call | solution.py:322
  73.2 2.5 %collective-permute-start.12 = (bf16[64,4096]{1,0:T(8,128)(2,1)S(1)}, bf16[64,4096]{1,0:T(8,128)(2,1)S(1)}, u32[]{:S(2)}, u32[]{:S(2)}) collective-permute-start(bf16[64,4096]{1,0:T(8,128)(2,1)S(1)} %get-tuple-element.40), channel_id=1, source_target_pairs={{0,1},{1,0},{2,3},{3,2},{4,5},{5,4},{6,7},{7,6},{8,9},{9,8},{10,11... | collective-permute-start | bytes 1572872 | tf_op jit(solution)/shard_map/ppermute | solution.py:362
  75.7 2.0 %back.2 = (bf16[64,4096]{1,0:T(8,128)(2,1)S(1)}, bf16[64,4096]{1,0:T(8,128)(2,1)S(1)}) custom-call(bf16[128,128]{1,0:T(8,128)(2,1)S(1)} %get-tuple-element.33.ext_ref, bf16[256,1280]{1,0:T(8,128)(2,1)S(1)} %bitcast.8, bf16[4096,1280]{1,0:T(8,128)(2,1)S(1)} %get-tuple-element.30.refs_8_.refs_0_, bf16[1280,3072]{1,0:T(8,128)(2,1)S(1)} %get-tuple-element.35.refs_1_), custom_call_target="tpu_custom_call" | custom-call | flops 1342177280 | bytes 10485760 | tf_op jit(solution)/shard_map/back/pallas_call | solution.py:322
  77.8 0.1 collective-permute-start.7
  77.9 0.0 collective-permute-done.12
  77.9 0.1 add_convert_fusion
  78.1 1.2 %collective-permute-start.13 = (bf16[16,4096]{1,0:T(8,128)(2,1)S(1)}, bf16[16,4096]{1,0:T(8,128)(2,1)S(1)}, u32[]{:S(2)}, u32[]{:S(2)}) collective-permute-start(bf16[16,4096]{1,0:T(8,128)(2,1)S(1)} %get-tuple-element.42), channel_id=1, source_target_pairs={{0,2},{1,7},{2,4},{3,1},{4,6},{5,3},{6,0},{7,5},{8,10},{9,15},{10,... | collective-permute-start | bytes 393224 | tf_op jit(solution)/shard_map/ppermute | solution.py:365
  79.3 0.5 collective-permute-done.7
  79.8 0.1 add_convert_fusion.1
  80.0 1.2 %collective-permute-start.8 = (bf16[16,4096]{1,0:T(8,128)(2,1)S(1)}, bf16[16,4096]{1,0:T(8,128)(2,1)S(1)}, u32[]{:S(2)}, u32[]{:S(2)}) collective-permute-start(bf16[16,4096]{1,0:T(8,128)(2,1)S(1)} %get-tuple-element.44), channel_id=1, source_target_pairs={{0,2},{1,7},{2,4},{3,1},{4,6},{5,3},{6,0},{7,5},{8,10},{9,15},{10,... | collective-permute-start | bytes 393224 | tf_op jit(solution)/shard_map/ppermute | solution.py:365
  81.1 0.6 collective-permute-start.10
  81.7 0.2 collective-permute-done.13
  82.0 2.4 %collective-permute-start.14 = (bf16[32,4096]{1,0:T(8,128)(2,1)S(1)}, bf16[32,4096]{1,0:T(8,128)(2,1)S(1)}, u32[]{:S(2)}, u32[]{:S(2)}) collective-permute-start(bf16[32,4096]{1,0:T(8,128)(2,1)S(1)} %pad_maximum_fusion), channel_id=1, source_target_pairs={{0,2},{1,7},{2,4},{3,1},{4,6},{5,3},{6,0},{7,5},{8,10},{9,15},{10,... | collective-permute-start | bytes 786440 | tf_op jit(solution)/shard_map/ppermute | solution.py:365
  84.4 0.0 collective-permute-done.8
  84.4 1.8 %collective-permute-start.9 = (bf16[16,4096]{1,0:T(8,128)(2,1)S(1)}, bf16[16,4096]{1,0:T(8,128)(2,1)S(1)}, u32[]{:S(2)}, u32[]{:S(2)}) collective-permute-start(bf16[16,4096]{1,0:T(8,128)(2,1)S(1)} %collective-permute-done.8), channel_id=1, source_target_pairs={{0,2},{1,7},{2,4},{3,1},{4,6},{5,3},{6,0},{7,5},{8,10},{9,15},{10,... | collective-permute-start | bytes 393224 | tf_op jit(solution)/shard_map/ppermute | solution.py:365
  86.2 0.8 collective-permute-done.10
  87.0 2.3 %collective-permute-start.11 = (bf16[16,4096]{1,0:T(8,128)(2,1)S(1)}, bf16[16,4096]{1,0:T(8,128)(2,1)S(1)}, u32[]{:S(2)}, u32[]{:S(2)}) collective-permute-start(bf16[16,4096]{1,0:T(8,128)(2,1)S(1)} %get-tuple-element.48), channel_id=1, source_target_pairs={{0,1},{1,0},{2,3},{3,2},{4,5},{5,4},{6,7},{7,6},{8,9},{9,8},{10,11... | collective-permute-start | bytes 393224 | tf_op jit(solution)/shard_map/ppermute | solution.py:362
  89.3 0.5 collective-permute-done.14
  89.8 2.8 %collective-permute-start.15 = (bf16[16,4096]{1,0:T(8,128)(2,1)S(1)}, bf16[16,4096]{1,0:T(8,128)(2,1)S(1)}, u32[]{:S(2)}, u32[]{:S(2)}) collective-permute-start(bf16[16,4096]{1,0:T(8,128)(2,1)S(1)} %get-tuple-element.46), channel_id=1, source_target_pairs={{0,1},{1,0},{2,3},{3,2},{4,5},{5,4},{6,7},{7,6},{8,9},{9,8},{10,11... | collective-permute-start | bytes 393224 | tf_op jit(solution)/shard_map/ppermute | solution.py:362
  92.6 0.0 collective-permute-done.9.refs_3_
  92.6 0.0 collective-permute-done.11.refs_5_
  92.6 1.0 %collective-permute-done.15.refs_8_ = bf16[16,4096]{1,0:T(8,128)(2,1)S(1)} collective-permute-done((bf16[16,4096]{1,0:T(8,128)(2,1)S(1)}, bf16[16,4096]{1,0:T(8,128)(2,1)S(1)}, u32[]{:S(2)}, u32[]{:S(2)}) %collective-permute-start.15) | collective-permute-done | bytes 131104 | tf_op jit(solution)/shard_map/ppermute | solution.py:362
  93.6 0.0 copy-done
  93.6 0.0 copy-done.1
  93.6 1.2 %finish.1 = bf16[16,8192]{1,0:T(8,128)(2,1)} custom-call(bf16[16,8192]{1,0:T(8,128)(2,1)S(1)} %copy-done, f32[1,8192]{1,0:T(1,128)S(1)} %bitcast.13, bf16[16,4096]{1,0:T(8,128)(2,1)S(1)} %get-tuple-element.45.refs_2_, bf16[16,4096]{1,0:T(8,128)(2,1)S(1)} %collective-permute-done.9.refs_3_, bf16[16,4096]{1,0:T(8,128)(2,1)S(1)} %get-tuple-element.49.refs_4_, ...), custom_call_target="tpu_custom_call" | custom-call | tf_op jit(solution)/shard_map/finish/pallas_call | solution.py:474
  (13 shorter events, 0.3 us)
Async XLA Ops:
  1.4 4.3 %collective-permute-start = (bf16[16,11392]{1,0:T(8,128)(2,1)S(1)}, bf16[16,11392]{1,0:T(8,128)(2,1)S(1)}, u32[]{:S(2)}, u32[]{:S(2)}) collective-permute-start(bf16[16,11392]{1,0:T(8,128)(2,1)S(1)} %get-tuple-element.24), channel_id=1, source_target_pairs={{0,1},{1,0},{2,3},{3,2},{4,5},{5,4},{6,7},{7,6},{8,9},{9,8},{10,11... | collective-permute-start | bytes 1093640 | tf_op jit(solution)/shard_map/ppermute | solution.py:362
  2.9 9.3 %collective-permute-start.1 = (bf16[16,10368]{1,0:T(8,128)(2,1)S(1)}, bf16[16,10368]{1,0:T(8,128)(2,1)S(1)}, u32[]{:S(2)}, u32[]{:S(2)}) collective-permute-start(bf16[16,10368]{1,0:T(8,128)(2,1)S(1)} %get-tuple-element.23.refs_0_), channel_id=1, source_target_pairs={{0,2},{1,7},{2,4},{3,1},{4,6},{5,3},{6,0},{7,5},{8,10},{9,15},{10,... | collective-permute-start | bytes 995336 | tf_op jit(solution)/shard_map/ppermute | solution.py:365
  5.7 14.2 %collective-permute-start.2 = (bf16[16,12416]{1,0:T(8,128)(2,1)S(1)}, bf16[16,12416]{1,0:T(8,128)(2,1)S(1)}, u32[]{:S(2)}, u32[]{:S(2)}) collective-permute-start(bf16[16,12416]{1,0:T(8,128)(2,1)S(1)} %join.1.refs_3_), channel_id=1, source_target_pairs={{0,2},{1,7},{2,4},{3,1},{4,6},{5,3},{6,0},{7,5},{8,10},{9,15},{10,... | collective-permute-start | bytes 1191944 | tf_op jit(solution)/shard_map/ppermute | solution.py:365
  12.3 6.3 %collective-permute-start.5 = (bf16[16,10368]{1,0:T(8,128)(2,1)S(1)}, bf16[16,10368]{1,0:T(8,128)(2,1)S(1)}, u32[]{:S(2)}, u32[]{:S(2)}) collective-permute-start(bf16[16,10368]{1,0:T(8,128)(2,1)S(1)} %relay.1.refs_3_), channel_id=1, source_target_pairs={{0,2},{1,7},{2,4},{3,1},{4,6},{5,3},{6,0},{7,5},{8,10},{9,15},{10,... | collective-permute-start | bytes 995336 | tf_op jit(solution)/shard_map/ppermute | solution.py:365
  18.6 2.6 %collective-permute-start.6 = (bf16[16,9344]{1,0:T(8,128)(2,1)S(1)}, bf16[16,9344]{1,0:T(8,128)(2,1)S(1)}, u32[]{:S(2)}, u32[]{:S(2)}) collective-permute-start(bf16[16,9344]{1,0:T(8,128)(2,1)S(1)} %half_far.1), channel_id=1, source_target_pairs={{0,1},{1,0},{2,3},{3,2},{4,5},{5,4},{6,7},{7,6},{8,9},{9,8},{10,11... | collective-permute-start | bytes 897032 | tf_op jit(solution)/shard_map/ppermute | solution.py:362
  20.0 1.7 %collective-permute-start.3 = (bf16[16,9344]{1,0:T(8,128)(2,1)S(1)}, bf16[16,9344]{1,0:T(8,128)(2,1)S(1)}, u32[]{:S(2)}, u32[]{:S(2)}) collective-permute-start(bf16[16,9344]{1,0:T(8,128)(2,1)S(1)} %get-tuple-element.28), channel_id=1, source_target_pairs={{0,1},{1,0},{2,3},{3,2},{4,5},{5,4},{6,7},{7,6},{8,9},{9,8},{10,11... | collective-permute-start | bytes 897032 | tf_op jit(solution)/shard_map/ppermute | solution.py:362
  20.1 2.0 %collective-permute-start.4 = (bf16[16,9344]{1,0:T(8,128)(2,1)S(1)}, bf16[16,9344]{1,0:T(8,128)(2,1)S(1)}, u32[]{:S(2)}, u32[]{:S(2)}) collective-permute-start(bf16[16,9344]{1,0:T(8,128)(2,1)S(1)} %get-tuple-element.29), channel_id=1, source_target_pairs={{0,1},{1,0},{2,3},{3,2},{4,5},{5,4},{6,7},{7,6},{8,9},{9,8},{10,11... | collective-permute-start | bytes 897032 | tf_op jit(solution)/shard_map/ppermute | solution.py:362
  22.1 30.3 %copy-start.2 = (s32[1,16]{1,0:T(1,128)S(1)}, s32[1,16]{1,0:T(1,128)}, u32[]{:S(2)}) copy-start(s32[1,16]{1,0:T(1,128)} %rewards_ref.1) | copy-start | bytes 196
  73.2 4.7 %collective-permute-start.12 = (bf16[64,4096]{1,0:T(8,128)(2,1)S(1)}, bf16[64,4096]{1,0:T(8,128)(2,1)S(1)}, u32[]{:S(2)}, u32[]{:S(2)}) collective-permute-start(bf16[64,4096]{1,0:T(8,128)(2,1)S(1)} %get-tuple-element.40), channel_id=1, source_target_pairs={{0,1},{1,0},{2,3},{3,2},{4,5},{5,4},{6,7},{7,6},{8,9},{9,8},{10,11... | collective-permute-start | bytes 1572872 | tf_op jit(solution)/shard_map/ppermute | solution.py:362
  75.7 17.9 %copy-start = (bf16[16,8192]{1,0:T(8,128)(2,1)S(1)}, bf16[16,8192]{1,0:T(8,128)(2,1)}, u32[]{:S(2)}) copy-start(bf16[16,8192]{1,0:T(8,128)(2,1)} %refs_0_.5) | copy-start | bytes 786436
  75.7 17.9 %copy-start.1 = (f32[8192]{0:T(1024)S(1)}, f32[8192]{0:T(1024)}, u32[]{:S(2)}) copy-start(f32[8192]{0:T(1024)} %param.10) | copy-start | bytes 98308
  77.8 2.0 %collective-permute-start.7 = (bf16[64,4096]{1,0:T(8,128)(2,1)S(1)}, bf16[64,4096]{1,0:T(8,128)(2,1)S(1)}, u32[]{:S(2)}, u32[]{:S(2)}) collective-permute-start(bf16[64,4096]{1,0:T(8,128)(2,1)S(1)} %get-tuple-element.37), channel_id=1, source_target_pairs={{0,1},{1,0},{2,3},{3,2},{4,5},{5,4},{6,7},{7,6},{8,9},{9,8},{10,11... | collective-permute-start | bytes 1572872 | tf_op jit(solution)/shard_map/ppermute | solution.py:362
  78.1 3.9 %collective-permute-start.13 = (bf16[16,4096]{1,0:T(8,128)(2,1)S(1)}, bf16[16,4096]{1,0:T(8,128)(2,1)S(1)}, u32[]{:S(2)}, u32[]{:S(2)}) collective-permute-start(bf16[16,4096]{1,0:T(8,128)(2,1)S(1)} %get-tuple-element.42), channel_id=1, source_target_pairs={{0,2},{1,7},{2,4},{3,1},{4,6},{5,3},{6,0},{7,5},{8,10},{9,15},{10,... | collective-permute-start | bytes 393224 | tf_op jit(solution)/shard_map/ppermute | solution.py:365
  80.0 4.5 %collective-permute-start.8 = (bf16[16,4096]{1,0:T(8,128)(2,1)S(1)}, bf16[16,4096]{1,0:T(8,128)(2,1)S(1)}, u32[]{:S(2)}, u32[]{:S(2)}) collective-permute-start(bf16[16,4096]{1,0:T(8,128)(2,1)S(1)} %get-tuple-element.44), channel_id=1, source_target_pairs={{0,2},{1,7},{2,4},{3,1},{4,6},{5,3},{6,0},{7,5},{8,10},{9,15},{10,... | collective-permute-start | bytes 393224 | tf_op jit(solution)/shard_map/ppermute | solution.py:365
  81.1 5.8 %collective-permute-start.10 = (bf16[32,4096]{1,0:T(8,128)(2,1)S(1)}, bf16[32,4096]{1,0:T(8,128)(2,1)S(1)}, u32[]{:S(2)}, u32[]{:S(2)}) collective-permute-start(bf16[32,4096]{1,0:T(8,128)(2,1)S(1)} %slice.49), channel_id=1, source_target_pairs={{0,2},{1,7},{2,4},{3,1},{4,6},{5,3},{6,0},{7,5},{8,10},{9,15},{10,... | collective-permute-start | bytes 786440 | tf_op jit(solution)/shard_map/ppermute | solution.py:365
  82.0 7.7 %collective-permute-start.14 = (bf16[32,4096]{1,0:T(8,128)(2,1)S(1)}, bf16[32,4096]{1,0:T(8,128)(2,1)S(1)}, u32[]{:S(2)}, u32[]{:S(2)}) collective-permute-start(bf16[32,4096]{1,0:T(8,128)(2,1)S(1)} %pad_maximum_fusion), channel_id=1, source_target_pairs={{0,2},{1,7},{2,4},{3,1},{4,6},{5,3},{6,0},{7,5},{8,10},{9,15},{10,... | collective-permute-start | bytes 786440 | tf_op jit(solution)/shard_map/ppermute | solution.py:365
  84.4 8.2 %collective-permute-start.9 = (bf16[16,4096]{1,0:T(8,128)(2,1)S(1)}, bf16[16,4096]{1,0:T(8,128)(2,1)S(1)}, u32[]{:S(2)}, u32[]{:S(2)}) collective-permute-start(bf16[16,4096]{1,0:T(8,128)(2,1)S(1)} %collective-permute-done.8), channel_id=1, source_target_pairs={{0,2},{1,7},{2,4},{3,1},{4,6},{5,3},{6,0},{7,5},{8,10},{9,15},{10,... | collective-permute-start | bytes 393224 | tf_op jit(solution)/shard_map/ppermute | solution.py:365
  87.0 5.6 %collective-permute-start.11 = (bf16[16,4096]{1,0:T(8,128)(2,1)S(1)}, bf16[16,4096]{1,0:T(8,128)(2,1)S(1)}, u32[]{:S(2)}, u32[]{:S(2)}) collective-permute-start(bf16[16,4096]{1,0:T(8,128)(2,1)S(1)} %get-tuple-element.48), channel_id=1, source_target_pairs={{0,1},{1,0},{2,3},{3,2},{4,5},{5,4},{6,7},{7,6},{8,9},{9,8},{10,11... | collective-permute-start | bytes 393224 | tf_op jit(solution)/shard_map/ppermute | solution.py:362
  89.8 3.8 %collective-permute-start.15 = (bf16[16,4096]{1,0:T(8,128)(2,1)S(1)}, bf16[16,4096]{1,0:T(8,128)(2,1)S(1)}, u32[]{:S(2)}, u32[]{:S(2)}) collective-permute-start(bf16[16,4096]{1,0:T(8,128)(2,1)S(1)} %get-tuple-element.46), channel_id=1, source_target_pairs={{0,1},{1,0},{2,3},{3,2},{4,5},{5,4},{6,7},{7,6},{8,9},{9,8},{10,11... | collective-permute-start | bytes 393224 | tf_op jit(solution)/shard_map/ppermute | solution.py:362
